TPU v7x, 256 devices: a whole 4x4x8 slice. The times are simulated.
256 devices in a mesh: sec: 4 (over x_lo, core), gy: 64 (over x_hi, z, y).
Axes of the slice: x: 4 (x_hi: 2, x_lo: 2; x = x_hi * 2 + x_lo), y: 4, z: 8, core: 2. Of those that a mesh axis runs over, the one named last changes fastest.
Arguments:
- fluid_dist: float32 [19, 8, 64, 8192], P(None, None, 'sec', 'gy'), may hold values from 0.02 to 0.1
- order_dist: float32 [19, 8, 64, 8192], P(None, None, 'sec', 'gy'), may hold values from -0.12 to 0.12
- plane_offset: int32 [2, 4], replicated, may hold values from 0 to 2097151, as said below
- plane_speed: int32 [4], replicated, may hold values from 1 to 32
Outputs:
- fluid_next: float32 [19, 8, 64, 8192], P(None, None, 'sec', 'gy')
- order_next: float32 [19, 8, 64, 8192], P(None, None, 'sec', 'gy')
Inputs may be any that keep to these rules, and one draw needn't show every extreme that they name: plane_offset[t, s] is the displacement along y, in 1/256 of a cell, of section s - 1 as seen from section s in step t. plane_speed[s] is the plane's sliding speed in 1/256 of a cell per step.
All inputs are finite; a program needn't handle non-finite values.
Results may differ from a plain program's by a relative error of at most 0.0001.
Values sent between devices are 32-bit elements; how exact they have to be, the bound alone decides.
A program may use at most 128 MiB of HBM per device.

v0:
```python
import jax
import jax.numpy as jnp
from jax import lax
from jax.sharding import PartitionSpec as P

STEPS = 2


VELOCITY = (
    (0, 0, 0),
    (1, 0, 0),
    (-1, 0, 0),
    (0, 1, 0),
    (0, -1, 0),
    (0, 0, 1),
    (0, 0, -1),
    (1, 1, 0),
    (-1, -1, 0),
    (1, -1, 0),
    (-1, 1, 0),
    (1, 0, 1),
    (-1, 0, -1),
    (1, 0, -1),
    (-1, 0, 1),
    (0, 1, 1),
    (0, -1, -1),
    (0, 1, -1),
    (0, -1, 1),
)
WEIGHTS = (1.0 / 3.0,) + (1.0 / 18.0,) * 6 + (1.0 / 36.0,) * 12
ALONG_X = tuple((vector[0] for vector in VELOCITY))
ALONG_Y = tuple((vector[1] for vector in VELOCITY))
ALONG_Z = tuple((vector[2] for vector in VELOCITY))
UPWARD = (1, 7, 9, 11, 13)
DOWNWARD = (2, 8, 10, 12, 14)
EVERY_ROW = tuple(range(19))
COEF_A = -0.0625
COEF_B = 0.0625
KAPPA_GRAD = 0.04
MOBILITY = 1.0
TAU_FLUID = 0.8
TAU_ORDER = 0.9


def shifted(value, axis, steps):
    count = lax.axis_size(axis)
    pairs = [(source, (source + steps) % count) for source in range(count)]
    return lax.ppermute(value, axis, pairs)


def with_halo(cells, sides, width):
    for axis, dim in sides:
        count = lax.axis_size(axis)
        head = lax.slice_in_dim(cells, 0, width, axis=dim)
        tail = lax.slice_in_dim(cells, cells.shape[dim] - width, cells.shape[dim], axis=dim)
        cells = jnp.concatenate(
            [
                lax.ppermute(tail, axis, [(i, (i + 1) % count) for i in range(count)]),
                cells,
                lax.ppermute(head, axis, [((i + 1) % count, i) for i in range(count)]),
            ],
            axis=dim,
        )
    return cells


def column(values):
    return jnp.asarray(values, jnp.float32)[:, None, None, None]


def moment(field, values):
    return jnp.tensordot(
        jnp.asarray(values, jnp.float32), field, axes=1, precision=lax.Precision.HIGHEST
    )


def projected(rows, vel_x, vel_y, vel_z):
    along = (
        column([ALONG_X[entry] for entry in rows]) * vel_x
        + column([ALONG_Y[entry] for entry in rows]) * vel_y
        + column([ALONG_Z[entry] for entry in rows]) * vel_z
    )
    square = vel_x * vel_x + vel_y * vel_y + vel_z * vel_z
    return (along, 3.0 * along + 4.5 * along * along - 1.5 * square)


def collide(fluid, order, density, order_field, potential, force):
    force_x, force_y, force_z = force
    vel_x = (moment(fluid, ALONG_X) + 0.5 * force_x) / density
    vel_y = (moment(fluid, ALONG_Y) + 0.5 * force_y) / density
    vel_z = (moment(fluid, ALONG_Z) + 0.5 * force_z) / density
    along, shape = projected(EVERY_ROW, vel_x, vel_y, vel_z)
    weight = column(WEIGHTS)
    fluid_eq = weight * density * (1.0 + shape)
    pushed = column(ALONG_X) * force_x + column(ALONG_Y) * force_y + column(ALONG_Z) * force_z
    drift = vel_x * force_x + vel_y * force_y + vel_z * force_z
    source = (1.0 - 0.5 / TAU_FLUID) * weight * (3.0 * (pushed - drift) + 9.0 * along * pushed)
    fluid_post = fluid - (fluid - fluid_eq) / TAU_FLUID + source
    order_eq = weight * (3.0 * MOBILITY * potential + order_field * shape)
    resting = order_field - jnp.sum(order_eq[1:], axis=0)
    order_eq = jnp.concatenate([resting[None], order_eq[1:]], axis=0)
    order_post = order - (order - order_eq) / TAU_ORDER
    return (fluid_post, order_post, (vel_x, vel_y, vel_z))


def frame_shift(fluid_post, order_post, density, order_field, velocity, layer, rows, jump):
    layer_cut = slice(layer, layer + 1)
    vel_x, vel_y, vel_z = [component[:, layer_cut, :] for component in velocity]
    before = projected(rows, vel_x, vel_y, vel_z)[1]
    after = projected(rows, vel_x, vel_y + jump, vel_z)[1]
    change = column([WEIGHTS[entry] for entry in rows]) * (after - before)
    fluid_rows = jnp.stack([fluid_post[entry, :, layer_cut, :] for entry in rows])
    order_rows = jnp.stack([order_post[entry, :, layer_cut, :] for entry in rows])
    return jnp.concatenate(
        [
            fluid_rows + density[:, layer_cut, :] * change,
            order_rows + order_field[:, layer_cut, :] * change,
        ],
        axis=0,
    )


def align(pair, units, rim):
    y_devices = lax.axis_size("gy")
    width_y = pair.shape[4]
    total_y = width_y * y_devices
    count = width_y + 2 * rim
    starts = [(units[side] // 256 - rim) % total_y for side in range(2)]
    fracs = [(units[side] % 256).astype(jnp.float32) / 256.0 for side in range(2)]
    first = lax.axis_index("gy") * width_y
    positions = jnp.arange(count, dtype=jnp.int32)
    piece = lax.all_gather(pair, "gy", axis=4, tiled=True)
    source = jnp.arange(piece.shape[4], dtype=jnp.int32)
    updated = []
    for side in range(2):
        target = (first + starts[side] + positions) % total_y
        beyond = (target + 1) % total_y
        table = (1.0 - fracs[side]) * (source[:, None] == target[None, :]).astype(
            jnp.float32
        ) + fracs[side] * (source[:, None] == beyond[None, :]).astype(jnp.float32)
        updated.append(
            jnp.einsum("kzxs,sj->kzxj", piece[side], table, precision=lax.Precision.HIGHEST)
        )
    return jnp.stack(updated)


def cross_faces(up_going, down_going, receiver_units, rim):
    from_below = shifted(up_going, "sec", 1)
    from_above = shifted(down_going, "sec", -1)
    lined = align(jnp.stack([from_below, from_above]), receiver_units, rim)
    return (lined[0], lined[1])


def edge_rows(both):
    rimmed = with_halo(both, (("gy", 3),), 1)
    return rimmed


def moved_row(post, row, lower_ghost, upper_ghost, width_y):
    base = row % 19
    shift_x, shift_y, shift_z = VELOCITY[base]
    lift = 5 if row >= 19 else 0
    if shift_x == 1:
        post = jnp.concatenate([lower_ghost[UPWARD.index(base) + lift], post[:, :-1, :]], axis=1)
    elif shift_x == -1:
        post = jnp.concatenate([post[:, 1:, :], upper_ghost[DOWNWARD.index(base) + lift]], axis=1)
    post = post[:, :, 1 - shift_y : 1 - shift_y + width_y]
    return jnp.roll(post, shift_z, axis=0)


def advance(fluid, order, offsets, speeds):
    sections = lax.axis_size("sec")
    y_devices = lax.axis_size("gy")
    section_index = lax.axis_index("sec")
    above = (section_index + 1) % sections
    width_x = fluid.shape[2]
    width_y = fluid.shape[3]
    span = width_y * y_devices * 256
    here_units = offsets[section_index]
    next_units = offsets[above]
    receiver_units = (here_units, (span - next_units) % span)
    rates = speeds.astype(jnp.float32) / 256.0
    order_field = jnp.sum(order, axis=0)
    density = jnp.sum(fluid, axis=0)
    lower, upper = cross_faces(
        order_field[None, :, width_x - 2 :, :], order_field[None, :, :2, :], receiver_units, 2
    )
    y_padded = with_halo(order_field, (("gy", 2),), 2)
    extended = jnp.concatenate([lower[0], y_padded, upper[0]], axis=1)
    center = extended[:, 1:-1, 1:-1]
    laplace = (
        extended[:, 2:, 1:-1]
        + extended[:, :-2, 1:-1]
        + extended[:, 1:-1, 2:]
        + extended[:, 1:-1, :-2]
        + jnp.roll(center, 1, 0)
        + jnp.roll(center, -1, 0)
        - 6.0 * center
    )
    potential = COEF_A * center + COEF_B * center * center * center - KAPPA_GRAD * laplace
    inner = potential[:, 1:-1, 1:-1]
    gradient = (
        (potential[:, 2:, 1:-1] - potential[:, :-2, 1:-1]) * 0.5,
        (potential[:, 1:-1, 2:] - potential[:, 1:-1, :-2]) * 0.5,
        (jnp.roll(inner, -1, 0) - jnp.roll(inner, 1, 0)) * 0.5,
    )
    force = tuple((-order_field * entry for entry in gradient))
    fluid_post, order_post, velocity = collide(fluid, order, density, order_field, inner, force)
    going_down = frame_shift(
        fluid_post, order_post, density, order_field, velocity, 0, DOWNWARD, rates[section_index]
    )
    going_up = frame_shift(
        fluid_post, order_post, density, order_field, velocity, width_x - 1, UPWARD, -rates[above]
    )
    lower_ghost, upper_ghost = cross_faces(going_up, going_down, receiver_units, 1)
    rimmed = edge_rows(jnp.concatenate([fluid_post, order_post], axis=0))
    rows_out = [moved_row(rimmed[row], row, lower_ghost, upper_ghost, width_y) for row in range(38)]
    return (jnp.stack(rows_out[:19]), jnp.stack(rows_out[19:]))


def per_device(fluid_dist, order_dist, plane_offset, plane_speed):
    fluid, order = (fluid_dist, order_dist)
    for step in range(STEPS):
        fluid, order = advance(fluid, order, plane_offset[step], plane_speed)
    return (fluid, order)


def solution(mesh):
    placed = (P(None, None, "sec", "gy"), P(None, None, "sec", "gy"), P(), P())
    return jax.shard_map(
        per_device,
        mesh=mesh,
        in_specs=placed,
        out_specs=(P(None, None, "sec", "gy"), P(None, None, "sec", "gy")),
        check_vma=False,
    )
```

profile of v0, /device:TPU:1, one launch (start us, length us, event | category | flops | bytes accessed | tf_op | source)
XLA Modules:
  0.0 569.6 jit_solution(15357143191666644105)
XLA Ops:
  16.6 9.2 %collective-permute-start.3 = (f32[8,16,2]{2,0,1:T(8,128)S(1)}, f32[8,16,2]{2,0,1:T(8,128)S(1)}, u32[]{:S(2)}, u32[]{:S(2)}) collective-permute-start(f32[8,16,2]{2,0,1:T(8,128)S(1)} %get-tuple-element.236), channel_id=1, source_target_pairs={{1,0},{2,1},{3,2},{4,3},{5,4},{6,5},{7,6},{8,7},{9,8},{10,9},{11,1... | collective-permute-start | bytes 3080 | tf_op jit(solution)/shard_map/ppermute | solution.py:60
  36.3 82.7 %all-gather.5.cloned.1.call-done = f32[2,1,8,2,8192]{4,2,3,1,0:T(8,128)} async-done(((f32[2,1,8,2,128]{4,2,3,1,0:T(8,128)}), f32[2,1,8,2,8192]{4,2,3,1,0:T(8,128)}) %all-gather.5.cloned.1.call-update) | async-done | bytes 1048592 | tf_op jit(solution)/shard_map/all_gather | solution.py:132
  118.9 5.2 fusion.12
  124.2 4.3 fusion.14
  135.7 3.9 collective-permute-start.7
  146.6 3.1 slice_maximum_fusion.1
  155.1 7.2 %collective-permute-start.5 = (f32[38,8,16,1]{0,2,3,1:T(8,128)S(1)}, f32[38,8,16,1]{0,2,3,1:T(8,128)S(1)}, u32[]{:S(2)}, u32[]{:S(2)}) collective-permute-start(f32[38,8,16,1]{0,2,3,1:T(8,128)S(1)} %copy.166), channel_id=1, source_target_pairs={{1,0},{2,1},{3,2},{4,3},{5,4},{6,5},{7,6},{8,7},{9,8},{10,9},{11,1... | collective-permute-start | bytes 58376 | tf_op jit(solution)/shard_map/ppermute | solution.py:60
  163.3 8.3 %collective-permute-done.4 = f32[38,8,16,1]{0,2,3,1:T(8,128)S(1)} collective-permute-done((f32[38,8,16,1]{0,2,3,1:T(8,128)S(1)}, f32[38,8,16,1]{0,2,3,1:T(8,128)S(1)}, u32[]{:S(2)}, u32[]{:S(2)}) %collective-permute-start.4) | collective-permute-done | bytes 19488 | tf_op jit(solution)/shard_map/ppermute | solution.py:58
  176.7 4.4 pad_maximum_fusion
  207.3 60.1 %all-gather.7.cloned.1.call-done = f32[2,10,8,1,8192]{4,2,1,3,0:T(8,128)} async-done(((f32[2,10,8,1,128]{4,2,1,3,0:T(8,128)}), f32[2,10,8,1,8192]{4,2,1,3,0:T(8,128)}) %all-gather.7.cloned.1.call-update) | async-done | bytes 5242896 | tf_op jit(solution)/shard_map/all_gather | solution.py:132
  267.4 6.9 %fusion.10 = f32[10,8,130]{2,1,0:T(8,128)S(1)} fusion(f32[2,10,8,1,8192]{4,2,1,3,0:T(8,128)} %all-gather.7.cloned.1.call-done, f32[]{:T(128)S(6)} %div.86, s32[130]{0:T(256)S(1)} %get-tuple-element.265, f32[]{:T(128)S(6)} %sub.419, s32[130]{0:T(256)S(1)} %get-tuple-element.266), kind=kOutput, calls=%fused_computation.12 | convolution fusion | flops 1027686400 | bytes 2664088 | tf_op jit(solution)/shard_map/kzxs,sj->kzxj/dot_general | solution.py:142
  275.1 5.2 fusion.8
  282.4 3.9 collective-permute-start.8
  287.5 5.9 %collective-permute-start.11 = (f32[8,16,2]{2,0,1:T(8,128)}, f32[8,16,2]{2,0,1:T(8,128)}, u32[]{:S(2)}, u32[]{:S(2)}) collective-permute-start(f32[8,16,2]{2,0,1:T(8,128)} %get-tuple-element.223), channel_id=1, source_target_pairs={{1,0},{2,1},{3,2},{4,3},{5,4},{6,5},{7,6},{8,7},{9,8},{10,9},{11,1... | collective-permute-start | bytes 3080 | tf_op jit(solution)/shard_map/ppermute | solution.py:60
  310.2 82.1 %all-gather.9.cloned.1.call-done = f32[2,1,8,2,8192]{4,2,3,1,0:T(8,128)} async-done(((f32[2,1,8,2,128]{4,2,3,1,0:T(8,128)}), f32[2,1,8,2,8192]{4,2,3,1,0:T(8,128)}) %all-gather.9.cloned.1.call-update) | async-done | bytes 1048592 | tf_op jit(solution)/shard_map/all_gather | solution.py:132
  392.3 5.2 fusion.4
  397.6 4.5 fusion.6
  412.8 3.9 collective-permute-start.15
  428.1 7.2 %collective-permute-start.13 = (f32[38,8,16,1]{0,2,3,1:T(8,128)S(1)}, f32[38,8,16,1]{0,2,3,1:T(8,128)S(1)}, u32[]{:S(2)}, u32[]{:S(2)}) collective-permute-start(f32[38,8,16,1]{0,2,3,1:T(8,128)S(1)} %copy.211), channel_id=1, source_target_pairs={{1,0},{2,1},{3,2},{4,3},{5,4},{6,5},{7,6},{8,7},{9,8},{10,9},{11,1... | collective-permute-start | bytes 58376 | tf_op jit(solution)/shard_map/ppermute | solution.py:60
  436.1 8.3 %collective-permute-done.12 = f32[38,8,16,1]{0,2,3,1:T(8,128)S(1)} collective-permute-done((f32[38,8,16,1]{0,2,3,1:T(8,128)S(1)}, f32[38,8,16,1]{0,2,3,1:T(8,128)S(1)}, u32[]{:S(2)}, u32[]{:S(2)}) %collective-permute-start.12) | collective-permute-done | bytes 19488 | tf_op jit(solution)/shard_map/ppermute | solution.py:58
  449.4 4.4 pad_maximum_fusion.1
  478.1 66.3 %all-gather.11.cloned.1.call-done = f32[2,10,8,1,8192]{4,2,1,3,0:T(8,128)} async-done(((f32[2,10,8,1,128]{4,2,1,3,0:T(8,128)}), f32[2,10,8,1,8192]{4,2,1,3,0:T(8,128)}) %all-gather.11.cloned.1.call-update) | async-done | bytes 5242896 | tf_op jit(solution)/shard_map/all_gather | solution.py:132
  544.4 6.9 %fusion.2 = f32[10,8,130]{2,1,0:T(8,128)S(1)} fusion(f32[2,10,8,1,8192]{4,2,1,3,0:T(8,128)} %all-gather.11.cloned.1.call-done, f32[]{:T(128)S(6)} %div.100, s32[130]{0:T(256)} %get-tuple-element.257, f32[]{:T(128)S(6)} %sub.458, s32[130]{0:T(256)} %get-tuple-element.258), kind=kOutput, calls=%fused_computation.4 | convolution fusion | flops 1027686400 | bytes 2665096 | tf_op jit(solution)/shard_map/kzxs,sj->kzxj/dot_general | solution.py:142
  551.4 5.2 fusion
  (643 shorter events, 140.4 us)
Async XLA Ops:
  7.2 111.7 %all-gather.5.cloned.1.call-start = ((), (), s32[]{:S(2)}) async-start(), calls=%async_computation | async-start | bytes 1064960 | tf_op jit(solution)/shard_map/all_gather | solution.py:132
  8.8 4.0 collective-permute-start
  11.5 3.4 collective-permute-start.1
  15.4 251.9 %all-gather.7.cloned.1.call-start = ((), (), s32[]{:S(2)}) async-start(), calls=%async_computation.1 | async-start | bytes 5324800 | tf_op jit(solution)/shard_map/all_gather | solution.py:132
  15.6 112.9 %collective-permute-start.2 = (f32[8,16,2]{2,0,1:T(8,128)S(1)}, f32[8,16,2]{2,0,1:T(8,128)S(1)}, u32[]{:S(2)}, u32[]{:S(2)}) collective-permute-start(f32[8,16,2]{2,0,1:T(8,128)S(1)} %get-tuple-element.235), channel_id=1, source_target_pairs={{0,1},{1,2},{2,3},{3,4},{4,5},{5,6},{6,7},{7,8},{8,9},{9,10},{10,1... | collective-permute-start | bytes 3080 | tf_op jit(solution)/shard_map/ppermute | solution.py:58
  16.6 111.8 %collective-permute-start.3 = (f32[8,16,2]{2,0,1:T(8,128)S(1)}, f32[8,16,2]{2,0,1:T(8,128)S(1)}, u32[]{:S(2)}, u32[]{:S(2)}) collective-permute-start(f32[8,16,2]{2,0,1:T(8,128)S(1)} %get-tuple-element.236), channel_id=1, source_target_pairs={{1,0},{2,1},{3,2},{4,3},{5,4},{6,5},{7,6},{8,7},{9,8},{10,9},{11,1... | collective-permute-start | bytes 3080 | tf_op jit(solution)/shard_map/ppermute | solution.py:60
  29.8 103.8 %copy-start.138 = (f32[18]{0:T(128)}, f32[18]{0:T(128)S(1)}, u32[]{:S(2)}) copy-start(f32[18]{0:T(128)S(1)} %slice.1779) | copy-start | bytes 220
  135.7 5.6 collective-permute-start.7
  139.7 1.6 collective-permute-start.6
  142.0 250.3 %all-gather.9.cloned.1.call-start = ((), (), s32[]{:S(2)}) async-start(), calls=%async_computation.2 | async-start | bytes 1064960 | tf_op jit(solution)/shard_map/all_gather | solution.py:132
  155.1 19.1 %collective-permute-start.5 = (f32[38,8,16,1]{0,2,3,1:T(8,128)S(1)}, f32[38,8,16,1]{0,2,3,1:T(8,128)S(1)}, u32[]{:S(2)}, u32[]{:S(2)}) collective-permute-start(f32[38,8,16,1]{0,2,3,1:T(8,128)S(1)} %copy.166), channel_id=1, source_target_pairs={{1,0},{2,1},{3,2},{4,3},{5,4},{6,5},{7,6},{8,7},{9,8},{10,9},{11,1... | collective-permute-start | bytes 58376 | tf_op jit(solution)/shard_map/ppermute | solution.py:60
  162.3 9.3 %collective-permute-start.4 = (f32[38,8,16,1]{0,2,3,1:T(8,128)S(1)}, f32[38,8,16,1]{0,2,3,1:T(8,128)S(1)}, u32[]{:S(2)}, u32[]{:S(2)}) collective-permute-start(f32[38,8,16,1]{0,2,3,1:T(8,128)S(1)} %copy.165), channel_id=1, source_target_pairs={{0,1},{1,2},{2,3},{3,4},{4,5},{5,6},{6,7},{7,8},{8,9},{9,10},{10,1... | collective-permute-start | bytes 58376 | tf_op jit(solution)/shard_map/ppermute | solution.py:58
  182.0 25.0 %copy-start.44 = (f32[8,16,130]{2,0,1:T(8,128)}, f32[8,16,130]{2,0,1:T(8,128)S(1)}, u32[]{:S(2)}) copy-start(f32[8,16,130]{2,0,1:T(8,128)S(1)} %get-tuple-element.80) | copy-start | bytes 199684
  282.4 14.4 %collective-permute-start.8 = (f32[1,8,2,128]{3,1,2,0:T(8,128)S(1)}, f32[1,8,2,128]{3,1,2,0:T(8,128)S(1)}, u32[]{:S(2)}, u32[]{:S(2)}) collective-permute-start(f32[1,8,2,128]{3,1,2,0:T(8,128)S(1)} %get-tuple-element.224), channel_id=1, source_target_pairs={{0,64},{64,128},{128,192},{192,0},{1,65},{65,129},{129,193},{193,1... | collective-permute-start | bytes 24584 | tf_op jit(solution)/shard_map/ppermute | solution.py:48
  286.3 10.5 %collective-permute-start.9 = (f32[1,8,2,128]{3,1,2,0:T(8,128)S(1)}, f32[1,8,2,128]{3,1,2,0:T(8,128)S(1)}, u32[]{:S(2)}, u32[]{:S(2)}) collective-permute-start(f32[1,8,2,128]{3,1,2,0:T(8,128)S(1)} %get-tuple-element.225), channel_id=1, source_target_pairs={{0,192},{64,0},{128,64},{192,128},{1,193},{65,1},{129,65},{193,129... | collective-permute-start | bytes 24584 | tf_op jit(solution)/shard_map/ppermute | solution.py:48
  286.3 116.1 %collective-permute-start.10 = (f32[8,16,2]{2,0,1:T(8,128)}, f32[8,16,2]{2,0,1:T(8,128)}, u32[]{:S(2)}, u32[]{:S(2)}) collective-permute-start(f32[8,16,2]{2,0,1:T(8,128)} %get-tuple-element.222), channel_id=1, source_target_pairs={{0,1},{1,2},{2,3},{3,4},{4,5},{5,6},{6,7},{7,8},{8,9},{9,10},{10,1... | collective-permute-start | bytes 3080 | tf_op jit(solution)/shard_map/ppermute | solution.py:58
  287.5 114.9 %collective-permute-start.11 = (f32[8,16,2]{2,0,1:T(8,128)}, f32[8,16,2]{2,0,1:T(8,128)}, u32[]{:S(2)}, u32[]{:S(2)}) collective-permute-start(f32[8,16,2]{2,0,1:T(8,128)} %get-tuple-element.223), channel_id=1, source_target_pairs={{1,0},{2,1},{3,2},{4,3},{5,4},{6,5},{7,6},{8,7},{9,8},{10,9},{11,1... | collective-permute-start | bytes 3080 | tf_op jit(solution)/shard_map/ppermute | solution.py:60
  297.4 247.0 %all-gather.11.cloned.1.call-start = ((), (), s32[]{:S(2)}) async-start(), calls=%async_computation.3 | async-start | bytes 5324800 | tf_op jit(solution)/shard_map/all_gather | solution.py:132
  305.4 86.9 %copy-start.153 = (s32[132]{0:T(256)S(1)}, s32[132]{0:T(256)}, u32[]{:S(2)}) copy-start(s32[132]{0:T(256)} %get-tuple-element.259) | copy-start | bytes 1588
  305.4 86.9 %copy-start.154 = (s32[132]{0:T(256)S(1)}, s32[132]{0:T(256)}, u32[]{:S(2)}) copy-start(s32[132]{0:T(256)} %get-tuple-element.260) | copy-start | bytes 1588
  412.8 5.6 collective-permute-start.15
  416.8 1.6 collective-permute-start.14
  428.1 18.8 %collective-permute-start.13 = (f32[38,8,16,1]{0,2,3,1:T(8,128)S(1)}, f32[38,8,16,1]{0,2,3,1:T(8,128)S(1)}, u32[]{:S(2)}, u32[]{:S(2)}) collective-permute-start(f32[38,8,16,1]{0,2,3,1:T(8,128)S(1)} %copy.211), channel_id=1, source_target_pairs={{1,0},{2,1},{3,2},{4,3},{5,4},{6,5},{7,6},{8,7},{9,8},{10,9},{11,1... | collective-permute-start | bytes 58376 | tf_op jit(solution)/shard_map/ppermute | solution.py:60
  435.4 9.0 %collective-permute-start.12 = (f32[38,8,16,1]{0,2,3,1:T(8,128)S(1)}, f32[38,8,16,1]{0,2,3,1:T(8,128)S(1)}, u32[]{:S(2)}, u32[]{:S(2)}) collective-permute-start(f32[38,8,16,1]{0,2,3,1:T(8,128)S(1)} %copy.210), channel_id=1, source_target_pairs={{0,1},{1,2},{2,3},{3,4},{4,5},{5,6},{6,7},{7,8},{8,9},{9,10},{10,1... | collective-permute-start | bytes 58376 | tf_op jit(solution)/shard_map/ppermute | solution.py:58
  (158 other events, 707.2 us)
Sparse Core Ops, SparseCore 0:
  15.6 103.3 all-gather.4
  142.1 125.2 all-gather.6
  297.5 94.7 all-gather.8
  419.2 125.1 all-gather.10
where the time goes:
time: 576 us; the launch traced here: 570 us
  waiting for transfers between devices  313 us (54%)
  local copies, waits for them, and re-layouts  83.9 us (15%)
  matrix products  55.4 us (10%)
  starting transfers between devices  48.1 us (8%)
  other arithmetic  44.1 us (8%)
  between operations  24.6 us (4%)
    all_gather x4, waiting for transfers between devices, align(): piece = lax.all_gather(pair, 'gy', axis=4, tiled=True)  291 us
    dot_general x8, matrix products, align(): jnp.einsum('kzxs,sj->kzxj', piece[side], table, precision=lax.Precision.H...  43.4 us
    slice x48, local copies, waits for them, and re-layouts, moved_row(): return jnp.roll(post, shift_z, axis=0)  30.2 us
    ppermute x4, starting transfers between devices, with_halo(): lax.ppermute(head, axis, [((i + 1) % count, i) for i in range(count)])  29.6 us
    ppermute x4, waiting for transfers between devices, with_halo(): lax.ppermute(tail, axis, [(i, (i + 1) % count) for i in range(count)])  16.6 us
    ppermute x8, starting transfers between devices, shifted(): return lax.ppermute(value, axis, pairs)  15.4 us
    dot_general x6, matrix products, moment(): jnp.tensordot(jnp.asarray(values, jnp.float32), field, axes=1, precision=...  12 us
  transfers between devices with their start and end apart: 20, of which 10 were waited for; matrix products, arithmetic and copies ran while one was open for 23% of the time, Pallas kernels for 0%

commit v1 on v0

v1 whole, which is shorter than its diff:
```python
import jax
import jax.numpy as jnp
from jax import lax
from jax.experimental import pallas as pl
from jax.experimental.pallas import tpu as pltpu
from jax.sharding import PartitionSpec as P

STEPS = 2
VELOCITY = (
    (0, 0, 0),
    (1, 0, 0),
    (-1, 0, 0),
    (0, 1, 0),
    (0, -1, 0),
    (0, 0, 1),
    (0, 0, -1),
    (1, 1, 0),
    (-1, -1, 0),
    (1, -1, 0),
    (-1, 1, 0),
    (1, 0, 1),
    (-1, 0, -1),
    (1, 0, -1),
    (-1, 0, 1),
    (0, 1, 1),
    (0, -1, -1),
    (0, 1, -1),
    (0, -1, 1),
)
WEIGHTS = (1.0 / 3.0,) + (1.0 / 18.0,) * 6 + (1.0 / 36.0,) * 12
UPWARD = (1, 7, 9, 11, 13)
DOWNWARD = (2, 8, 10, 12, 14)
Y_PLUS = (3, 7, 10, 15, 17)
Y_MINUS = (4, 8, 9, 16, 18)
COEF_A = -0.0625
COEF_B = 0.0625
KAPPA_GRAD = 0.04
MOBILITY = 1.0
TAU_FLUID = 0.8
TAU_ORDER = 0.9
NZ = 8
LX = 16
LY = 128
N_SEC = 4
N_GY = 64
SPAN = LY * N_GY * 256
ROLES = 20
MESH = pl.DeviceIdType.MESH


def lanes(shape):
    return lax.broadcasted_iota(jnp.int32, shape, len(shape) - 1)


def turn(value, shift):
    return pltpu.roll(value, shift, value.ndim - 1)


def signed_sum(terms, signs):
    total = None
    for term, sign in zip(terms, signs):
        if sign == 0:
            continue
        if total is None:
            total = term if sign > 0 else -term
        else:
            total = total + term if sign > 0 else total - term
    return total


def wait_bytes(ref, sem):
    pltpu.make_async_copy(ref, ref, sem).wait()


def slid_block(land, slot, block, offset):
    offset = offset & (LY * N_GY - 1)
    first = block + (offset >> 7)
    inside = offset & (LY - 1)
    here = land[slot, first & (N_GY - 1)]
    beyond = land[slot, (first + 1) & (N_GY - 1)]
    shift = (LY - inside) & (LY - 1)
    return jnp.where(lanes(here.shape) < LY - inside, turn(here, shift), turn(beyond, shift))


def kernel(
    fluid_in, order_in, offsets, speeds, fluid_out, order_out,
    state, post, field, pot, mom, face,
    a_up, a_down, a_edge, a_land, a_slid, a_ghost, a_near,
    b_send, b_edge, b_land, b_slid, b_ghost, b_near,
    in_sem, out_sem, send_sem, recv_sem,
):
    sec = lax.axis_index("sec")
    gy = lax.axis_index("gy")
    above = (sec + 1) & (N_SEC - 1)
    below = (sec + N_SEC - 1) & (N_SEC - 1)
    left = (gy + N_GY - 1) & (N_GY - 1)
    right = (gy + 1) & (N_GY - 1)
    is_down = gy & 1
    owner = gy >> 1
    a_z = owner & 7
    a_part = owner >> 3
    b_role = (5 * owner + 7) >> 3
    is_owner = jnp.logical_and((8 * b_role) // 5 == owner, b_role < ROLES)

    load_order = pltpu.make_async_copy(order_in, state.at[pl.ds(19, 19)], in_sem.at[0])
    load_order.start()
    load_fluid = pltpu.make_async_copy(fluid_in, state.at[pl.ds(0, 19)], in_sem.at[1])
    load_fluid.start()

    barrier = pltpu.get_barrier_semaphore()
    source_sec = jnp.where(is_down == 0, below, above)

    def greet_source(j, carry):
        pl.semaphore_signal(
            barrier, inc=1, device_id=(source_sec, (gy + j) & (N_GY - 1)), device_id_type=MESH
        )
        return carry

    def greet_own(j, carry):
        pl.semaphore_signal(
            barrier, inc=1, device_id=(sec, (gy + j) & (N_GY - 1)), device_id_type=MESH
        )
        return carry

    lax.fori_loop(0, N_GY, greet_source, 0, unroll=8)
    lax.fori_loop(1, N_GY, greet_own, 0, unroll=7)

    plane = (LX, LY)
    lane = lanes(plane)
    row = lax.broadcasted_iota(jnp.int32, plane, 0)
    field[...] = jnp.zeros_like(field)

    def order_pass():
        def one(z, carry):
            to_left, to_right = carry
            phi = state[19, z]
            for i in range(1, 19):
                phi = phi + state[19 + i, z]
            field[z, pl.ds(8, LX), pl.ds(0, LY)] = phi
            a_up[z] = phi[LX - 2 :]
            a_down[z] = phi[:2]
            mine = (lane >> 1) == z
            to_left = jnp.where(mine, turn(phi, 2 * z), to_left)
            to_right = jnp.where(mine, turn(phi, 2 * z + 2), to_right)
            return to_left, to_right

        zero = jnp.zeros(plane, jnp.float32)
        to_left, to_right = lax.fori_loop(0, NZ, one, (zero, zero))
        a_edge[0] = to_left
        a_edge[1] = to_right

    def send(src, dst, which, slot, to_sec, to_gy):
        pltpu.make_async_remote_copy(
            src_ref=src,
            dst_ref=dst,
            send_sem=send_sem.at[which],
            recv_sem=recv_sem.at[which, slot],
            device_id=(to_sec, to_gy),
            device_id_type=MESH,
        ).start()

    load_order.wait()
    order_pass()
    load_fluid.wait()
    pl.semaphore_wait(barrier, 2 * N_GY - 1)

    def step_body(step, carry):
        here_units = offsets[step, sec]
        next_units = offsets[step, above]
        units = jnp.where(is_down == 0, here_units, (SPAN - next_units) & (SPAN - 1))
        whole = units >> 8
        frac = (units & 255).astype(jnp.float32) * (1.0 / 256.0)
        keep = 1.0 - frac

        def send_order(j, carry):
            z = (j + gy) & (NZ - 1)
            for k in range(4):
                target = 2 * (8 * ((k + (gy >> 4)) & 3) + z)
                send(a_up.at[z], a_land.at[step, gy], 0, step, above, target)
                send(a_down.at[z], a_land.at[step, gy], 0, step, below, target + 1)
            return carry

        lax.fori_loop(0, NZ, send_order, 0, unroll=2)
        send(a_edge.at[0], a_near.at[step, 1], 1, step, sec, left)
        send(a_edge.at[1], a_near.at[step, 0], 1, step, sec, right)

        def moments(z, carry):
            tiles = [state[i, z] for i in range(19)]
            mom[0, z] = signed_sum(tiles, (1,) * 19)
            for axis in range(3):
                mom[1 + axis, z] = signed_sum(tiles, [vector[axis] for vector in VELOCITY])
            return carry

        lax.fori_loop(0, NZ, moments, 0)

        wait_bytes(a_land.at[step], recv_sem.at[0, step])

        def slide_order(block):
            values = [slid_block(a_land, step, block, whole + shift) for shift in (-1, 0, 1, 2)]
            for k in range(3):
                a_slid[block & 15, k] = keep * values[k] + frac * values[k + 1]

        a_role = 8 * is_down + a_z
        slide_order(gy)
        pltpu.make_async_copy(
            a_slid.at[gy & 15], a_ghost.at[step, a_role], recv_sem.at[2, step]
        ).start()

        def send_slid_order(j, carry):
            block = 16 * a_part + ((gy + j) & 15)
            slide_order(block)
            send(a_slid.at[block & 15], a_ghost.at[step, a_role], 2, step, sec, block)
            return carry

        lax.fori_loop(1, 16, send_slid_order, 0, unroll=5)

        wait_bytes(a_near.at[step], recv_sem.at[1, step])
        from_left = a_near[step, 0]
        from_right = a_near[step, 1]

        def put_columns(z, carry):
            field[z, pl.ds(8, LX), pl.ds(LY, LY)] = jnp.where(
                lane < 2,
                turn(from_right, (LY - 2 * z) & (LY - 1)),
                jnp.where(lane >= LY - 2, turn(from_left, (LY - 2 - 2 * z) & (LY - 1)), 0.0),
            )
            return carry

        lax.fori_loop(0, NZ, put_columns, 0)

        wait_bytes(a_ghost.at[step], recv_sem.at[2, step])
        pair = lanes((2, LY))

        def put_ghosts(z, carry):
            for side, start in ((0, 6), (1, 24)):
                rows = [a_ghost[step, 8 * side + z, k] for k in range(3)]
                field[z, pl.ds(start, 2), pl.ds(0, LY)] = rows[1]
                field[z, pl.ds(start, 2), pl.ds(LY, LY)] = jnp.where(
                    pair == 0, turn(rows[2], 1), jnp.where(pair == LY - 1, turn(rows[0], LY - 1), 0.0)
                )
            return carry

        lax.fori_loop(0, NZ, put_ghosts, 0)

        def potentials(z, carry):
            tall = lanes((32, LY))
            tiles = [field[z, :, pl.ds(0, LY)], field[z, :, pl.ds(LY, LY)]]
            ahead = [turn(tile, LY - 1) for tile in tiles]
            behind = [turn(tile, 1) for tile in tiles]
            for k in range(2):
                tile = tiles[k]
                cut = pl.ds(k * LY, LY)
                lap = (
                    pltpu.roll(tile, 1, 0)
                    + pltpu.roll(tile, 31, 0)
                    + jnp.where(tall == LY - 1, ahead[1 - k], ahead[k])
                    + jnp.where(tall == 0, behind[1 - k], behind[k])
                    + field[(z + 1) & 7, :, cut]
                    + field[(z + 7) & 7, :, cut]
                    - 6.0 * tile
                )
                pot[z, :, cut] = tile * (COEF_A + COEF_B * tile * tile) - KAPPA_GRAD * lap
            return carry

        lax.fori_loop(0, NZ, potentials, 0)

        def collide(z, carry):
            to_left, to_right = carry
            own = pl.ds(0, LY)
            inner = pot[z, pl.ds(8, LX), own]
            halo = pot[z, pl.ds(8, LX), pl.ds(LY, LY)]
            phi = field[z, pl.ds(8, LX), own]
            half = -0.5 * phi
            force = (
                half * (pot[z, pl.ds(9, LX), own] - pot[z, pl.ds(7, LX), own]),
                half
                * (
                    jnp.where(lane == LY - 1, turn(halo, LY - 1), turn(inner, LY - 1))
                    - jnp.where(lane == 0, turn(halo, 1), turn(inner, 1))
                ),
                half * (pot[(z + 1) & 7, pl.ds(8, LX), own] - pot[(z + 7) & 7, pl.ds(8, LX), own]),
            )
            density = mom[0, z]
            inverse = 1.0 / density
            vel = tuple((mom[1 + k, z] + 0.5 * force[k]) * inverse for k in range(3))
            square = vel[0] * vel[0] + vel[1] * vel[1] + vel[2] * vel[2]
            drift = vel[0] * force[0] + vel[1] * force[1] + vel[2] * force[2]
            kick = 1.0 - 0.5 / TAU_FLUID
            scaled = density * (1.0 / TAU_FLUID)
            base = scaled * (1.0 - 1.5 * square) - (3.0 * kick) * drift
            square_phi = phi * (1.0 / TAU_ORDER)
            base_phi = (3.0 * MOBILITY / TAU_ORDER) * inner - 1.5 * square_phi * square
            left_f = 1.0 - 1.0 / TAU_FLUID
            left_g = 1.0 - 1.0 / TAU_ORDER
            fluid = [None] * 19
            order = [None] * 19
            fluid[0] = left_f * state[0, z] + WEIGHTS[0] * base
            order[0] = left_g * state[19, z] + (
                square_phi * (1.0 - 0.5 * square) - (2.0 * MOBILITY / TAU_ORDER) * inner
            )
            for i in range(1, 19, 2):
                vector = VELOCITY[i]
                along = signed_sum(vel, vector)
                pushed = signed_sum(force, vector)
                weight = WEIGHTS[i]
                even = weight * (base + along * (4.5 * scaled * along + (9.0 * kick) * pushed))
                odd = weight * (3.0 * scaled * along + (3.0 * kick) * pushed)
                fluid[i] = left_f * state[i, z] + (even + odd)
                fluid[i + 1] = left_f * state[i + 1, z] + (even - odd)
                carried = square_phi * along
                even = weight * (base_phi + 4.5 * carried * along)
                odd = (3.0 * weight) * carried
                order[i] = left_g * state[19 + i, z] + (even + odd)
                order[i + 1] = left_g * state[20 + i, z] + (even - odd)
            for i in range(19):
                post[i, z] = fluid[i]
                post[19 + i, z] = order[i]
            for side, members, x in ((0, UPWARD, LX - 1), (1, DOWNWARD, 0)):
                rows = [fluid[i] for i in members] + [order[i] for i in members]
                rows += [density, phi, vel[0], vel[1], vel[2]]
                for k, tile in enumerate(rows):
                    face[side, k, pl.ds(z, 1), :] = tile[x : x + 1, :]
            going_left = jnp.zeros(plane, jnp.float32)
            going_right = jnp.zeros(plane, jnp.float32)
            for k in range(10):
                part = fluid if k < 5 else order
                going_right = jnp.where(
                    lane == 8 * k, turn(part[Y_PLUS[k % 5]], 8 * k + 1), going_right
                )
                going_left = jnp.where(
                    lane == 8 * k, turn(part[Y_MINUS[k % 5]], 8 * k), going_left
                )
            mine = (lane & 7) == z
            to_left = jnp.where(mine, turn(going_left, z), to_left)
            to_right = jnp.where(mine, turn(going_right, z), to_right)
            return to_left, to_right

        zero = jnp.zeros(plane, jnp.float32)
        to_left, to_right = lax.fori_loop(0, NZ, collide, (zero, zero))
        b_edge[0] = to_left
        b_edge[1] = to_right

        jump_up = speeds[above].astype(jnp.float32) * (-1.0 / 256.0)
        jump_down = speeds[sec].astype(jnp.float32) * (1.0 / 256.0)
        for side, members, jump in ((0, UPWARD, jump_up), (1, DOWNWARD, jump_down)):
            density, phi, vel_x, vel_y, vel_z = [face[side, 10 + k] for k in range(5)]
            moved = vel_y + jump
            change_square = 1.5 * (moved * moved - vel_y * vel_y)
            for k, i in enumerate(members):
                vector = VELOCITY[i]
                before = signed_sum((vel_x, vel_y, vel_z), vector)
                after = signed_sum((vel_x, moved, vel_z), vector)
                change = WEIGHTS[i] * (
                    3.0 * (after - before) + 4.5 * (after * after - before * before) - change_square
                )
                for lift, mass in ((0, density), (5, phi)):
                    value = face[side, k + lift] + mass * change
                    b_send[side, 2 * (k + lift)] = value[:4]
                    b_send[side, 2 * (k + lift) + 1] = value[4:]

        def send_ghost(j, carry):
            role = lax.rem(j + gy, ROLES)
            target = 2 * ((8 * role) // 5)
            send(b_send.at[0, role], b_land.at[step, gy], 3, step, above, target)
            send(b_send.at[1, role], b_land.at[step, gy], 3, step, below, target + 1)
            return carry

        lax.fori_loop(0, ROLES, send_ghost, 0, unroll=5)
        send(b_edge.at[0], b_near.at[step, 1], 4, step, sec, left)
        send(b_edge.at[1], b_near.at[step, 0], 4, step, sec, right)

        @pl.when(is_owner)
        def _():
            wait_bytes(b_land.at[step], recv_sem.at[3, step])
            member = lax.rem(b_role >> 1, 5)
            along_y = jnp.where(member == 1, 1, jnp.where(member == 2, -1, 0)) * (1 - 2 * is_down)
            start = whole - along_y
            b_slot = ROLES * is_down + b_role

            def slide_ghost(block):
                b_slid[block] = keep * slid_block(b_land, step, block, start) + frac * slid_block(
                    b_land, step, block, start + 1
                )

            slide_ghost(gy)
            pltpu.make_async_copy(
                b_slid.at[gy], b_ghost.at[step, b_slot], recv_sem.at[5, step]
            ).start()

            def send_slid_ghost(j, carry):
                block = (gy + j) & (N_GY - 1)
                slide_ghost(block)
                send(b_slid.at[block], b_ghost.at[step, b_slot], 5, step, sec, block)
                return carry

            lax.fori_loop(1, N_GY, send_slid_ghost, 0, unroll=7)

        wait_bytes(b_near.at[step], recv_sem.at[4, step])
        near_left = b_near[step, 0]
        near_right = b_near[step, 1]

        def stream(z, carry):
            columns = {}
            for shift_z in (-1, 0, 1):
                source = (z - shift_z) & 7
                back = (LY - source) & (LY - 1)
                columns[1, shift_z] = turn(near_left, back)
                columns[-1, shift_z] = turn(near_right, back)
            for which in range(38):
                i = which % 19
                shift_x, shift_y, shift_z = VELOCITY[i]
                tile = post[which, (z - shift_z) & 7]
                if shift_y == 1:
                    k = Y_PLUS.index(i) + (5 if which >= 19 else 0)
                    outer = turn(columns[1, shift_z], (LY - 8 * k) % LY)
                    tile = jnp.where(lane == 0, outer, turn(tile, 1))
                elif shift_y == -1:
                    k = Y_MINUS.index(i) + (5 if which >= 19 else 0)
                    outer = turn(columns[-1, shift_z], (LY - 1 - 8 * k) % LY)
                    tile = jnp.where(lane == LY - 1, outer, turn(tile, LY - 1))
                if shift_x:
                    tile = pltpu.roll(tile, shift_x % LX, 0)
                state[which, z] = tile
            return carry

        lax.fori_loop(0, NZ, stream, 0)

        wait_bytes(a_land.at[step], send_sem.at[0])
        wait_bytes(a_edge, send_sem.at[1])
        wait_bytes(a_slid.at[pl.ds(0, 15)], send_sem.at[2])
        wait_bytes(b_send, send_sem.at[3])
        wait_bytes(b_edge, send_sem.at[4])

        @pl.when(is_owner)
        def _():
            wait_bytes(b_slid.at[pl.ds(0, N_GY - 1)], send_sem.at[5])

        wait_bytes(b_ghost.at[step], recv_sem.at[5, step])
        for side, members, x in ((0, UPWARD, 0), (1, DOWNWARD, LX - 1)):
            for k in range(10):
                i = members[k % 5]
                which = i + (19 if k >= 5 else 0)
                for z in range(NZ):
                    source = (z - VELOCITY[i][2]) % NZ
                    slot = ROLES * side + 2 * k + source // 4
                    state[which, z, pl.ds(x, 1), :] = b_ghost[step, slot, pl.ds(source % 4, 1), :]

        @pl.when(step < STEPS - 1)
        def _():
            order_pass()

        return carry

    lax.fori_loop(0, STEPS, step_body, 0)
    store_fluid = pltpu.make_async_copy(state.at[pl.ds(0, 19)], fluid_out, out_sem.at[0])
    store_order = pltpu.make_async_copy(state.at[pl.ds(19, 19)], order_out, out_sem.at[1])
    store_fluid.start()
    store_order.start()
    store_fluid.wait()
    store_order.wait()


def per_device(fluid_dist, order_dist, plane_offset, plane_speed):
    shape = jax.ShapeDtypeStruct((19, NZ, LX, LY), jnp.float32)

    def scratch(*dims):
        return pltpu.VMEM(dims, jnp.float32)

    return pl.pallas_call(
        kernel,
        out_shape=(shape, shape),
        in_specs=[
            pl.BlockSpec(memory_space=pl.ANY),
            pl.BlockSpec(memory_space=pl.ANY),
            pl.BlockSpec(memory_space=pltpu.SMEM),
            pl.BlockSpec(memory_space=pltpu.SMEM),
        ],
        out_specs=(pl.BlockSpec(memory_space=pl.ANY), pl.BlockSpec(memory_space=pl.ANY)),
        scratch_shapes=[
            scratch(38, NZ, LX, LY),
            scratch(38, NZ, LX, LY),
            scratch(NZ, 32, 2 * LY),
            scratch(NZ, 32, 2 * LY),
            scratch(4, NZ, LX, LY),
            scratch(2, 15, NZ, LY),
            scratch(NZ, 2, LY),
            scratch(NZ, 2, LY),
            scratch(2, LX, LY),
            scratch(STEPS, N_GY, 2, LY),
            scratch(16, 3, 2, LY),
            scratch(STEPS, 16, 3, 2, LY),
            scratch(STEPS, 2, LX, LY),
            scratch(2, ROLES, 4, LY),
            scratch(2, LX, LY),
            scratch(STEPS, N_GY, 4, LY),
            scratch(N_GY, 4, LY),
            scratch(STEPS, 2 * ROLES, 4, LY),
            scratch(STEPS, 2, LX, LY),
            pltpu.SemaphoreType.DMA((2,)),
            pltpu.SemaphoreType.DMA((2,)),
            pltpu.SemaphoreType.DMA((6,)),
            pltpu.SemaphoreType.DMA((6, STEPS)),
        ],
        compiler_params=pltpu.CompilerParams(
            collective_id=0, has_side_effects=True, vmem_limit_bytes=40 * 1024 * 1024
        ),
    )(fluid_dist, order_dist, plane_offset, plane_speed)


def solution(mesh):
    split = P(None, None, "sec", "gy")
    return jax.shard_map(
        per_device,
        mesh=mesh,
        in_specs=(split, split, P(), P()),
        out_specs=(split, split),
        check_vma=False,
    )
```

time: 576 us -> 87 us (0.15); the launches traced: 570 us -> 86.9 us
  waiting for transfers between devices: 313 us -> 0 us
  Pallas kernels: 0 us -> 80.2 us
  local copies, waits for them, and re-layouts: 83.9 us -> 5.98 us
  matrix products: 55.4 us -> 0 us
  starting transfers between devices: 48.1 us -> 0 us
  other arithmetic: 44.1 us -> 0 us
  between operations: 24.6 us -> 0.65 us
    all_gather x4 -> x0, waiting for transfers between devices: 291 us -> none  [align(): piece = lax.all_gather(pair, 'gy', axis=4, tiled=True)]
    pallas_call x0 -> x1, Pallas kernels: none -> 80.2 us  [per_device(): pl.pallas_call(kernel, out_shape=(shape, shape), in_specs=[pl.BlockSpec(m...]
    slice x104 -> x0, local copies, waits for them, and re-layouts: 58.5 us -> none  [the longest x48 30.2 us: moved_row(): return jnp.roll(post, shift_z, axis=0)]
    dot_general x14 -> x0, matrix products: 55.4 us -> none  [the longest x8 43.4 us: align(): jnp.einsum('kzxs,sj->kzxj', piece[side], table, precision=lax.Precision.H...]
    ppermute x16 -> x0, starting transfers between devices: 47.9 us -> none  [the longest x4 29.6 us: with_halo(): lax.ppermute(head, axis, [((i + 1) % count, i) for i in range(count)])]
    ppermute x16 -> x0, waiting for transfers between devices: 22.2 us -> none  [the longest x4 16.6 us: with_halo(): lax.ppermute(tail, axis, [(i, (i + 1) % count) for i in range(count)])]
    concatenate x18 -> x0, other arithmetic: 18.5 us -> none  [the longest x2 8.88 us: with_halo(): jnp.concatenate([lax.ppermute(tail, axis, [(i, (i + 1) % count) for i in...]
    ppermute x4 -> x0, local copies, waits for them, and re-layouts: 10.1 us -> none  [the longest x2 5.17 us: with_halo(): lax.ppermute(tail, axis, [(i, (i + 1) % count) for i in range(count)])]
  transfers between devices with their start and end apart: 20 -> 0, of which waited for: 10 -> 0; matrix products, arithmetic and copies ran while one was open for 23% -> 0% of each run, Pallas kernels for 0% -> 0%
where the time goes in v1:
time: 87 us; the launch traced here: 86.9 us
  Pallas kernels  80.2 us (92%)
  local copies, waits for them, and re-layouts  5.98 us (7%)
    pallas_call x1, Pallas kernels, per_device(): pl.pallas_call(kernel, out_shape=(shape, shape), in_specs=[pl.BlockSpec(m...  80.2 us
    unnamed x10, local copies, waits for them, and re-layouts  5.98 us

profile of v1, /device:TPU:1, one launch (start us, length us, event | category | flops | bytes accessed | tf_op | source)
XLA Modules:
  0.0 86.9 jit_solution(6701256542559564593)
XLA Ops:
  0.6 0.0 copy-start
  0.6 1.3 %copy-done = f32[19,8,16,128]{3,2,1,0:T(8,128)S(1)} copy-done((f32[19,8,16,128]{3,2,1,0:T(8,128)S(1)}, f32[19,8,16,128]{3,2,1,0:T(8,128)}, u32[]{:S(2)}) %copy-start) | copy-done | bytes 1245208
  1.9 0.0 copy-start.1
  1.9 1.3 %copy-done.1 = f32[19,8,16,128]{3,2,1,0:T(8,128)S(1)} copy-done((f32[19,8,16,128]{3,2,1,0:T(8,128)S(1)}, f32[19,8,16,128]{3,2,1,0:T(8,128)}, u32[]{:S(2)}) %copy-start.1) | copy-done | bytes 1245208
  3.2 0.0 copy-start.2
  3.2 0.7 copy-done.2
  3.9 0.0 copy-start.3
  3.9 0.7 copy-done.3
  4.6 80.2 %shard_map.59 = (f32[19,8,16,128]{3,2,1,0:T(8,128)S(1)}, f32[19,8,16,128]{3,2,1,0:T(8,128)S(1)}) custom-call(f32[19,8,16,128]{3,2,1,0:T(8,128)S(1)} %copy-done, f32[19,8,16,128]{3,2,1,0:T(8,128)S(1)} %copy-done.1, s32[2,4]{1,0:T(2,128)S(1)} %copy-done.2, s32[4]{0:T(128)S(1)} %copy-done.3), custom_call_target="tpu_custom_call" | custom-call | tf_op jit(solution)/shard_map/pallas_call | solution.py:469
  84.8 1.0 %copy.8 = f32[19,8,16,128]{3,2,1,0:T(8,128)} copy(f32[19,8,16,128]{3,2,1,0:T(8,128)S(1)} %get-tuple-element.4) | data formatting | bytes 2490368
  85.8 1.0 %copy.9 = f32[19,8,16,128]{3,2,1,0:T(8,128)} copy(f32[19,8,16,128]{3,2,1,0:T(8,128)S(1)} %get-tuple-element.5) | data formatting | bytes 2490368
Async XLA Ops:
  0.6 1.3 %copy-start = (f32[19,8,16,128]{3,2,1,0:T(8,128)S(1)}, f32[19,8,16,128]{3,2,1,0:T(8,128)}, u32[]{:S(2)}) copy-start(f32[19,8,16,128]{3,2,1,0:T(8,128)} %fluid_in.1) | copy-start | bytes 3735556
  1.9 1.3 %copy-start.1 = (f32[19,8,16,128]{3,2,1,0:T(8,128)S(1)}, f32[19,8,16,128]{3,2,1,0:T(8,128)}, u32[]{:S(2)}) copy-start(f32[19,8,16,128]{3,2,1,0:T(8,128)} %order_in.1) | copy-start | bytes 3735556
  3.2 0.7 copy-start.2
  3.9 0.7 copy-start.3

commit v2 on v1

--- a/solution.py
+++ b/solution.py
@@ -46,6 +46,7 @@
 SPAN = LY * N_GY * 256
 ROLES = 20
 MESH = pl.DeviceIdType.MESH
+ACROSS = ((1, 2), (1, 1), (1, 3), (0, 2), (1, 0), (0, 1), (0, 3), (0, 0))
 
 
 def lanes(shape):
@@ -54,6 +55,16 @@
 
 def turn(value, shift):
     return pltpu.roll(value, shift, value.ndim - 1)
+
+
+def ring_z(gy, k):
+    half = (k + 1) >> 1
+    return ((gy >> 2) + 4 + jnp.where((k & 1) == 1, -half, half)) & 7
+
+
+def far_first(gy, k, m):
+    across, along = ACROSS[m]
+    return (((gy >> 5) ^ across) << 5) + (ring_z(gy, k) << 2) + ((gy + along) & 3)
 
 
 def signed_sum(terms, signs):
@@ -83,8 +94,8 @@
 
 
 def kernel(
-    fluid_in, order_in, offsets, speeds, fluid_out, order_out,
-    state, post, field, pot, mom, face,
+    fluid_in, order_in, offsets_in, speeds_in, fluid_out, order_out,
+    offsets, speeds, state, post, field, pot, mom,
     a_up, a_down, a_edge, a_land, a_slid, a_ghost, a_near,
     b_send, b_edge, b_land, b_slid, b_ghost, b_near,
     in_sem, out_sem, send_sem, recv_sem,
@@ -104,26 +115,34 @@
 
     load_order = pltpu.make_async_copy(order_in, state.at[pl.ds(19, 19)], in_sem.at[0])
     load_order.start()
+    load_offsets = pltpu.make_async_copy(offsets_in, offsets, in_sem.at[2])
+    load_offsets.start()
+    load_speeds = pltpu.make_async_copy(speeds_in, speeds, in_sem.at[3])
+    load_speeds.start()
     load_fluid = pltpu.make_async_copy(fluid_in, state.at[pl.ds(0, 19)], in_sem.at[1])
     load_fluid.start()
 
     barrier = pltpu.get_barrier_semaphore()
     source_sec = jnp.where(is_down == 0, below, above)
 
-    def greet_source(j, carry):
+    def greet(k, carry):
+        for m in range(8):
+            other = far_first(gy, k, m)
+            pl.semaphore_signal(
+                barrier, inc=1, device_id=(source_sec, other), device_id_type=MESH
+            )
+            if m < 7:
+                pl.semaphore_signal(barrier, inc=1, device_id=(sec, other), device_id_type=MESH)
+        return carry
+
+    def greet_rest(k, carry):
         pl.semaphore_signal(
-            barrier, inc=1, device_id=(source_sec, (gy + j) & (N_GY - 1)), device_id_type=MESH
+            barrier, inc=1, device_id=(sec, far_first(gy, k, 7)), device_id_type=MESH
         )
         return carry
 
-    def greet_own(j, carry):
-        pl.semaphore_signal(
-            barrier, inc=1, device_id=(sec, (gy + j) & (N_GY - 1)), device_id_type=MESH
-        )
-        return carry
-
-    lax.fori_loop(0, N_GY, greet_source, 0, unroll=8)
-    lax.fori_loop(1, N_GY, greet_own, 0, unroll=7)
+    lax.fori_loop(0, 8, greet, 0)
+    lax.fori_loop(0, 7, greet_rest, 0)
 
     plane = (LX, LY)
     lane = lanes(plane)
@@ -132,22 +151,94 @@
 
     def order_pass():
         def one(z, carry):
-            to_left, to_right = carry
             phi = state[19, z]
             for i in range(1, 19):
                 phi = phi + state[19 + i, z]
             field[z, pl.ds(8, LX), pl.ds(0, LY)] = phi
-            a_up[z] = phi[LX - 2 :]
-            a_down[z] = phi[:2]
+            return carry
+
+        lax.fori_loop(0, NZ, one, 0)
+
+    def pack_order():
+        for j in range(2):
+            a_up[:, j, :] = field[:, 8 + LX - 2 + j, pl.ds(0, LY)]
+            a_down[:, j, :] = field[:, 8 + j, pl.ds(0, LY)]
+        to_left = jnp.zeros(plane, jnp.float32)
+        to_right = to_left
+        for z in range(NZ):
+            phi = field[z, pl.ds(8, LX), pl.ds(0, LY)]
             mine = (lane >> 1) == z
             to_left = jnp.where(mine, turn(phi, 2 * z), to_left)
             to_right = jnp.where(mine, turn(phi, 2 * z + 2), to_right)
-            return to_left, to_right
-
-        zero = jnp.zeros(plane, jnp.float32)
-        to_left, to_right = lax.fori_loop(0, NZ, one, (zero, zero))
         a_edge[0] = to_left
         a_edge[1] = to_right
+
+    def next_y(near, far):
+        tile = lanes(near.shape)
+        return jnp.where(tile == LY - 1, turn(far, LY - 1), turn(near, LY - 1))
+
+    def last_y(near, far):
+        tile = lanes(near.shape)
+        return jnp.where(tile == 0, turn(far, 1), turn(near, 1))
+
+    def face_potential(x, half):
+        cut = pl.ds(half * LY, LY)
+        tile = field[:, 8 + x, cut]
+        other = field[:, 8 + x, pl.ds((1 - half) * LY, LY)]
+        lap = (
+            field[:, 9 + x, cut]
+            + field[:, 7 + x, cut]
+            + next_y(tile, other)
+            + last_y(tile, other)
+            + pltpu.roll(tile, 1, 0)
+            + pltpu.roll(tile, NZ - 1, 0)
+            - 6.0 * tile
+        )
+        return tile * (COEF_A + COEF_B * tile * tile) - KAPPA_GRAD * lap
+
+    def face_collide(side, members, x, jump):
+        phi = field[:, 8 + x, pl.ds(0, LY)]
+        middle = face_potential(x, 0)
+        beyond = face_potential(x, 1)
+        half = -0.5 * phi
+        force = (
+            half * (face_potential(x + 1, 0) - face_potential(x - 1, 0)),
+            half * (next_y(middle, beyond) - last_y(middle, beyond)),
+            half * (pltpu.roll(middle, NZ - 1, 0) - pltpu.roll(middle, 1, 0)),
+        )
+        density = mom[0, :, x, :]
+        inverse = 1.0 / density
+        vel = tuple((mom[1 + k, :, x, :] + 0.5 * force[k]) * inverse for k in range(3))
+        square = vel[0] * vel[0] + vel[1] * vel[1] + vel[2] * vel[2]
+        drift = vel[0] * force[0] + vel[1] * force[1] + vel[2] * force[2]
+        kick = 1.0 - 0.5 / TAU_FLUID
+        scaled = density * (1.0 / TAU_FLUID)
+        base = scaled * (1.0 - 1.5 * square) - (3.0 * kick) * drift
+        square_phi = phi * (1.0 / TAU_ORDER)
+        base_phi = (3.0 * MOBILITY / TAU_ORDER) * middle - 1.5 * square_phi * square
+        moved = vel[1] + jump
+        change_square = 1.5 * (moved * moved - vel[1] * vel[1])
+        for k, i in enumerate(members):
+            vector = VELOCITY[i]
+            weight = WEIGHTS[i]
+            along = signed_sum(vel, vector)
+            pushed = signed_sum(force, vector)
+            after = signed_sum((vel[0], moved, vel[2]), vector)
+            change = weight * (
+                3.0 * (after - along) + 4.5 * (after * after - along * along) - change_square
+            )
+            fluid = (1.0 - 1.0 / TAU_FLUID) * state[i, :, x, :] + weight * (
+                base
+                + along * (4.5 * scaled * along + (9.0 * kick) * pushed)
+                + (3.0 * scaled * along + (3.0 * kick) * pushed)
+            )
+            carried = square_phi * along
+            order = (1.0 - 1.0 / TAU_ORDER) * state[19 + i, :, x, :] + weight * (
+                base_phi + 4.5 * carried * along + 3.0 * carried
+            )
+            for lift, value in ((0, fluid + density * change), (5, order + phi * change)):
+                b_send[side, 2 * (k + lift)] = value[:4]
+                b_send[side, 2 * (k + lift) + 1] = value[4:]
 
     def send(src, dst, which, slot, to_sec, to_gy):
         pltpu.make_async_remote_copy(
@@ -161,7 +252,10 @@
 
     load_order.wait()
     order_pass()
+    pack_order()
     load_fluid.wait()
+    load_offsets.wait()
+    load_speeds.wait()
     pl.semaphore_wait(barrier, 2 * N_GY - 1)
 
     def step_body(step, carry):
@@ -172,15 +266,17 @@
         frac = (units & 255).astype(jnp.float32) * (1.0 / 256.0)
         keep = 1.0 - frac
 
-        def send_order(j, carry):
-            z = (j + gy) & (NZ - 1)
-            for k in range(4):
-                target = 2 * (8 * ((k + (gy >> 4)) & 3) + z)
+        def send_order(k, carry):
+            for across, along in ((1, 1), (1, 0), (0, 1), (0, 0)):
+                target = (
+                    (((gy >> 5) ^ across) << 5) + (ring_z(gy, k) << 2) + ((gy & 2) ^ (2 * along))
+                )
+                z = (target >> 1) & 7
                 send(a_up.at[z], a_land.at[step, gy], 0, step, above, target)
                 send(a_down.at[z], a_land.at[step, gy], 0, step, below, target + 1)
             return carry
 
-        lax.fori_loop(0, NZ, send_order, 0, unroll=2)
+        lax.fori_loop(0, 8, send_order, 0, unroll=2)
         send(a_edge.at[0], a_near.at[step, 1], 1, step, sec, left)
         send(a_edge.at[1], a_near.at[step, 0], 1, step, sec, right)
 
@@ -207,7 +303,7 @@
         ).start()
 
         def send_slid_order(j, carry):
-            block = 16 * a_part + ((gy + j) & 15)
+            block = gy ^ (16 - j)
             slide_order(block)
             send(a_slid.at[block & 15], a_ghost.at[step, a_role], 2, step, sec, block)
             return carry
@@ -229,18 +325,31 @@
         lax.fori_loop(0, NZ, put_columns, 0)
 
         wait_bytes(a_ghost.at[step], recv_sem.at[2, step])
-        pair = lanes((2, LY))
-
-        def put_ghosts(z, carry):
-            for side, start in ((0, 6), (1, 24)):
-                rows = [a_ghost[step, 8 * side + z, k] for k in range(3)]
-                field[z, pl.ds(start, 2), pl.ds(0, LY)] = rows[1]
-                field[z, pl.ds(start, 2), pl.ds(LY, LY)] = jnp.where(
-                    pair == 0, turn(rows[2], 1), jnp.where(pair == LY - 1, turn(rows[0], LY - 1), 0.0)
-                )
-            return carry
-
-        lax.fori_loop(0, NZ, put_ghosts, 0)
+        rim = lanes((NZ, LY))
+        for side, near_x, far_x in ((0, -1, -2), (1, LX, LX + 1)):
+            roles = pl.ds(8 * side, 8)
+            place = 1 - side
+            field[:, 8 + near_x, pl.ds(0, LY)] = a_ghost[step, roles, 1, place, :]
+            field[:, 8 + far_x, pl.ds(0, LY)] = a_ghost[step, roles, 1, 1 - place, :]
+            field[:, 8 + near_x, pl.ds(LY, LY)] = jnp.where(
+                rim == 0,
+                turn(a_ghost[step, roles, 2, place, :], 1),
+                jnp.where(rim == LY - 1, turn(a_ghost[step, roles, 0, place, :], LY - 1), 0.0),
+            )
+
+        jump_up = speeds[above].astype(jnp.float32) * (-1.0 / 256.0)
+        jump_down = speeds[sec].astype(jnp.float32) * (1.0 / 256.0)
+        face_collide(0, UPWARD, LX - 1, jump_up)
+        face_collide(1, DOWNWARD, 0, jump_down)
+
+        def send_ghost(j, carry):
+            role = lax.rem(j + gy, ROLES)
+            target = 2 * ((8 * role) // 5)
+            send(b_send.at[0, role], b_land.at[step, gy], 3, step, above, target)
+            send(b_send.at[1, role], b_land.at[step, gy], 3, step, below, target + 1)
+            return carry
+
+        lax.fori_loop(0, ROLES, send_ghost, 0, unroll=5)
 
         def potentials(z, carry):
             tall = lanes((32, LY))
@@ -315,11 +424,6 @@
             for i in range(19):
                 post[i, z] = fluid[i]
                 post[19 + i, z] = order[i]
-            for side, members, x in ((0, UPWARD, LX - 1), (1, DOWNWARD, 0)):
-                rows = [fluid[i] for i in members] + [order[i] for i in members]
-                rows += [density, phi, vel[0], vel[1], vel[2]]
-                for k, tile in enumerate(rows):
-                    face[side, k, pl.ds(z, 1), :] = tile[x : x + 1, :]
             going_left = jnp.zeros(plane, jnp.float32)
             going_right = jnp.zeros(plane, jnp.float32)
             for k in range(10):
@@ -340,32 +444,6 @@
         b_edge[0] = to_left
         b_edge[1] = to_right
 
-        jump_up = speeds[above].astype(jnp.float32) * (-1.0 / 256.0)
-        jump_down = speeds[sec].astype(jnp.float32) * (1.0 / 256.0)
-        for side, members, jump in ((0, UPWARD, jump_up), (1, DOWNWARD, jump_down)):
-            density, phi, vel_x, vel_y, vel_z = [face[side, 10 + k] for k in range(5)]
-            moved = vel_y + jump
-            change_square = 1.5 * (moved * moved - vel_y * vel_y)
-            for k, i in enumerate(members):
-                vector = VELOCITY[i]
-                before = signed_sum((vel_x, vel_y, vel_z), vector)
-                after = signed_sum((vel_x, moved, vel_z), vector)
-                change = WEIGHTS[i] * (
-                    3.0 * (after - before) + 4.5 * (after * after - before * before) - change_square
-                )
-                for lift, mass in ((0, density), (5, phi)):
-                    value = face[side, k + lift] + mass * change
-                    b_send[side, 2 * (k + lift)] = value[:4]
-                    b_send[side, 2 * (k + lift) + 1] = value[4:]
-
-        def send_ghost(j, carry):
-            role = lax.rem(j + gy, ROLES)
-            target = 2 * ((8 * role) // 5)
-            send(b_send.at[0, role], b_land.at[step, gy], 3, step, above, target)
-            send(b_send.at[1, role], b_land.at[step, gy], 3, step, below, target + 1)
-            return carry
-
-        lax.fori_loop(0, ROLES, send_ghost, 0, unroll=5)
         send(b_edge.at[0], b_near.at[step, 1], 4, step, sec, left)
         send(b_edge.at[1], b_near.at[step, 0], 4, step, sec, right)
 
@@ -387,13 +465,19 @@
                 b_slid.at[gy], b_ghost.at[step, b_slot], recv_sem.at[5, step]
             ).start()
 
-            def send_slid_ghost(j, carry):
-                block = (gy + j) & (N_GY - 1)
+            def send_slid_ghost(k, m):
+                block = far_first(gy, k, m)
                 slide_ghost(block)
                 send(b_slid.at[block], b_ghost.at[step, b_slot], 5, step, sec, block)
+
+            def send_slid_ghosts(k, carry):
+                for m in range(8):
+                    send_slid_ghost(k, m)
                 return carry
 
-            lax.fori_loop(1, N_GY, send_slid_ghost, 0, unroll=7)
+            lax.fori_loop(0, 7, send_slid_ghosts, 0)
+            for m in range(7):
+                send_slid_ghost(7, m)
 
         wait_bytes(b_near.at[step], recv_sem.at[4, step])
         near_left = b_near[step, 0]
@@ -425,6 +509,15 @@
 
         lax.fori_loop(0, NZ, stream, 0)
 
+        incoming = ((0, UPWARD, 0), (1, DOWNWARD, LX - 1))
+
+        @pl.when(step < STEPS - 1)
+        def _():
+            for side, members, x in incoming:
+                for i in members:
+                    state[19 + i, :, x, :] = jnp.zeros((NZ, LY), jnp.float32)
+            order_pass()
+
         wait_bytes(a_land.at[step], send_sem.at[0])
         wait_bytes(a_edge, send_sem.at[1])
         wait_bytes(a_slid.at[pl.ds(0, 15)], send_sem.at[2])
@@ -436,18 +529,22 @@
             wait_bytes(b_slid.at[pl.ds(0, N_GY - 1)], send_sem.at[5])
 
         wait_bytes(b_ghost.at[step], recv_sem.at[5, step])
-        for side, members, x in ((0, UPWARD, 0), (1, DOWNWARD, LX - 1)):
+        for side, members, x in incoming:
+            total = None
             for k in range(10):
                 i = members[k % 5]
-                which = i + (19 if k >= 5 else 0)
-                for z in range(NZ):
-                    source = (z - VELOCITY[i][2]) % NZ
-                    slot = ROLES * side + 2 * k + source // 4
-                    state[which, z, pl.ds(x, 1), :] = b_ghost[step, slot, pl.ds(source % 4, 1), :]
+                rows = b_ghost[step, pl.ds(ROLES * side + 2 * k, 2)].reshape(NZ, LY)
+                if VELOCITY[i][2]:
+                    rows = pltpu.roll(rows, VELOCITY[i][2] % NZ, 0)
+                state[i + (19 if k >= 5 else 0), :, x, :] = rows
+                if k >= 5:
+                    total = rows if total is None else total + rows
+            cut = pl.ds(0, LY)
+            field[:, 8 + x, cut] = field[:, 8 + x, cut] + total
 
         @pl.when(step < STEPS - 1)
         def _():
-            order_pass()
+            pack_order()
 
         return carry
 
@@ -460,29 +557,50 @@
     store_order.wait()
 
 
+def copy_out(fluid_in, order_in, fluid_out, order_out, held, in_sem, out_sem):
+    parts = [(0, 5), (5, 5), (10, 5), (15, 4)]
+    loads, stores = [], []
+    for start, size in parts:
+        for half, src, dst in ((0, fluid_in, fluid_out), (19, order_in, order_out)):
+            k = len(loads)
+            here = held.at[pl.ds(half + start, size)]
+            cut = pl.ds(start, size)
+            loads.append(pltpu.make_async_copy(src.at[cut], here, in_sem.at[k]))
+            stores.append(pltpu.make_async_copy(here, dst.at[cut], out_sem.at[k]))
+    for load in loads:
+        load.start()
+    for load, store in zip(loads, stores):
+        load.wait()
+        store.start()
+    for store in stores:
+        store.wait()
+
+
 def per_device(fluid_dist, order_dist, plane_offset, plane_speed):
     shape = jax.ShapeDtypeStruct((19, NZ, LX, LY), jnp.float32)
 
     def scratch(*dims):
         return pltpu.VMEM(dims, jnp.float32)
 
-    return pl.pallas_call(
+    hbm = pl.BlockSpec(memory_space=pl.ANY)
+    results = pl.pallas_call(
         kernel,
         out_shape=(shape, shape),
         in_specs=[
             pl.BlockSpec(memory_space=pl.ANY),
             pl.BlockSpec(memory_space=pl.ANY),
-            pl.BlockSpec(memory_space=pltpu.SMEM),
-            pl.BlockSpec(memory_space=pltpu.SMEM),
+            pl.BlockSpec(memory_space=pl.ANY),
+            pl.BlockSpec(memory_space=pl.ANY),
         ],
         out_specs=(pl.BlockSpec(memory_space=pl.ANY), pl.BlockSpec(memory_space=pl.ANY)),
         scratch_shapes=[
+            pltpu.SMEM((STEPS, N_SEC), jnp.int32),
+            pltpu.SMEM((N_SEC,), jnp.int32),
             scratch(38, NZ, LX, LY),
             scratch(38, NZ, LX, LY),
             scratch(NZ, 32, 2 * LY),
             scratch(NZ, 32, 2 * LY),
             scratch(4, NZ, LX, LY),
-            scratch(2, 15, NZ, LY),
             scratch(NZ, 2, LY),
             scratch(NZ, 2, LY),
             scratch(2, LX, LY),
@@ -496,15 +614,27 @@
             scratch(N_GY, 4, LY),
             scratch(STEPS, 2 * ROLES, 4, LY),
             scratch(STEPS, 2, LX, LY),
-            pltpu.SemaphoreType.DMA((2,)),
+            pltpu.SemaphoreType.DMA((4,)),
             pltpu.SemaphoreType.DMA((2,)),
             pltpu.SemaphoreType.DMA((6,)),
             pltpu.SemaphoreType.DMA((6, STEPS)),
         ],
         compiler_params=pltpu.CompilerParams(
-            collective_id=0, has_side_effects=True, vmem_limit_bytes=40 * 1024 * 1024
+            collective_id=0, has_side_effects=True, vmem_limit_bytes=60 * 1024 * 1024
         ),
     )(fluid_dist, order_dist, plane_offset, plane_speed)
+    return pl.pallas_call(
+        copy_out,
+        out_shape=(shape, shape),
+        in_specs=[hbm, hbm],
+        out_specs=(hbm, hbm),
+        scratch_shapes=[
+            scratch(38, NZ, LX, LY),
+            pltpu.SemaphoreType.DMA((8,)),
+            pltpu.SemaphoreType.DMA((8,)),
+        ],
+        compiler_params=pltpu.CompilerParams(vmem_limit_bytes=60 * 1024 * 1024),
+    )(*results)
 
 
 def solution(mesh):

time: 87 us -> 71.8 us (0.83)
  Pallas kernels: 80.2 us -> 71.1 us
  local copies, waits for them, and re-layouts: 5.98 us -> 0 us
    pallas_call x1, Pallas kernels: 80.2 us -> 68.5 us  [per_device(): pl.pallas_call(kernel, out_shape=(shape, shape), in_specs=[pl.BlockSpec(m...]
    unnamed x10 -> x0, local copies, waits for them, and re-layouts: 5.98 us -> none
    pallas_call x0 -> x1, Pallas kernels: none -> 2.55 us  [per_device(): pl.pallas_call(copy_out, out_shape=(shape, shape), in_specs=[hbm, hbm], o...]
where the time goes in v2:
time: 71.8 us; the launch traced here: 71.7 us
  Pallas kernels  71.1 us (99%)
    pallas_call x1, Pallas kernels, per_device(): pl.pallas_call(kernel, out_shape=(shape, shape), in_specs=[pl.BlockSpec(m...  68.5 us
    pallas_call x1, Pallas kernels, per_device(): pl.pallas_call(copy_out, out_shape=(shape, shape), in_specs=[hbm, hbm], o...  2.55 us

profile of v2, /device:TPU:1, one launch (start us, length us, event | category | flops | bytes accessed | tf_op | source)
XLA Modules:
  0.0 71.7 jit_solution(17925654624911495701)
XLA Ops:
  0.6 68.5 %shard_map.59 = (f32[19,8,16,128]{3,2,1,0:T(8,128)}, f32[19,8,16,128]{3,2,1,0:T(8,128)}) custom-call(f32[19,8,16,128]{3,2,1,0:T(8,128)} %fluid_in.1, f32[19,8,16,128]{3,2,1,0:T(8,128)} %order_in.1, s32[2,4]{1,0:T(2,128)} %offsets_in.1, s32[4]{0:T(128)} %speeds_in.1), custom_call_target="tpu_custom_call" | custom-call | tf_op jit(solution)/shard_map/pallas_call | solution.py:586
  69.2 2.5 %shard_map.60 = (f32[19,8,16,128]{3,2,1,0:T(8,128)}, f32[19,8,16,128]{3,2,1,0:T(8,128)}) custom-call(f32[19,8,16,128]{3,2,1,0:T(8,128)} %get-tuple-element.4.fluid_in, f32[19,8,16,128]{3,2,1,0:T(8,128)} %get-tuple-element.5.order_in), custom_call_target="tpu_custom_call" | custom-call | tf_op jit(solution)/shard_map/pallas_call | solution.py:626

commit v3 on v2

v3 whole, which is shorter than its diff:
```python
import jax
import jax.numpy as jnp
from jax import lax
from jax.experimental import pallas as pl
from jax.experimental.pallas import tpu as pltpu
from jax.sharding import PartitionSpec as P

STEPS = 2
VELOCITY = (
    (0, 0, 0),
    (1, 0, 0),
    (-1, 0, 0),
    (0, 1, 0),
    (0, -1, 0),
    (0, 0, 1),
    (0, 0, -1),
    (1, 1, 0),
    (-1, -1, 0),
    (1, -1, 0),
    (-1, 1, 0),
    (1, 0, 1),
    (-1, 0, -1),
    (1, 0, -1),
    (-1, 0, 1),
    (0, 1, 1),
    (0, -1, -1),
    (0, 1, -1),
    (0, -1, 1),
)
WEIGHTS = (1.0 / 3.0,) + (1.0 / 18.0,) * 6 + (1.0 / 36.0,) * 12
UPWARD = (1, 7, 9, 11, 13)
DOWNWARD = (2, 8, 10, 12, 14)
Y_PLUS = (3, 7, 10, 15, 17)
Y_MINUS = (4, 8, 9, 16, 18)
COEF_A = -0.0625
COEF_B = 0.0625
KAPPA_GRAD = 0.04
MOBILITY = 1.0
TAU_FLUID = 0.8
TAU_ORDER = 0.9
NZ = 8
LX = 16
LY = 128
N_SEC = 4
N_GY = 64
SPAN = LY * N_GY * 256
ROLES = 20
GHOSTS = 2 * ROLES
MESH = pl.DeviceIdType.MESH
ACROSS = ((1, 2), (1, 1), (1, 3), (0, 2), (1, 0), (0, 1), (0, 3), (0, 0))


def lanes(shape):
    return lax.broadcasted_iota(jnp.int32, shape, len(shape) - 1)


def turn(value, shift):
    return pltpu.roll(value, shift, value.ndim - 1)


def ring_z(gy, k):
    half = (k + 1) >> 1
    return ((gy >> 2) + 4 + jnp.where((k & 1) == 1, -half, half)) & 7


def far_first(gy, k, m):
    across, along = ACROSS[m]
    return (((gy >> 5) ^ across) << 5) + (ring_z(gy, k) << 2) + ((gy + along) & 3)


def signed_sum(terms, signs):
    total = None
    for term, sign in zip(terms, signs):
        if sign == 0:
            continue
        if total is None:
            total = term if sign > 0 else -term
        else:
            total = total + term if sign > 0 else total - term
    return total


def wait_bytes(ref, sem):
    pltpu.make_async_copy(ref, ref, sem).wait()


def slid_block(load, block, offset):
    offset = offset & (LY * N_GY - 1)
    first = block + (offset >> 7)
    inside = offset & (LY - 1)
    here = load(first & (N_GY - 1))
    beyond = load((first + 1) & (N_GY - 1))
    shift = (LY - inside) & (LY - 1)
    return jnp.where(lanes(here.shape) < LY - inside, turn(here, shift), turn(beyond, shift))


def parts_of(units):
    frac = (units & 255).astype(jnp.float32) * (1.0 / 256.0)
    return units >> 8, 1.0 - frac, frac


def slide(load, block, parts, along_y=0):
    whole, keep, frac = parts
    start = whole + along_y
    return keep * slid_block(load, block, start) + frac * slid_block(load, block, start + 1)


def kernel(
    fluid_in, order_in, offsets_in, speeds_in, fluid_out, order_out, ghosts_out,
    offsets, speeds, state, post, field, pot, mom,
    a_up, a_down, a_edge, a_land, a_slid, a_ghost, a_near,
    b_send, b_part, b_own, b_edge, b_land_0, b_land_1, b_back, b_full, b_line, b_turned, b_slid, b_ghost, b_near,
    in_sem, out_sem, send_sem, recv_sem,
):
    b_lands = (b_land_0, b_land_1)
    sec = lax.axis_index("sec")
    gy = lax.axis_index("gy")
    above = (sec + 1) & (N_SEC - 1)
    below = (sec + N_SEC - 1) & (N_SEC - 1)
    left = (gy + N_GY - 1) & (N_GY - 1)
    right = (gy + 1) & (N_GY - 1)
    is_down = gy & 1
    owner = gy >> 1
    a_z = owner & 7
    a_part = owner >> 3
    place = owner & 3
    b_role = 8 * place + (owner >> 2)
    is_owner = b_role < ROLES
    is_phi = place == 3
    phi_z = owner >> 2

    load_order = pltpu.make_async_copy(order_in, state.at[pl.ds(19, 19)], in_sem.at[0])
    load_order.start()
    load_offsets = pltpu.make_async_copy(offsets_in, offsets, in_sem.at[2])
    load_offsets.start()
    load_speeds = pltpu.make_async_copy(speeds_in, speeds, in_sem.at[3])
    load_speeds.start()
    load_fluid = pltpu.make_async_copy(fluid_in, state.at[pl.ds(0, 19)], in_sem.at[1])
    load_fluid.start()

    barrier = pltpu.get_barrier_semaphore()
    source_sec = jnp.where(is_down == 0, below, above)

    def greet(k, carry):
        for m in range(8):
            other = far_first(gy, k, m)
            pl.semaphore_signal(
                barrier, inc=1, device_id=(source_sec, other), device_id_type=MESH
            )
            if m < 7:
                pl.semaphore_signal(barrier, inc=1, device_id=(sec, other), device_id_type=MESH)
        return carry

    def greet_rest(k, carry):
        pl.semaphore_signal(
            barrier, inc=1, device_id=(sec, far_first(gy, k, 7)), device_id_type=MESH
        )
        return carry

    lax.fori_loop(0, 8, greet, 0)
    lax.fori_loop(0, 7, greet_rest, 0)

    plane = (LX, LY)
    lane = lanes(plane)
    field[...] = jnp.zeros_like(field)

    def order_pass():
        def one(z, carry):
            phi = state[19, z]
            for i in range(1, 19):
                phi = phi + state[19 + i, z]
            field[z, pl.ds(8, LX), pl.ds(0, LY)] = phi
            return carry

        lax.fori_loop(0, NZ, one, 0)

    def pack_faces():
        for j in range(2):
            a_up[:, j, :] = field[:, 8 + LX - 2 + j, pl.ds(0, LY)]
            a_down[:, j, :] = field[:, 8 + j, pl.ds(0, LY)]

    def pack_columns():
        to_left = jnp.zeros(plane, jnp.float32)
        to_right = to_left
        for z in range(NZ):
            phi = field[z, pl.ds(8, LX), pl.ds(0, LY)]
            mine = (lane >> 1) == z
            to_left = jnp.where(mine, turn(phi, 2 * z), to_left)
            to_right = jnp.where(mine, turn(phi, 2 * z + 2), to_right)
        a_edge[0] = to_left
        a_edge[1] = to_right

    def next_y(near, far):
        tile = lanes(near.shape)
        return jnp.where(tile == LY - 1, turn(far, LY - 1), turn(near, LY - 1))

    def last_y(near, far):
        tile = lanes(near.shape)
        return jnp.where(tile == 0, turn(far, 1), turn(near, 1))

    def face_potential(x, half):
        cut = pl.ds(half * LY, LY)
        tile = field[:, 8 + x, cut]
        other = field[:, 8 + x, pl.ds((1 - half) * LY, LY)]
        lap = (
            field[:, 9 + x, cut]
            + field[:, 7 + x, cut]
            + next_y(tile, other)
            + last_y(tile, other)
            + pltpu.roll(tile, 1, 0)
            + pltpu.roll(tile, NZ - 1, 0)
            - 6.0 * tile
        )
        return tile * (COEF_A + COEF_B * tile * tile) - KAPPA_GRAD * lap

    left_f = 1.0 - 1.0 / TAU_FLUID
    left_g = 1.0 - 1.0 / TAU_ORDER
    kick = 1.0 - 0.5 / TAU_FLUID
    rim = lanes((NZ, LY))

    def face_layer(x, potential):
        phi = field[:, 8 + x, pl.ds(0, LY)]
        middle = potential(x, 0)
        beyond = potential(x, 1)
        half = -0.5 * phi
        force = (
            half * (potential(x + 1, 0) - potential(x - 1, 0)),
            half * (next_y(middle, beyond) - last_y(middle, beyond)),
            half * (pltpu.roll(middle, NZ - 1, 0) - pltpu.roll(middle, 1, 0)),
        )
        density = mom[0, :, x, :]
        inverse = 1.0 / density
        vel = tuple((mom[1 + k, :, x, :] + 0.5 * force[k]) * inverse for k in range(3))
        square = vel[0] * vel[0] + vel[1] * vel[1] + vel[2] * vel[2]
        square_phi = phi * (1.0 / TAU_ORDER)
        base_phi = (3.0 * MOBILITY / TAU_ORDER) * middle - 1.5 * square_phi * square
        return phi, middle, force, density, vel, square, square_phi, base_phi

    def face_order(x, i, layer):
        _, middle, _, _, vel, square, square_phi, base_phi = layer
        kept = left_g * state[19 + i, :, x, :]
        if i == 0:
            return kept + (
                square_phi * (1.0 - 0.5 * square) - (2.0 * MOBILITY / TAU_ORDER) * middle
            )
        along = signed_sum(vel, VELOCITY[i])
        carried = square_phi * along
        return kept + WEIGHTS[i] * (base_phi + 4.5 * carried * along + 3.0 * carried)

    def streamed_sum(terms):
        groups = {0: None, 1: None, -1: None}
        for i, tile in terms:
            _, shift_y, shift_z = VELOCITY[i]
            if shift_z:
                tile = pltpu.roll(tile, shift_z % NZ, 0)
            held = groups[shift_y]
            groups[shift_y] = tile if held is None else held + tile
        total = (
            groups[0]
            + jnp.where(rim == 0, 0.0, turn(groups[1], 1))
            + jnp.where(rim == LY - 1, 0.0, turn(groups[-1], LY - 1))
        )
        return total, groups[1], groups[-1]

    def crossing(sums):
        result = jnp.zeros((NZ, LY), jnp.float32)
        for j, (_, forward, back) in enumerate(sums):
            result = jnp.where(rim == j, turn(forward, 1 + j), result)
            result = jnp.where(rim == LY - 1 - j, turn(back, LY - 1 - j), result)
        return result

    def face_collide(side, jump):
        members, others, x, inward = ((UPWARD, DOWNWARD, LX - 1, -1), (DOWNWARD, UPWARD, 0, 1))[side]
        made = {}

        def potential(layer_x, half):
            if (layer_x, half) not in made:
                made[layer_x, half] = face_potential(layer_x, half)
            return made[layer_x, half]

        layer = face_layer(x, potential)
        phi, middle, force, density, vel, square, square_phi, base_phi = layer
        drift = vel[0] * force[0] + vel[1] * force[1] + vel[2] * force[2]
        scaled = density * (1.0 / TAU_FLUID)
        base = scaled * (1.0 - 1.5 * square) - (3.0 * kick) * drift
        moved = vel[1] + jump
        change_square = 1.5 * (moved * moved - vel[1] * vel[1])
        leaving = []
        for k, i in enumerate(members):
            vector = VELOCITY[i]
            weight = WEIGHTS[i]
            along = signed_sum(vel, vector)
            pushed = signed_sum(force, vector)
            after = signed_sum((vel[0], moved, vel[2]), vector)
            change = weight * (
                3.0 * (after - along) + 4.5 * (after * after - along * along) - change_square
            )
            fluid = left_f * state[i, :, x, :] + weight * (
                base
                + along * (4.5 * scaled * along + (9.0 * kick) * pushed)
                + (3.0 * scaled * along + (3.0 * kick) * pushed)
            )
            order = face_order(x, i, layer) + phi * change
            leaving.append((i, order))
            for lift, value in ((0, fluid + density * change), (5, order)):
                b_send[side, 2 * (k + lift)] = value[:4]
                b_send[side, 2 * (k + lift) + 1] = value[4:]

        def make_parts():
            second = x + inward
            third = second + inward
            layers = {x: layer}
            for layer_x in (second, third):
                layers[layer_x] = face_layer(layer_x, potential)
            still = [i for i in range(19) if VELOCITY[i][0] == 0]

            def terms(layer_x, rows):
                return [(i, face_order(layer_x, i, layers[layer_x])) for i in rows]

            sums = [
                streamed_sum(terms(x, still) + terms(second, members)),
                streamed_sum(terms(second, still) + terms(third, members) + terms(x, others)),
                streamed_sum(leaving),
            ]
            for j in range(3):
                b_part[side, :, j, :] = sums[j][0]
            b_part[side, :, 3, :] = crossing(sums)
            b_own[side, :, 0, :] = sums[2][0]
            b_own[side, :, 1, :] = crossing(sums[2:])

        return make_parts

    def send(src, dst, which, slot, to_sec, to_gy):
        pltpu.make_async_remote_copy(
            src_ref=src,
            dst_ref=dst,
            send_sem=send_sem.at[which],
            recv_sem=recv_sem.at[which, slot],
            device_id=(to_sec, to_gy),
            device_id_type=MESH,
        ).start()

    load_order.wait()
    order_pass()
    pack_faces()
    pack_columns()
    load_offsets.wait()
    load_speeds.wait()
    pl.semaphore_wait(barrier, 2 * N_GY - 1)

    own = pl.ds(0, LY)
    halo = pl.ds(LY, LY)
    incoming = ((0, UPWARD, 0), (1, DOWNWARD, LX - 1))
    outside = ((0, -1, -2), (1, LX, LX + 1))

    def units_of(step):
        return jnp.where(
            is_down == 0, offsets[step, sec], (SPAN - offsets[step, above]) & (SPAN - 1)
        )

    def send_columns(step):
        send(a_edge.at[0], a_near.at[step, 1], 1, step, sec, left)
        send(a_edge.at[1], a_near.at[step, 0], 1, step, sec, right)

    def put_columns(step):
        wait_bytes(a_near.at[step], recv_sem.at[1, step])
        from_left = a_near[step, 0]
        from_right = a_near[step, 1]

        def one(z, carry):
            field[z, pl.ds(8, LX), halo] = jnp.where(
                lane < 2,
                turn(from_right, (LY - 2 * z) & (LY - 1)),
                jnp.where(lane >= LY - 2, turn(from_left, (LY - 2 - 2 * z) & (LY - 1)), 0.0),
            )
            return carry

        lax.fori_loop(0, NZ, one, 0)

    def moments():
        def one(z, carry):
            tiles = [state[i, z] for i in range(19)]
            mom[0, z] = signed_sum(tiles, (1,) * 19)
            for axis in range(3):
                mom[1 + axis, z] = signed_sum(tiles, [vector[axis] for vector in VELOCITY])
            return carry

        lax.fori_loop(0, NZ, one, 0)

    def exchange_order():
        def send_order(k, carry):
            for across, along in ((1, 1), (1, 0), (0, 1), (0, 0)):
                target = (
                    (((gy >> 5) ^ across) << 5) + (ring_z(gy, k) << 2) + ((gy & 2) ^ (2 * along))
                )
                z = (target >> 1) & 7
                send(a_up.at[z], a_land.at[gy], 0, 0, above, target)
                send(a_down.at[z], a_land.at[gy], 0, 0, below, target + 1)
            return carry

        lax.fori_loop(0, 8, send_order, 0, unroll=2)
        send_columns(0)
        load_fluid.wait()
        moments()
        parts = parts_of(units_of(0))
        whole, keep, frac = parts
        wait_bytes(a_land, recv_sem.at[0, 0])

        def slide_order(block):
            values = [
                slid_block(lambda i: a_land[i], block, whole + shift) for shift in (-1, 0, 1, 2)
            ]
            for k in range(3):
                a_slid[block & 15, k] = keep * values[k] + frac * values[k + 1]

        a_role = 8 * is_down + a_z
        slide_order(gy)
        pltpu.make_async_copy(
            a_slid.at[gy & 15], a_ghost.at[a_role], recv_sem.at[2, 0]
        ).start()

        def send_slid_order(j, carry):
            block = gy ^ (16 - j)
            slide_order(block)
            send(a_slid.at[block & 15], a_ghost.at[a_role], 2, 0, sec, block)
            return carry

        lax.fori_loop(1, 16, send_slid_order, 0, unroll=5)
        put_columns(0)
        wait_bytes(a_ghost, recv_sem.at[2, 0])
        for side, near_x, far_x in outside:
            roles = pl.ds(8 * side, 8)
            first = 1 - side
            field[:, 8 + near_x, own] = a_ghost[roles, 1, first, :]
            field[:, 8 + far_x, own] = a_ghost[roles, 1, 1 - first, :]
            field[:, 8 + near_x, halo] = jnp.where(
                rim == 0,
                turn(a_ghost[roles, 2, first, :], 1),
                jnp.where(rim == LY - 1, turn(a_ghost[roles, 0, first, :], LY - 1), 0.0),
            )
        wait_bytes(a_land, send_sem.at[0])
        wait_bytes(a_slid.at[pl.ds(0, 15)], send_sem.at[2])

    def potentials(z, carry):
        tall = lanes((32, LY))
        tiles = [field[z, :, own], field[z, :, halo]]
        ahead = [turn(tile, LY - 1) for tile in tiles]
        behind = [turn(tile, 1) for tile in tiles]
        for k in range(2):
            tile = tiles[k]
            cut = pl.ds(k * LY, LY)
            lap = (
                pltpu.roll(tile, 1, 0)
                + pltpu.roll(tile, 31, 0)
                + jnp.where(tall == LY - 1, ahead[1 - k], ahead[k])
                + jnp.where(tall == 0, behind[1 - k], behind[k])
                + field[(z + 1) & 7, :, cut]
                + field[(z + 7) & 7, :, cut]
                - 6.0 * tile
            )
            pot[z, :, cut] = tile * (COEF_A + COEF_B * tile * tile) - KAPPA_GRAD * lap
        return carry

    def collide(z, carry):
        to_left, to_right = carry
        rows = pl.ds(8, LX)
        inner = pot[z, rows, own]
        beyond = pot[z, rows, halo]
        phi = field[z, rows, own]
        half = -0.5 * phi
        force = (
            half * (pot[z, pl.ds(9, LX), own] - pot[z, pl.ds(7, LX), own]),
            half * (next_y(inner, beyond) - last_y(inner, beyond)),
            half * (pot[(z + 1) & 7, rows, own] - pot[(z + 7) & 7, rows, own]),
        )
        density = mom[0, z]
        inverse = 1.0 / density
        vel = tuple((mom[1 + k, z] + 0.5 * force[k]) * inverse for k in range(3))
        square = vel[0] * vel[0] + vel[1] * vel[1] + vel[2] * vel[2]
        drift = vel[0] * force[0] + vel[1] * force[1] + vel[2] * force[2]
        scaled = density * (1.0 / TAU_FLUID)
        base = scaled * (1.0 - 1.5 * square) - (3.0 * kick) * drift
        square_phi = phi * (1.0 / TAU_ORDER)
        base_phi = (3.0 * MOBILITY / TAU_ORDER) * inner - 1.5 * square_phi * square
        fluid = [None] * 19
        order = [None] * 19
        fluid[0] = left_f * state[0, z] + WEIGHTS[0] * base
        order[0] = left_g * state[19, z] + (
            square_phi * (1.0 - 0.5 * square) - (2.0 * MOBILITY / TAU_ORDER) * inner
        )
        for i in range(1, 19, 2):
            vector = VELOCITY[i]
            along = signed_sum(vel, vector)
            pushed = signed_sum(force, vector)
            weight = WEIGHTS[i]
            even = weight * (base + along * (4.5 * scaled * along + (9.0 * kick) * pushed))
            odd = weight * (3.0 * scaled * along + (3.0 * kick) * pushed)
            fluid[i] = left_f * state[i, z] + (even + odd)
            fluid[i + 1] = left_f * state[i + 1, z] + (even - odd)
            carried = square_phi * along
            even = weight * (base_phi + 4.5 * carried * along)
            odd = (3.0 * weight) * carried
            order[i] = left_g * state[19 + i, z] + (even + odd)
            order[i + 1] = left_g * state[20 + i, z] + (even - odd)
        for i in range(19):
            post[i, z] = fluid[i]
            post[19 + i, z] = order[i]
        going_left = jnp.zeros(plane, jnp.float32)
        going_right = jnp.zeros(plane, jnp.float32)
        for k in range(10):
            part = fluid if k < 5 else order
            going_right = jnp.where(
                lane == 8 * k, turn(part[Y_PLUS[k % 5]], 8 * k + 1), going_right
            )
            going_left = jnp.where(lane == 8 * k, turn(part[Y_MINUS[k % 5]], 8 * k), going_left)
        mine = (lane & 7) == z
        to_left = jnp.where(mine, turn(going_left, z), to_left)
        to_right = jnp.where(mine, turn(going_right, z), to_right)
        return to_left, to_right

    def pass_ghosts(step):
        member = lax.rem(b_role >> 1, 5)
        along_y = jnp.where(member == 1, -1, jnp.where(member == 2, 1, 0)) * (1 - 2 * is_down)
        parts = parts_of(units_of(step))
        slot = ROLES * is_down + b_role
        wait_bytes(b_lands[step], recv_sem.at[3, step])

        def make(block):
            b_slid[block] = slide(lambda i: b_lands[step][i], block, parts, along_y)

        pass_on(step, slot, make)

    def pass_on(step, slot, make):
        make(gy)
        pltpu.make_async_copy(
            b_slid.at[gy], b_ghost.at[step, slot], recv_sem.at[5, step]
        ).start()

        def one(k, m):
            block = far_first(gy, k, m)
            make(block)
            send(b_slid.at[block], b_ghost.at[step, slot], 5, step, sec, block)

        def several(k, carry):
            for m in range(8):
                one(k, m)
            return carry

        lax.fori_loop(0, 7, several, 0)
        for m in range(7):
            one(7, m)

    def pass_order(step):
        units = units_of(step)
        parts = parts_of(units)
        parts_back = parts_of((SPAN - units) & (SPAN - 1))
        parts_next = parts_of(units_of(step + 1))
        wait_bytes(b_lands[step], recv_sem.at[6, step])
        wait_bytes(b_back, recv_sem.at[7, step])
        four = lanes((4, LY))
        which = lax.broadcasted_iota(jnp.int32, (4, LY), 0)
        line = lanes((1, LY))

        def complete(block, carry):
            before = (block + N_GY - 1) & (N_GY - 1)
            after = (block + 1) & (N_GY - 1)
            forward = jnp.broadcast_to(b_lands[step][before, pl.ds(3, 1), :], (4, LY))
            back = jnp.broadcast_to(b_lands[step][after, pl.ds(3, 1), :], (4, LY))
            for j in (1, 2):
                forward = jnp.where(which == j, turn(forward, LY - j), forward)
                back = jnp.where(which == j, turn(back, j), back)
            b_full[block] = (
                b_lands[step][block]
                + jnp.where(four == 0, forward, 0.0)
                + jnp.where(four == LY - 1, back, 0.0)
            )
            b_line[block] = (
                b_back[block, pl.ds(0, 1), :]
                + jnp.where(line == 0, b_back[before, pl.ds(1, 1), :], 0.0)
                + jnp.where(line == LY - 1, b_back[after, pl.ds(1, 1), :], 0.0)
            )
            return carry

        lax.fori_loop(0, N_GY, complete, 0, unroll=4)

        def add_own(block, carry):
            b_full[block, pl.ds(0, 1), :] = b_full[block, pl.ds(0, 1), :] + slide(
                lambda i: b_line[i], block, parts_back
            )
            return carry

        lax.fori_loop(0, N_GY, add_own, 0, unroll=4)

        def turn_all(block, carry):
            ahead = slide(lambda i: b_full[i], block, parts_next)
            now = slide(lambda i: b_full[i], block, parts)
            b_turned[block] = jnp.where(which == 2, now, ahead)
            return carry

        lax.fori_loop(0, N_GY, turn_all, 0, unroll=4)

        def make(block):
            before = (block + N_GY - 1) & (N_GY - 1)
            after = (block + 1) & (N_GY - 1)
            b_slid[block, pl.ds(0, 2), :] = b_turned[block, pl.ds(0, 2), :]
            b_slid[block, pl.ds(2, 1), :] = jnp.where(
                line == 0,
                b_turned[after, pl.ds(0, 1), :],
                jnp.where(line == LY - 1, b_turned[before, pl.ds(0, 1), :], 0.0),
            )
            b_slid[block, pl.ds(3, 1), :] = jnp.where(
                line < 2,
                b_turned[after, pl.ds(2, 1), :],
                jnp.where(line >= LY - 2, b_turned[before, pl.ds(2, 1), :], 0.0),
            )

        pass_on(step, GHOSTS + 8 * is_down + phi_z, make)

    def stream(z, carry):
        near_left, near_right = carry
        columns = {}
        for shift_z in (-1, 0, 1):
            source = (z - shift_z) & 7
            back = (LY - source) & (LY - 1)
            columns[1, shift_z] = turn(near_left, back)
            columns[-1, shift_z] = turn(near_right, back)
        for which in range(38):
            i = which % 19
            shift_x, shift_y, shift_z = VELOCITY[i]
            tile = post[which, (z - shift_z) & 7]
            if shift_y == 1:
                k = Y_PLUS.index(i) + (5 if which >= 19 else 0)
                outer = turn(columns[1, shift_z], (LY - 8 * k) % LY)
                tile = jnp.where(lane == 0, outer, turn(tile, 1))
            elif shift_y == -1:
                k = Y_MINUS.index(i) + (5 if which >= 19 else 0)
                outer = turn(columns[-1, shift_z], (LY - 1 - 8 * k) % LY)
                tile = jnp.where(lane == LY - 1, outer, turn(tile, LY - 1))
            if shift_x:
                tile = pltpu.roll(tile, shift_x % LX, 0)
            state[which, z] = tile
        return carry

    def take_ghosts(step):
        for side, members, x in incoming:
            order_sum = None
            tiles = []
            for k in range(10):
                i = members[k % 5]
                rows = b_ghost[step, pl.ds(ROLES * side + 2 * k, 2)].reshape(NZ, LY)
                if VELOCITY[i][2]:
                    rows = pltpu.roll(rows, VELOCITY[i][2] % NZ, 0)
                state[i + (19 if k >= 5 else 0), :, x, :] = rows
                if k >= 5:
                    order_sum = rows if order_sum is None else order_sum + rows
                else:
                    tiles.append(rows)
            field[:, 8 + x, own] = field[:, 8 + x, own] + order_sum
            mom[0, :, x, :] = mom[0, :, x, :] + signed_sum(tiles, (1,) * 5)
            for axis in range(3):
                mom[1 + axis, :, x, :] = mom[1 + axis, :, x, :] + signed_sum(
                    tiles, [VELOCITY[i][axis] for i in members]
                )
        for side, near_x, far_x in outside:
            roles = pl.ds(GHOSTS + 8 * side, 8)
            x = 0 if side == 0 else LX - 1
            field[:, 8 + near_x, own] = b_ghost[step, roles, 0, :]
            field[:, 8 + far_x, own] = b_ghost[step, roles, 1, :]
            field[:, 8 + near_x, halo] = b_ghost[step, roles, 2, :]
            field[:, 8 + x, halo] = field[:, 8 + x, halo] + b_ghost[step, roles, 3, :]

    def send_ghosts(step):
        def one(j, carry):
            role = lax.rem(j + gy, ROLES)
            target = 2 * (4 * (role & 7) + (role >> 3))
            send(b_send.at[0, role], b_lands[step].at[gy], 3, step, above, target)
            send(b_send.at[1, role], b_lands[step].at[gy], 3, step, below, target + 1)
            return carry

        lax.fori_loop(0, ROLES, one, 0, unroll=5)

    def send_parts(step):
        def one(j, carry):
            z = (j + (gy >> 3)) & 7
            target = 8 * z + 6
            send(b_part.at[0, z], b_lands[step].at[gy], 6, step, above, target)
            send(b_part.at[1, z], b_lands[step].at[gy], 6, step, below, target + 1)
            for side in (0, 1):
                to = target + 1 - side

                @pl.when(to != gy)
                def _():
                    send(b_own.at[side, z], b_back.at[gy], 7, step, sec, to)

            return carry

        lax.fori_loop(0, 8, one, 0)

        @pl.when(is_phi)
        def _():
            pltpu.make_async_copy(
                b_own.at[1 - is_down, phi_z], b_back.at[gy], recv_sem.at[7, step]
            ).start()

    exchange_order()
    for step in range(STEPS):
        last = step == STEPS - 1
        jump_up = speeds[above].astype(jnp.float32) * (-1.0 / 256.0)
        jump_down = speeds[sec].astype(jnp.float32) * (1.0 / 256.0)
        make_parts = [face_collide(0, jump_up), face_collide(1, jump_down)]
        send_ghosts(step)
        if not last:
            for make in make_parts:
                make()
            send_parts(step)

        lax.fori_loop(0, NZ, potentials, 0)
        zero = jnp.zeros(plane, jnp.float32)
        to_left, to_right = lax.fori_loop(0, NZ, collide, (zero, zero))
        b_edge[0] = to_left
        b_edge[1] = to_right
        send(b_edge.at[0], b_near.at[step, 1], 4, step, sec, left)
        send(b_edge.at[1], b_near.at[step, 0], 4, step, sec, right)

        if step > 0:
            @pl.when(jnp.logical_or(is_owner, is_phi))
            def _():
                wait_bytes(b_slid.at[pl.ds(0, N_GY - 1)], send_sem.at[5])

        @pl.when(is_owner)
        def _():
            pass_ghosts(step)

        if not last:

            @pl.when(is_phi)
            def _():
                pass_order(step)

        wait_bytes(b_near.at[step], recv_sem.at[4, step])
        lax.fori_loop(0, NZ, stream, (b_near[step, 0], b_near[step, 1]))
        wait_bytes(a_edge, send_sem.at[1])
        if last:
            store_fluid = pltpu.make_async_copy(state.at[pl.ds(0, 19)], fluid_out, out_sem.at[0])
            store_order = pltpu.make_async_copy(state.at[pl.ds(19, 19)], order_out, out_sem.at[1])
            store_fluid.start()
            store_order.start()
        else:
            for side, members, x in incoming:
                for i in members:
                    state[i, :, x, :] = jnp.zeros((NZ, LY), jnp.float32)
                    state[19 + i, :, x, :] = jnp.zeros((NZ, LY), jnp.float32)
            order_pass()
            pack_columns()
            send_columns(step + 1)
            moments()
            put_columns(step + 1)

        wait_bytes(b_send, send_sem.at[3])
        wait_bytes(b_edge, send_sem.at[4])
        if last:
            wait_bytes(b_ghost.at[step, pl.ds(0, GHOSTS)], recv_sem.at[5, step])
            store_ghosts = pltpu.make_async_copy(
                b_ghost.at[step, pl.ds(0, GHOSTS)], ghosts_out, out_sem.at[2]
            )
            store_ghosts.start()

            @pl.when(is_owner)
            def _():
                wait_bytes(b_slid.at[pl.ds(0, N_GY - 1)], send_sem.at[5])

            store_fluid.wait()
            store_order.wait()
            store_ghosts.wait()
        else:
            wait_bytes(b_part, send_sem.at[6])
            wait_bytes(b_ghost.at[step], recv_sem.at[5, step])
            take_ghosts(step)

            @pl.when(is_phi)
            def _():
                wait_bytes(b_own.at[:, pl.ds(0, 7)], send_sem.at[7])
                wait_bytes(b_own.at[0, 0], send_sem.at[7])

            @pl.when(jnp.logical_not(is_phi))
            def _():
                wait_bytes(b_own, send_sem.at[7])


def finish(
    fluid_in, order_in, ghosts_in, fluid_out, order_out, held, ghosts, in_sem, out_sem, ghost_sem
):
    load_ghosts = pltpu.make_async_copy(ghosts_in, ghosts, ghost_sem)
    load_ghosts.start()
    loads, stores, firsts = [], [], []
    for start, size in ((0, 5), (5, 5), (10, 5), (15, 4)):
        for half, src, dst in ((0, fluid_in, fluid_out), (19, order_in, order_out)):
            k = len(loads)
            here = held.at[pl.ds(half + start, size)]
            cut = pl.ds(start, size)
            loads.append(pltpu.make_async_copy(src.at[cut], here, in_sem.at[k]))
            stores.append(pltpu.make_async_copy(here, dst.at[cut], out_sem.at[k]))
            firsts.append((half + start, size))
    for load in loads:
        load.start()
    load_ghosts.wait()
    for load, store, (first, size) in zip(loads, stores, firsts):
        load.wait()
        for side, members, x in ((0, UPWARD, 0), (1, DOWNWARD, LX - 1)):
            for k in range(10):
                i = members[k % 5]
                which = i + (19 if k >= 5 else 0)
                if first <= which < first + size:
                    rows = ghosts[pl.ds(ROLES * side + 2 * k, 2)].reshape(NZ, LY)
                    if VELOCITY[i][2]:
                        rows = pltpu.roll(rows, VELOCITY[i][2] % NZ, 0)
                    held[which, :, x, :] = rows
        store.start()
    for store in stores:
        store.wait()


def per_device(fluid_dist, order_dist, plane_offset, plane_speed):
    shape = jax.ShapeDtypeStruct((19, NZ, LX, LY), jnp.float32)
    ghosts = jax.ShapeDtypeStruct((GHOSTS, 4, LY), jnp.float32)
    hbm = pl.BlockSpec(memory_space=pl.ANY)
    dma = pltpu.SemaphoreType.DMA

    def scratch(*dims):
        return pltpu.VMEM(dims, jnp.float32)

    results = pl.pallas_call(
        kernel,
        out_shape=(shape, shape, ghosts),
        in_specs=[hbm] * 4,
        out_specs=(hbm, hbm, hbm),
        scratch_shapes=[
            pltpu.SMEM((STEPS, N_SEC), jnp.int32),
            pltpu.SMEM((N_SEC,), jnp.int32),
            scratch(38, NZ, LX, LY),
            scratch(38, NZ, LX, LY),
            scratch(NZ, 32, 2 * LY),
            scratch(NZ, 32, 2 * LY),
            scratch(4, NZ, LX, LY),
            scratch(NZ, 2, LY),
            scratch(NZ, 2, LY),
            scratch(2, LX, LY),
            scratch(N_GY, 2, LY),
            scratch(16, 3, 2, LY),
            scratch(16, 3, 2, LY),
            scratch(STEPS, 2, LX, LY),
            scratch(2, ROLES, 4, LY),
            scratch(2, NZ, 4, LY),
            scratch(2, NZ, 2, LY),
            scratch(2, LX, LY),
            scratch(N_GY, 4, LY),
            scratch(N_GY, 4, LY),
            scratch(N_GY, 2, LY),
            scratch(N_GY, 4, LY),
            scratch(N_GY, 1, LY),
            scratch(N_GY, 4, LY),
            scratch(N_GY, 4, LY),
            scratch(STEPS, GHOSTS + 16, 4, LY),
            scratch(STEPS, 2, LX, LY),
            dma((4,)),
            dma((3,)),
            dma((8,)),
            dma((8, STEPS)),
        ],
        compiler_params=pltpu.CompilerParams(
            collective_id=0, has_side_effects=True, vmem_limit_bytes=60 * 1024 * 1024
        ),
    )(fluid_dist, order_dist, plane_offset, plane_speed)
    return pl.pallas_call(
        finish,
        out_shape=(shape, shape),
        in_specs=[hbm] * 3,
        out_specs=(hbm, hbm),
        scratch_shapes=[
            scratch(38, NZ, LX, LY),
            scratch(GHOSTS, 4, LY),
            dma((8,)),
            dma((8,)),
            dma,
        ],
        compiler_params=pltpu.CompilerParams(vmem_limit_bytes=60 * 1024 * 1024),
    )(*results)


def solution(mesh):
    split = P(None, None, "sec", "gy")
    return jax.shard_map(
        per_device,
        mesh=mesh,
        in_specs=(split, split, P(), P()),
        out_specs=(split, split),
        check_vma=False,
    )
```

time: 71.8 us -> 66.6 us (0.928)
  Pallas kernels: 71.1 us -> 65.8 us
    pallas_call x2, Pallas kernels: 71.1 us -> 65.8 us  [the longest x1 62.7 us: per_device(): pl.pallas_call(kernel, out_shape=(shape, shape, ghosts), in_specs=[hbm] *...]
where the time goes in v3:
time: 66.6 us; the launch traced here: 66.5 us
  Pallas kernels  65.8 us (99%)
    pallas_call x1, Pallas kernels, per_device(): pl.pallas_call(kernel, out_shape=(shape, shape, ghosts), in_specs=[hbm] *...  62.7 us
    pallas_call x1, Pallas kernels, per_device(): pl.pallas_call(finish, out_shape=(shape, shape), in_specs=[hbm] * 3, out_...  3.15 us

profile of v3, /device:TPU:1, one launch (start us, length us, event | category | flops | bytes accessed | tf_op | source)
XLA Modules:
  0.0 66.5 jit_solution(2103242104813119702)
XLA Ops:
  0.6 62.7 %shard_map.59 = (f32[19,8,16,128]{3,2,1,0:T(8,128)}, f32[19,8,16,128]{3,2,1,0:T(8,128)}, f32[40,4,128]{2,1,0:T(4,128)}) custom-call(f32[19,8,16,128]{3,2,1,0:T(8,128)} %fluid_in.1, f32[19,8,16,128]{3,2,1,0:T(8,128)} %order_in.1, s32[2,4]{1,0:T(2,128)} %offsets_in.1, s32[4]{0:T(128)} %speeds_in.1), custom_call_target="tpu_custom_call" | custom-call | tf_op jit(solution)/shard_map/pallas_call | solution.py:832
  63.3 3.1 %shard_map.60 = (f32[19,8,16,128]{3,2,1,0:T(8,128)}, f32[19,8,16,128]{3,2,1,0:T(8,128)}) custom-call(f32[19,8,16,128]{3,2,1,0:T(8,128)} %get-tuple-element.5.fluid_in, f32[19,8,16,128]{3,2,1,0:T(8,128)} %get-tuple-element.6.order_in, f32[40,4,128]{2,1,0:T(4,128)} %get-tuple-element.7.ghosts_in), custom_call_target="tpu_custom_call" | custom-call | tf_op jit(solution)/shard_map/pallas_call | solution.py:874

commit v4 on v3

--- a/solution.py
+++ b/solution.py
@@ -47,6 +47,7 @@
 ROLES = 20
 GHOSTS = 2 * ROLES
 MESH = pl.DeviceIdType.MESH
+FAR_GROUPS = (6, 5, 7, 2, 4, 1, 3, 0)
 ACROSS = ((1, 2), (1, 1), (1, 3), (0, 2), (1, 0), (0, 1), (0, 3), (0, 0))
 
 
@@ -84,32 +85,45 @@
     pltpu.make_async_copy(ref, ref, sem).wait()
 
 
-def slid_block(load, block, offset):
-    offset = offset & (LY * N_GY - 1)
-    first = block + (offset >> 7)
-    inside = offset & (LY - 1)
-    here = load(first & (N_GY - 1))
-    beyond = load((first + 1) & (N_GY - 1))
-    shift = (LY - inside) & (LY - 1)
-    return jnp.where(lanes(here.shape) < LY - inside, turn(here, shift), turn(beyond, shift))
-
-
 def parts_of(units):
     frac = (units & 255).astype(jnp.float32) * (1.0 / 256.0)
     return units >> 8, 1.0 - frac, frac
 
 
-def slide(load, block, parts, along_y=0):
+def rows_after(value):
+    return pltpu.roll(value, N_GY - 1, 0)
+
+
+def rows_before(value):
+    return pltpu.roll(value, 1, 0)
+
+
+def slide(value, parts, along_y=0):
     whole, keep, frac = parts
-    start = whole + along_y
-    return keep * slid_block(load, block, start) + frac * slid_block(load, block, start + 1)
+    whole = (whole + along_y) & (LY * N_GY - 1)
+    inside = whole & (LY - 1)
+    tile = lanes(value.shape)
+    first = turn(value, LY - 1)
+    value = keep * value + frac * jnp.where(tile == LY - 1, rows_after(first), first)
+    value = turn(value, (LY - inside) & (LY - 1))
+    value = jnp.where(tile < LY - inside, value, rows_after(value))
+    return pltpu.roll(value, (N_GY - (whole >> 7)) & (N_GY - 1), 0)
+
+
+def rim_of(value, width):
+    tile = lanes(value.shape)
+    return jnp.where(
+        tile < width,
+        rows_after(value),
+        jnp.where(tile >= LY - width, rows_before(value), 0.0),
+    )
 
 
 def kernel(
     fluid_in, order_in, offsets_in, speeds_in, fluid_out, order_out, ghosts_out,
     offsets, speeds, state, post, field, pot, mom,
     a_up, a_down, a_edge, a_land, a_slid, a_ghost, a_near,
-    b_send, b_part, b_own, b_edge, b_land_0, b_land_1, b_back, b_full, b_line, b_turned, b_slid, b_ghost, b_near,
+    b_send, b_part, b_own, b_edge, b_land_0, b_land_1, b_back, b_slid, b_ghost, b_near,
     in_sem, out_sem, send_sem, recv_sem,
 ):
     b_lands = (b_land_0, b_land_1)
@@ -124,10 +138,10 @@
     a_z = owner & 7
     a_part = owner >> 3
     place = owner & 3
-    b_role = 8 * place + (owner >> 2)
-    is_owner = b_role < ROLES
+    group = owner >> 2
+    b_role = jnp.where(place == 2, 16 + (group >> 1), 8 * place + group)
+    is_owner = jnp.logical_or(place < 2, jnp.logical_and(place == 2, (group & 1) == 0))
     is_phi = place == 3
-    phi_z = owner >> 2
 
     load_order = pltpu.make_async_copy(order_in, state.at[pl.ds(19, 19)], in_sem.at[0])
     load_order.start()
@@ -176,7 +190,7 @@
 
     def pack_faces():
         for j in range(2):
-            a_up[:, j, :] = field[:, 8 + LX - 2 + j, pl.ds(0, LY)]
+            a_up[:, j, :] = field[:, 8 + LX - 1 - j, pl.ds(0, LY)]
             a_down[:, j, :] = field[:, 8 + j, pl.ds(0, LY)]
 
     def pack_columns():
@@ -403,41 +417,27 @@
         load_fluid.wait()
         moments()
         parts = parts_of(units_of(0))
-        whole, keep, frac = parts
         wait_bytes(a_land, recv_sem.at[0, 0])
-
-        def slide_order(block):
-            values = [
-                slid_block(lambda i: a_land[i], block, whole + shift) for shift in (-1, 0, 1, 2)
-            ]
-            for k in range(3):
-                a_slid[block & 15, k] = keep * values[k] + frac * values[k + 1]
-
+        near = slide(a_land[:, 0, :], parts)
+        a_slid[:, 0, :] = near
+        a_slid[:, 1, :] = slide(a_land[:, 1, :], parts)
+        a_slid[:, 2, :] = rim_of(near, 1)
         a_role = 8 * is_down + a_z
-        slide_order(gy)
-        pltpu.make_async_copy(
-            a_slid.at[gy & 15], a_ghost.at[a_role], recv_sem.at[2, 0]
-        ).start()
 
         def send_slid_order(j, carry):
             block = gy ^ (16 - j)
-            slide_order(block)
-            send(a_slid.at[block & 15], a_ghost.at[a_role], 2, 0, sec, block)
+            send(a_slid.at[block], a_ghost.at[a_role], 2, 0, sec, block)
             return carry
 
         lax.fori_loop(1, 16, send_slid_order, 0, unroll=5)
+        pltpu.make_async_copy(a_slid.at[gy], a_ghost.at[a_role], recv_sem.at[2, 0]).start()
         put_columns(0)
         wait_bytes(a_ghost, recv_sem.at[2, 0])
         for side, near_x, far_x in outside:
             roles = pl.ds(8 * side, 8)
-            first = 1 - side
-            field[:, 8 + near_x, own] = a_ghost[roles, 1, first, :]
-            field[:, 8 + far_x, own] = a_ghost[roles, 1, 1 - first, :]
-            field[:, 8 + near_x, halo] = jnp.where(
-                rim == 0,
-                turn(a_ghost[roles, 2, first, :], 1),
-                jnp.where(rim == LY - 1, turn(a_ghost[roles, 0, first, :], LY - 1), 0.0),
-            )
+            field[:, 8 + near_x, own] = a_ghost[roles, 0, :]
+            field[:, 8 + far_x, own] = a_ghost[roles, 1, :]
+            field[:, 8 + near_x, halo] = a_ghost[roles, 2, :]
         wait_bytes(a_land, send_sem.at[0])
         wait_bytes(a_slid.at[pl.ds(0, 15)], send_sem.at[2])
 
@@ -525,20 +525,13 @@
         slot = ROLES * is_down + b_role
         wait_bytes(b_lands[step], recv_sem.at[3, step])
 
-        def make(block):
-            b_slid[block] = slide(lambda i: b_lands[step][i], block, parts, along_y)
-
-        pass_on(step, slot, make)
-
-    def pass_on(step, slot, make):
-        make(gy)
-        pltpu.make_async_copy(
-            b_slid.at[gy], b_ghost.at[step, slot], recv_sem.at[5, step]
-        ).start()
-
+        for j in range(4):
+            b_slid[:, j, :] = slide(b_lands[step][:, j, :], parts, along_y)
+        pass_on(step, slot)
+
+    def pass_on(step, slot):
         def one(k, m):
             block = far_first(gy, k, m)
-            make(block)
             send(b_slid.at[block], b_ghost.at[step, slot], 5, step, sec, block)
 
         def several(k, carry):
@@ -549,74 +542,45 @@
         lax.fori_loop(0, 7, several, 0)
         for m in range(7):
             one(7, m)
+        pltpu.make_async_copy(
+            b_slid.at[gy], b_ghost.at[step, slot], recv_sem.at[5, step]
+        ).start()
 
     def pass_order(step):
         units = units_of(step)
         parts = parts_of(units)
         parts_back = parts_of((SPAN - units) & (SPAN - 1))
         parts_next = parts_of(units_of(step + 1))
+        line = lanes((N_GY, LY))
+
+        def complete(sums, crossed, j):
+            forward = rows_before(turn(crossed, (LY - j) % LY) if j else crossed)
+            back = rows_after(turn(crossed, j) if j else crossed)
+            return sums + jnp.where(line == 0, forward, jnp.where(line == LY - 1, back, 0.0))
+
+        wait_bytes(b_back, recv_sem.at[7, step])
+        returned = slide(complete(b_back[:, 0, :], b_back[:, 1, :], 0), parts_back)
         wait_bytes(b_lands[step], recv_sem.at[6, step])
-        wait_bytes(b_back, recv_sem.at[7, step])
-        four = lanes((4, LY))
-        which = lax.broadcasted_iota(jnp.int32, (4, LY), 0)
-        line = lanes((1, LY))
-
-        def complete(block, carry):
-            before = (block + N_GY - 1) & (N_GY - 1)
-            after = (block + 1) & (N_GY - 1)
-            forward = jnp.broadcast_to(b_lands[step][before, pl.ds(3, 1), :], (4, LY))
-            back = jnp.broadcast_to(b_lands[step][after, pl.ds(3, 1), :], (4, LY))
-            for j in (1, 2):
-                forward = jnp.where(which == j, turn(forward, LY - j), forward)
-                back = jnp.where(which == j, turn(back, j), back)
-            b_full[block] = (
-                b_lands[step][block]
-                + jnp.where(four == 0, forward, 0.0)
-                + jnp.where(four == LY - 1, back, 0.0)
-            )
-            b_line[block] = (
-                b_back[block, pl.ds(0, 1), :]
-                + jnp.where(line == 0, b_back[before, pl.ds(1, 1), :], 0.0)
-                + jnp.where(line == LY - 1, b_back[after, pl.ds(1, 1), :], 0.0)
-            )
-            return carry
-
-        lax.fori_loop(0, N_GY, complete, 0, unroll=4)
-
-        def add_own(block, carry):
-            b_full[block, pl.ds(0, 1), :] = b_full[block, pl.ds(0, 1), :] + slide(
-                lambda i: b_line[i], block, parts_back
-            )
-            return carry
-
-        lax.fori_loop(0, N_GY, add_own, 0, unroll=4)
-
-        def turn_all(block, carry):
-            ahead = slide(lambda i: b_full[i], block, parts_next)
-            now = slide(lambda i: b_full[i], block, parts)
-            b_turned[block] = jnp.where(which == 2, now, ahead)
-            return carry
-
-        lax.fori_loop(0, N_GY, turn_all, 0, unroll=4)
-
-        def make(block):
-            before = (block + N_GY - 1) & (N_GY - 1)
-            after = (block + 1) & (N_GY - 1)
-            b_slid[block, pl.ds(0, 2), :] = b_turned[block, pl.ds(0, 2), :]
-            b_slid[block, pl.ds(2, 1), :] = jnp.where(
-                line == 0,
-                b_turned[after, pl.ds(0, 1), :],
-                jnp.where(line == LY - 1, b_turned[before, pl.ds(0, 1), :], 0.0),
-            )
-            b_slid[block, pl.ds(3, 1), :] = jnp.where(
-                line < 2,
-                b_turned[after, pl.ds(2, 1), :],
-                jnp.where(line >= LY - 2, b_turned[before, pl.ds(2, 1), :], 0.0),
-            )
-
-        pass_on(step, GHOSTS + 8 * is_down + phi_z, make)
-
-    def stream(z, carry):
+        land = b_lands[step]
+        crossed = land[:, 3, :]
+        near = slide(complete(land[:, 0, :], crossed, 0) + returned, parts_next)
+        b_slid[:, 0, :] = near
+        b_slid[:, 1, :] = slide(complete(land[:, 1, :], crossed, 1), parts_next)
+        b_slid[:, 2, :] = rim_of(near, 1)
+        b_slid[:, 3, :] = rim_of(slide(complete(land[:, 2, :], crossed, 2), parts), 2)
+        pass_on(step, GHOSTS + 8 * is_down + group)
+
+    def stream_level(z, carry):
+        for which in range(38):
+            shift_x, shift_y, shift_z = VELOCITY[which % 19]
+            if shift_y == 0:
+                tile = post[which, (z - shift_z) & 7]
+                if shift_x:
+                    tile = pltpu.roll(tile, shift_x % LX, 0)
+                state[which, z] = tile
+        return carry
+
+    def stream_along_y(z, carry):
         near_left, near_right = carry
         columns = {}
         for shift_z in (-1, 0, 1):
@@ -627,12 +591,14 @@
         for which in range(38):
             i = which % 19
             shift_x, shift_y, shift_z = VELOCITY[i]
+            if shift_y == 0:
+                continue
             tile = post[which, (z - shift_z) & 7]
             if shift_y == 1:
                 k = Y_PLUS.index(i) + (5 if which >= 19 else 0)
                 outer = turn(columns[1, shift_z], (LY - 8 * k) % LY)
                 tile = jnp.where(lane == 0, outer, turn(tile, 1))
-            elif shift_y == -1:
+            else:
                 k = Y_MINUS.index(i) + (5 if which >= 19 else 0)
                 outer = turn(columns[-1, shift_z], (LY - 1 - 8 * k) % LY)
                 tile = jnp.where(lane == LY - 1, outer, turn(tile, LY - 1))
@@ -670,36 +636,40 @@
             field[:, 8 + x, halo] = field[:, 8 + x, halo] + b_ghost[step, roles, 3, :]
 
     def send_ghosts(step):
-        def one(j, carry):
-            role = lax.rem(j + gy, ROLES)
-            target = 2 * (4 * (role & 7) + (role >> 3))
-            send(b_send.at[0, role], b_lands[step].at[gy], 3, step, above, target)
-            send(b_send.at[1, role], b_lands[step].at[gy], 3, step, below, target + 1)
-            return carry
-
-        lax.fori_loop(0, ROLES, one, 0, unroll=5)
+        for change in FAR_GROUPS:
+            other = (gy >> 3) ^ change
+            for place in range(2):
+                role = 8 * place + other
+                target = 8 * other + 2 * place
+                send(b_send.at[0, role], b_lands[step].at[gy], 3, step, above, target)
+                send(b_send.at[1, role], b_lands[step].at[gy], 3, step, below, target + 1)
+            if change & 1 == 0:
+                even = other & 6
+                role = 16 + (even >> 1)
+                target = 8 * even + 4
+                send(b_send.at[0, role], b_lands[step].at[gy], 3, step, above, target)
+                send(b_send.at[1, role], b_lands[step].at[gy], 3, step, below, target + 1)
 
     def send_parts(step):
-        def one(j, carry):
-            z = (j + (gy >> 3)) & 7
+        for change in FAR_GROUPS:
+            z = (gy >> 3) ^ change
             target = 8 * z + 6
             send(b_part.at[0, z], b_lands[step].at[gy], 6, step, above, target)
             send(b_part.at[1, z], b_lands[step].at[gy], 6, step, below, target + 1)
             for side in (0, 1):
                 to = target + 1 - side
-
-                @pl.when(to != gy)
-                def _():
+                if change:
                     send(b_own.at[side, z], b_back.at[gy], 7, step, sec, to)
-
-            return carry
-
-        lax.fori_loop(0, 8, one, 0)
+                else:
+
+                    @pl.when(to != gy)
+                    def _():
+                        send(b_own.at[side, z], b_back.at[gy], 7, step, sec, to)
 
         @pl.when(is_phi)
         def _():
             pltpu.make_async_copy(
-                b_own.at[1 - is_down, phi_z], b_back.at[gy], recv_sem.at[7, step]
+                b_own.at[1 - is_down, group], b_back.at[gy], recv_sem.at[7, step]
             ).start()
 
     exchange_order()
@@ -721,6 +691,7 @@
         b_edge[1] = to_right
         send(b_edge.at[0], b_near.at[step, 1], 4, step, sec, left)
         send(b_edge.at[1], b_near.at[step, 0], 4, step, sec, right)
+        lax.fori_loop(0, NZ, stream_level, 0)
 
         if step > 0:
             @pl.when(jnp.logical_or(is_owner, is_phi))
@@ -738,7 +709,7 @@
                 pass_order(step)
 
         wait_bytes(b_near.at[step], recv_sem.at[4, step])
-        lax.fori_loop(0, NZ, stream, (b_near[step, 0], b_near[step, 1]))
+        lax.fori_loop(0, NZ, stream_along_y, (b_near[step, 0], b_near[step, 1]))
         wait_bytes(a_edge, send_sem.at[1])
         if last:
             store_fluid = pltpu.make_async_copy(state.at[pl.ds(0, 19)], fluid_out, out_sem.at[0])
@@ -846,8 +817,8 @@
             scratch(NZ, 2, LY),
             scratch(2, LX, LY),
             scratch(N_GY, 2, LY),
-            scratch(16, 3, 2, LY),
-            scratch(16, 3, 2, LY),
+            scratch(N_GY, 3, LY),
+            scratch(16, 3, LY),
             scratch(STEPS, 2, LX, LY),
             scratch(2, ROLES, 4, LY),
             scratch(2, NZ, 4, LY),
@@ -856,9 +827,6 @@
             scratch(N_GY, 4, LY),
             scratch(N_GY, 4, LY),
             scratch(N_GY, 2, LY),
-            scratch(N_GY, 4, LY),
-            scratch(N_GY, 1, LY),
-            scratch(N_GY, 4, LY),
             scratch(N_GY, 4, LY),
             scratch(STEPS, GHOSTS + 16, 4, LY),
             scratch(STEPS, 2, LX, LY),

time: 66.6 us -> 60.1 us (0.902)
  Pallas kernels: 65.8 us -> 59.3 us
    pallas_call x1, Pallas kernels: 62.7 us -> 56.2 us  [per_device(): pl.pallas_call(kernel, out_shape=(shape, shape, ghosts), in_specs=[hbm] *...]
where the time goes in v4:
time: 60.1 us; the launch traced here: 60 us
  Pallas kernels  59.3 us (99%)
  between operations  0.64 us (1%)
    pallas_call x1, Pallas kernels, per_device(): pl.pallas_call(kernel, out_shape=(shape, shape, ghosts), in_specs=[hbm] *...  56.2 us
    pallas_call x1, Pallas kernels, per_device(): pl.pallas_call(finish, out_shape=(shape, shape), in_specs=[hbm] * 3, out_...  3.15 us

profile of v4, /device:TPU:1, one launch (start us, length us, event | category | flops | bytes accessed | tf_op | source)
XLA Modules:
  0.0 60.0 jit_solution(16197536320864863948)
XLA Ops:
  0.6 56.2 %shard_map.59 = (f32[19,8,16,128]{3,2,1,0:T(8,128)}, f32[19,8,16,128]{3,2,1,0:T(8,128)}, f32[40,4,128]{2,1,0:T(4,128)}) custom-call(f32[19,8,16,128]{3,2,1,0:T(8,128)} %fluid_in.1, f32[19,8,16,128]{3,2,1,0:T(8,128)} %order_in.1, s32[2,4]{1,0:T(2,128)} %offsets_in.1, s32[4]{0:T(128)} %speeds_in.1), custom_call_target="tpu_custom_call" | custom-call | tf_op jit(solution)/shard_map/pallas_call | solution.py:803
  56.8 3.1 %shard_map.60 = (f32[19,8,16,128]{3,2,1,0:T(8,128)}, f32[19,8,16,128]{3,2,1,0:T(8,128)}) custom-call(f32[19,8,16,128]{3,2,1,0:T(8,128)} %get-tuple-element.5.fluid_in, f32[19,8,16,128]{3,2,1,0:T(8,128)} %get-tuple-element.6.order_in, f32[40,4,128]{2,1,0:T(4,128)} %get-tuple-element.7.ghosts_in), custom_call_target="tpu_custom_call" | custom-call | tf_op jit(solution)/shard_map/pallas_call | solution.py:842

commit v5 on v4

v5 whole, which is shorter than its diff:
```python
import jax
import jax.numpy as jnp
from jax import lax
from jax.experimental import pallas as pl
from jax.experimental.pallas import tpu as pltpu
from jax.sharding import PartitionSpec as P

STEPS = 2
VELOCITY = (
    (0, 0, 0),
    (1, 0, 0),
    (-1, 0, 0),
    (0, 1, 0),
    (0, -1, 0),
    (0, 0, 1),
    (0, 0, -1),
    (1, 1, 0),
    (-1, -1, 0),
    (1, -1, 0),
    (-1, 1, 0),
    (1, 0, 1),
    (-1, 0, -1),
    (1, 0, -1),
    (-1, 0, 1),
    (0, 1, 1),
    (0, -1, -1),
    (0, 1, -1),
    (0, -1, 1),
)
WEIGHTS = (1.0 / 3.0,) + (1.0 / 18.0,) * 6 + (1.0 / 36.0,) * 12
UPWARD = (1, 7, 9, 11, 13)
DOWNWARD = (2, 8, 10, 12, 14)
Y_PLUS = (3, 7, 10, 15, 17)
Y_MINUS = (4, 8, 9, 16, 18)
COEF_A = -0.0625
COEF_B = 0.0625
KAPPA_GRAD = 0.04
MOBILITY = 1.0
TAU_FLUID = 0.8
TAU_ORDER = 0.9
NZ = 8
LX = 16
LY = 128
N_SEC = 4
N_GY = 64
SPAN = LY * N_GY * 256
ROLES = 32
KINDS = 17
WIDE = 2 * LY
EDGES = (0, 1, LX - 2, LX - 1)
MESH = pl.DeviceIdType.MESH
FAR_GROUPS = (6, 5, 7, 2, 4, 1, 3, 0)
ACROSS = ((1, 2), (1, 1), (1, 3), (0, 2), (1, 0), (0, 1), (0, 3), (0, 0))


def lanes(shape):
    return lax.broadcasted_iota(jnp.int32, shape, len(shape) - 1)


def turn(value, shift):
    return pltpu.roll(value, shift, value.ndim - 1)


def ring_z(gy, k):
    half = (k + 1) >> 1
    return ((gy >> 2) + 4 + jnp.where((k & 1) == 1, -half, half)) & 7


def far_first(gy, k, m):
    across, along = ACROSS[m]
    return (((gy >> 5) ^ across) << 5) + (ring_z(gy, k) << 2) + ((gy + along) & 3)


def signed_sum(terms, signs):
    total = None
    for term, sign in zip(terms, signs):
        if sign == 0:
            continue
        if total is None:
            total = term if sign > 0 else -term
        else:
            total = total + term if sign > 0 else total - term
    return total


def wait_bytes(ref, sem):
    pltpu.make_async_copy(ref, ref, sem).wait()


def parts_of(units):
    frac = (units & 255).astype(jnp.float32) * (1.0 / 256.0)
    return units >> 8, 1.0 - frac, frac


def rows_after(value):
    return pltpu.roll(value, N_GY - 1, 0)


def rows_before(value):
    return pltpu.roll(value, 1, 0)


def shifted_line(value, whole):
    inside = whole & (LY - 1)
    tile = lanes(value.shape)
    value = turn(value, (LY - inside) & (LY - 1))
    value = jnp.where(tile < LY - inside, value, rows_after(value))
    return pltpu.roll(value, (N_GY - (whole >> 7)) & (N_GY - 1), 0)


def potential_of(middle, one, other):
    lap = (
        one
        + other
        + turn(middle, 1)
        + turn(middle, WIDE - 1)
        + pltpu.roll(middle, 1, 0)
        + pltpu.roll(middle, NZ - 1, 0)
        - 6.0 * middle
    )
    return middle * (COEF_A + COEF_B * middle * middle) - KAPPA_GRAD * lap


LEFT_F = 1.0 - 1.0 / TAU_FLUID
LEFT_G = 1.0 - 1.0 / TAU_ORDER
KICK = 1.0 - 0.5 / TAU_FLUID


class Layer:
    def __init__(self, phi, low, middle, high, density, flow):
        half = -0.5 * phi
        self.phi, self.middle, self.density = phi, middle, density
        self.force = (
            half * (high - low),
            half * (turn(middle, WIDE - 1) - turn(middle, 1)),
            half * (pltpu.roll(middle, NZ - 1, 0) - pltpu.roll(middle, 1, 0)),
        )
        inverse = 1.0 / density
        self.vel = tuple((flow[k] + 0.5 * self.force[k]) * inverse for k in range(3))
        vel, force = self.vel, self.force
        self.square = vel[0] * vel[0] + vel[1] * vel[1] + vel[2] * vel[2]
        drift = vel[0] * force[0] + vel[1] * force[1] + vel[2] * force[2]
        self.scaled = density * (1.0 / TAU_FLUID)
        self.base = self.scaled * (1.0 - 1.5 * self.square) - (3.0 * KICK) * drift
        self.square_phi = phi * (1.0 / TAU_ORDER)
        self.base_phi = (
            3.0 * MOBILITY / TAU_ORDER
        ) * middle - 1.5 * self.square_phi * self.square

    def fluid(self, i, value):
        kept = LEFT_F * value
        if i == 0:
            return kept + WEIGHTS[0] * self.base
        along = signed_sum(self.vel, VELOCITY[i])
        pushed = signed_sum(self.force, VELOCITY[i])
        return kept + WEIGHTS[i] * (
            self.base
            + along * (4.5 * self.scaled * along + (9.0 * KICK) * pushed)
            + (3.0 * self.scaled * along + (3.0 * KICK) * pushed)
        )

    def order(self, i, value):
        kept = LEFT_G * value
        if i == 0:
            return kept + (
                self.square_phi * (1.0 - 0.5 * self.square)
                - (2.0 * MOBILITY / TAU_ORDER) * self.middle
            )
        along = signed_sum(self.vel, VELOCITY[i])
        carried = self.square_phi * along
        return kept + WEIGHTS[i] * (self.base_phi + 4.5 * carried * along + 3.0 * carried)

    def change(self, i, jump):
        moved = self.vel[1] + jump
        along = signed_sum(self.vel, VELOCITY[i])
        after = signed_sum((self.vel[0], moved, self.vel[2]), VELOCITY[i])
        return WEIGHTS[i] * (
            3.0 * (after - along)
            + 4.5 * (after * after - along * along)
            - 1.5 * (moved * moved - self.vel[1] * self.vel[1])
        )


def streamed(value, i):
    _, shift_y, shift_z = VELOCITY[i]
    if shift_y:
        value = turn(value, shift_y % WIDE)
    if shift_z:
        value = pltpu.roll(value, shift_z % NZ, 0)
    return value[:, :LY]


def kernel(
    fluid_in, order_in, offsets_in, speeds_in, fluid_out, order_out,
    offsets, speeds, state, post, field, pot, mom, kept,
    a_edge, a_near,
    r_send, r_land_0, r_land_1, r_slid, r_ghost,
    in_sem, out_sem, send_sem, recv_sem,
):
    lands = (r_land_0, r_land_1)
    sec = lax.axis_index("sec")
    gy = lax.axis_index("gy")
    above = (sec + 1) & (N_SEC - 1)
    below = (sec + N_SEC - 1) & (N_SEC - 1)
    left = (gy + N_GY - 1) & (N_GY - 1)
    right = (gy + 1) & (N_GY - 1)
    is_down = gy & 1
    slot = ROLES * (gy & 1) + (gy >> 1)
    load_order = pltpu.make_async_copy(order_in, state.at[pl.ds(19, 19)], in_sem.at[0])
    load_order.start()
    load_offsets = pltpu.make_async_copy(offsets_in, offsets, in_sem.at[2])
    load_offsets.start()
    load_speeds = pltpu.make_async_copy(speeds_in, speeds, in_sem.at[3])
    load_speeds.start()
    load_fluid = pltpu.make_async_copy(fluid_in, state.at[pl.ds(0, 19)], in_sem.at[1])
    load_fluid.start()

    barrier = pltpu.get_barrier_semaphore()
    source_sec = jnp.where(is_down == 0, below, above)

    def greet(k, carry):
        for m in range(8):
            other = far_first(gy, k, m)
            pl.semaphore_signal(
                barrier, inc=1, device_id=(source_sec, other), device_id_type=MESH
            )
            if m < 7:
                pl.semaphore_signal(barrier, inc=1, device_id=(sec, other), device_id_type=MESH)
        return carry

    def greet_rest(k, carry):
        pl.semaphore_signal(
            barrier, inc=1, device_id=(sec, far_first(gy, k, 7)), device_id_type=MESH
        )
        return carry

    lax.fori_loop(0, 8, greet, 0)
    lax.fori_loop(0, 7, greet_rest, 0)

    plane = (LX, LY)
    lane = lanes(plane)
    rim = lanes((NZ, LY))
    level = lax.broadcasted_iota(jnp.int32, (NZ, LY), 0) & 3
    field[...] = jnp.zeros_like(field)
    r_send[...] = jnp.zeros_like(r_send)

    def order_pass():
        def one(z, carry):
            phi = state[19, z]
            for i in range(1, 19):
                phi = phi + state[19 + i, z]
            field[z, pl.ds(8, LX), pl.ds(0, LY)] = phi
            return carry

        lax.fori_loop(0, NZ, one, 0)

    def prepare_faces():
        for side, members, x, inward in ((0, UPWARD, LX - 1, -1), (1, DOWNWARD, 0, 1)):
            fluid = [state[i, :, x, :] for i in range(19)]
            tiles = [fluid[i] for i in members] + [state[19 + i, :, x, :] for i in members]
            tiles.append(signed_sum(fluid, (1,) * 19))
            for axis in range(3):
                tiles.append(signed_sum(fluid, [vector[axis] for vector in VELOCITY]))
            for depth in range(3):
                layer = [state[19 + i, :, x + depth * inward, :] for i in range(19)]
                tiles.append(signed_sum(layer, (1,) * 19))
            for k in range(KINDS - 1):
                r_send[side, 2 * k, pl.ds(0, 4), :] = tiles[k][:4]
                r_send[side, 2 * k + 1, pl.ds(0, 4), :] = tiles[k][4:]
            r_send[side, pl.ds(0, NZ), 4, :] = tiles[KINDS - 1]

    def send_faces(step):
        for change in FAR_GROUPS:
            for place in range(4):
                role = 4 * ((gy >> 3) ^ change) + place
                send(r_send.at[0, role], lands[step].at[gy], 0, step, above, 2 * role)
                send(r_send.at[1, role], lands[step].at[gy], 0, step, below, 2 * role + 1)

    def pack_columns():
        to_left = jnp.zeros(plane, jnp.float32)
        to_right = to_left
        for z in range(NZ):
            phi = field[z, pl.ds(8, LX), pl.ds(0, LY)]
            mine = (lane >> 2) == z
            to_left = jnp.where(mine, turn(phi, 4 * z), to_left)
            to_right = jnp.where(mine, turn(phi, 4 * z + 4), to_right)
        a_edge[0, pl.ds(0, LX), :] = to_left
        a_edge[1, pl.ds(0, LX), :] = to_right
        for side, rows in ((0, Y_MINUS), (1, Y_PLUS)):
            packed = jnp.zeros((NZ, LY), jnp.float32)
            for n, x in enumerate(EDGES):
                tiles = [kept[i, n] for i in rows] + [kept[19 + i, n] for i in rows]
                tiles += [mom[k, :, x, :] for k in range(4)]
                for k, tile in enumerate(tiles):
                    at = 32 * n + k
                    packed = jnp.where(rim == at, turn(tile, (at + side) % LY), packed)
            a_edge[side, pl.ds(LX, NZ), :] = packed

        def pack(z, carry):
            result = []
            for side, rows in ((0, Y_MINUS), (1, Y_PLUS)):
                tiles = [state[i, z] for i in rows] + [state[19 + i, z] for i in rows]
                tiles += [mom[k, z] for k in range(4)]
                going = jnp.zeros(plane, jnp.float32)
                for k, tile in enumerate(tiles):
                    going = jnp.where(lane == 8 * k, turn(tile, 8 * k + side), going)
                result.append(jnp.where((lane & 7) == z, turn(going, z), carry[side]))
            return tuple(result)

        zero = jnp.zeros(plane, jnp.float32)
        packed = lax.fori_loop(0, NZ, pack, (zero, zero))
        for side in range(2):
            a_edge[side, pl.ds(LX + NZ, LX), :] = packed[side]

    def keep_edges():
        for which in range(38):
            for n, x in enumerate(EDGES):
                kept[which, n] = state[which, :, x, :]

    def next_y(near, far):
        tile = lanes(near.shape)
        return jnp.where(tile == LY - 1, turn(far, LY - 1), turn(near, LY - 1))

    def last_y(near, far):
        tile = lanes(near.shape)
        return jnp.where(tile == 0, turn(far, 1), turn(near, 1))

    left_f, left_g, kick = LEFT_F, LEFT_G, KICK

    def send(src, dst, which, slot, to_sec, to_gy):
        pltpu.make_async_remote_copy(
            src_ref=src,
            dst_ref=dst,
            send_sem=send_sem.at[which],
            recv_sem=recv_sem.at[which, slot],
            device_id=(to_sec, to_gy),
            device_id_type=MESH,
        ).start()

    def moments():
        def one(z, carry):
            tiles = [state[i, z] for i in range(19)]
            mom[0, z] = signed_sum(tiles, (1,) * 19)
            for axis in range(3):
                mom[1 + axis, z] = signed_sum(tiles, [vector[axis] for vector in VELOCITY])
            return carry

        lax.fori_loop(0, NZ, one, 0)

    load_order.wait()
    order_pass()
    load_fluid.wait()
    prepare_faces()
    moments()
    keep_edges()
    pack_columns()
    load_offsets.wait()
    load_speeds.wait()
    pl.semaphore_wait(barrier, 2 * N_GY - 1)

    own = pl.ds(0, LY)
    halo = pl.ds(LY, LY)
    def units_of(step):
        return jnp.where(
            is_down == 0, offsets[step, sec], (SPAN - offsets[step, above]) & (SPAN - 1)
        )

    def send_columns(step):
        send(a_edge.at[0], a_near.at[step, 1], 1, step, sec, left)
        send(a_edge.at[1], a_near.at[step, 0], 1, step, sec, right)

    def put_columns(step):
        wait_bytes(a_near.at[step], recv_sem.at[1, step])
        from_left = a_near[step, 0, pl.ds(0, LX), :]
        from_right = a_near[step, 1, pl.ds(0, LX), :]

        def one(z, carry):
            field[z, pl.ds(8, LX), halo] = jnp.where(
                lane < 4,
                turn(from_right, (LY - 4 * z) & (LY - 1)),
                jnp.where(lane >= LY - 4, turn(from_left, (LY - 4 - 4 * z) & (LY - 1)), 0.0),
            )
            return carry

        lax.fori_loop(0, NZ, one, 0)

    def potentials(z, carry):
        tall = lanes((32, LY))
        tiles = [field[z, :, own], field[z, :, halo]]
        ahead = [turn(tile, LY - 1) for tile in tiles]
        behind = [turn(tile, 1) for tile in tiles]
        for k in range(2):
            tile = tiles[k]
            cut = pl.ds(k * LY, LY)
            lap = (
                pltpu.roll(tile, 1, 0)
                + pltpu.roll(tile, 31, 0)
                + jnp.where(tall == LY - 1, ahead[1 - k], ahead[k])
                + jnp.where(tall == 0, behind[1 - k], behind[k])
                + field[(z + 1) & 7, :, cut]
                + field[(z + 7) & 7, :, cut]
                - 6.0 * tile
            )
            pot[z, :, cut] = tile * (COEF_A + COEF_B * tile * tile) - KAPPA_GRAD * lap
        return carry

    def collide(z, carry):
        rows = pl.ds(8, LX)
        inner = pot[z, rows, own]
        beyond = pot[z, rows, halo]
        phi = field[z, rows, own]
        half = -0.5 * phi
        force = (
            half * (pot[z, pl.ds(9, LX), own] - pot[z, pl.ds(7, LX), own]),
            half * (next_y(inner, beyond) - last_y(inner, beyond)),
            half * (pot[(z + 1) & 7, rows, own] - pot[(z + 7) & 7, rows, own]),
        )
        density = mom[0, z]
        inverse = 1.0 / density
        vel = tuple((mom[1 + k, z] + 0.5 * force[k]) * inverse for k in range(3))
        square = vel[0] * vel[0] + vel[1] * vel[1] + vel[2] * vel[2]
        drift = vel[0] * force[0] + vel[1] * force[1] + vel[2] * force[2]
        scaled = density * (1.0 / TAU_FLUID)
        base = scaled * (1.0 - 1.5 * square) - (3.0 * kick) * drift
        square_phi = phi * (1.0 / TAU_ORDER)
        base_phi = (3.0 * MOBILITY / TAU_ORDER) * inner - 1.5 * square_phi * square
        fluid = [None] * 19
        order = [None] * 19
        fluid[0] = left_f * state[0, z] + WEIGHTS[0] * base
        order[0] = left_g * state[19, z] + (
            square_phi * (1.0 - 0.5 * square) - (2.0 * MOBILITY / TAU_ORDER) * inner
        )
        for i in range(1, 19, 2):
            vector = VELOCITY[i]
            along = signed_sum(vel, vector)
            pushed = signed_sum(force, vector)
            weight = WEIGHTS[i]
            even = weight * (base + along * (4.5 * scaled * along + (9.0 * kick) * pushed))
            odd = weight * (3.0 * scaled * along + (3.0 * kick) * pushed)
            fluid[i] = left_f * state[i, z] + (even + odd)
            fluid[i + 1] = left_f * state[i + 1, z] + (even - odd)
            carried = square_phi * along
            even = weight * (base_phi + 4.5 * carried * along)
            odd = (3.0 * weight) * carried
            order[i] = left_g * state[19 + i, z] + (even + odd)
            order[i + 1] = left_g * state[20 + i, z] + (even - odd)
        for i in range(19):
            post[i, z] = fluid[i]
            post[19 + i, z] = order[i]
        return carry

    def collide_beyond(step):
        from_left = a_near[step, 0, pl.ds(LX + NZ, LX), :]
        from_right = a_near[step, 1, pl.ds(LX + NZ, LX), :]
        at_left = lane < LY // 2

        def both(k):
            return jnp.where(
                at_left, turn(from_left, (LY - 8 * k) % LY), turn(from_right, (LY // 2 - 8 * k) % LY)
            )

        def gathered(left_tile, left_lane, right_tile, right_lane, height):
            result = jnp.zeros((height, LY), jnp.float32)
            tall = lanes((height, LY))
            for z in range(NZ):
                moved_left = turn(left_tile(z), (z - left_lane) % LY)
                moved_right = turn(right_tile(z), (LY // 2 + z - right_lane) % LY)
                result = jnp.where(
                    tall == z, moved_left, jnp.where(tall == LY // 2 + z, moved_right, result)
                )
            return result

        rows = pl.ds(8, LX)
        before = gathered(lambda z: pot[z, rows, halo], LY - 2, lambda z: pot[z, rows, own], LY - 1, LX)
        after = gathered(lambda z: pot[z, rows, own], 0, lambda z: pot[z, rows, halo], 1, LX)
        middle = gathered(lambda z: pot[z, :, halo], LY - 1, lambda z: pot[z, :, halo], 0, 32)
        phi = gathered(lambda z: field[z, rows, halo], LY - 1, lambda z: field[z, rows, halo], 0, LX)
        inner = middle[8:24]
        half = -0.5 * phi
        next_z = jnp.where((lane & 7) == 7, turn(inner, 7), turn(inner, LY - 1))
        last_z = jnp.where((lane & 7) == 0, turn(inner, LY - 7), turn(inner, 1))
        force = (half * (middle[9:25] - middle[7:23]), half * (after - before), half * (next_z - last_z))
        density = both(10)
        inverse = 1.0 / density
        vel = tuple((both(11 + k) + 0.5 * force[k]) * inverse for k in range(3))
        square = vel[0] * vel[0] + vel[1] * vel[1] + vel[2] * vel[2]
        drift = vel[0] * force[0] + vel[1] * force[1] + vel[2] * force[2]
        scaled = density * (1.0 / TAU_FLUID)
        base = scaled * (1.0 - 1.5 * square) - (3.0 * kick) * drift
        square_phi = phi * (1.0 / TAU_ORDER)
        base_phi = (3.0 * MOBILITY / TAU_ORDER) * inner - 1.5 * square_phi * square
        sign = jnp.where(at_left, 1.0, -1.0)
        to_left = jnp.zeros(plane, jnp.float32)
        to_right = to_left
        for k, i in enumerate(Y_PLUS):
            weight = WEIGHTS[i]
            along = sign * signed_sum(vel, VELOCITY[i])
            pushed = sign * signed_sum(force, VELOCITY[i])
            carried = square_phi * along
            fluid = left_f * both(k) + weight * (
                base
                + along * (4.5 * scaled * along + (9.0 * kick) * pushed)
                + (3.0 * scaled * along + (3.0 * kick) * pushed)
            )
            order = left_g * both(5 + k) + weight * (
                base_phi + 4.5 * carried * along + 3.0 * carried
            )
            for at, value in ((k, fluid), (5 + k, order)):
                to_left = jnp.where((lane >> 3) == at, turn(value, 8 * at), to_left)
                to_right = jnp.where(
                    (lane >> 3) == at, turn(value, (8 * at + LY // 2) % LY), to_right
                )
        return to_left, to_right

    def pass_faces(step):
        whole = units_of(step) >> 8
        wait_bytes(lands[step], recv_sem.at[0, step])
        tall = lanes((N_GY, LY))
        ends = jnp.zeros((N_GY, LY), jnp.float32)
        for j in range(5):
            line = shifted_line(lands[step][:, j, :], whole)
            r_slid[:, j, :] = line
            ends = jnp.where(
                (tall >> 2) == 2 * j,
                turn(rows_after(line), 8 * j) if j else rows_after(line),
                jnp.where((tall >> 2) == 2 * j + 1, turn(rows_before(line), 8 * j + 8), ends),
            )
        r_slid[:, 5, :] = ends

        def one(k, m):
            block = far_first(gy, k, m)
            send(r_slid.at[block], r_ghost.at[step, slot], 2, step, sec, block)

        def several(k, carry):
            for m in range(8):
                one(k, m)
            return carry

        lax.fori_loop(0, 7, several, 0)
        for m in range(7):
            one(7, m)
        pltpu.make_async_copy(
            r_slid.at[gy], r_ghost.at[step, slot], recv_sem.at[2, step]
        ).start()

    def stream_level(z, carry):
        for which in range(38):
            shift_x, shift_y, shift_z = VELOCITY[which % 19]
            if shift_y == 0:
                tile = post[which, (z - shift_z) & 7]
                if shift_x:
                    tile = pltpu.roll(tile, shift_x % LX, 0)
                state[which, z] = tile
        return carry

    def stream_along_y(z, carry):
        near_left, near_right = carry
        columns = {}
        for shift_z in (-1, 0, 1):
            source = (z - shift_z) & 7
            back = (LY - source) & (LY - 1)
            columns[1, shift_z] = turn(near_left, back)
            columns[-1, shift_z] = turn(near_right, back)
        for which in range(38):
            i = which % 19
            shift_x, shift_y, shift_z = VELOCITY[i]
            if shift_y == 0:
                continue
            tile = post[which, (z - shift_z) & 7]
            if shift_y == 1:
                k = Y_PLUS.index(i) + (5 if which >= 19 else 0)
                outer = turn(columns[1, shift_z], (LY - 8 * k) % LY)
                tile = jnp.where(lane == 0, outer, turn(tile, 1))
            else:
                k = Y_MINUS.index(i) + (5 if which >= 19 else 0)
                outer = turn(columns[-1, shift_z], (LY - 1 - 8 * k) % LY)
                tile = jnp.where(lane == LY - 1, outer, turn(tile, LY - 1))
            if shift_x:
                tile = pltpu.roll(tile, shift_x % LX, 0)
            state[which, z] = tile
        return carry

    def take_faces(step, side):
        members, (x, second, third, fourth), units, jump = (
            (UPWARD, (0, 1, 2, 3), offsets[step, sec], -1.0 * speeds[sec].astype(jnp.float32)),
            (
                DOWNWARD,
                (LX - 1, LX - 2, LX - 3, LX - 4),
                (SPAN - offsets[step, above]) & (SPAN - 1),
                speeds[above].astype(jnp.float32),
            ),
        )[side]
        jump = jump * (1.0 / 256.0)
        _, keep, frac = parts_of(units)
        first = ROLES * side

        def ordered(outer, inner):
            return (outer, inner) if side == 0 else (inner, outer)

        def unpacked(tile, crossed):
            ends = crossed
            for j in (1, 2, 3):
                ends = jnp.where(level == j, turn(crossed, LY - 8 * j), ends)
            return widened(tile, ends)

        def widened(tile, ends):
            ends = jnp.where(rim < 4, ends, jnp.where(rim >= LY - 4, turn(ends, LY - 8), 0.0))
            return jnp.concatenate([tile, ends], axis=1)

        def kind(k):
            if k == KINDS - 1:
                roles = pl.ds(first, NZ)
                return widened(
                    r_ghost[step, roles, 4, :], turn(r_ghost[step, roles, 5, :], LY - 32)
                )
            pair = r_ghost[step, pl.ds(first + 2 * k, 2), pl.ds(0, 4), :].reshape(NZ, LY)
            ends = [
                jnp.broadcast_to(r_ghost[step, first + 2 * k + j, pl.ds(5, 1), :], (4, LY))
                for j in range(2)
            ]
            return unpacked(pair, jnp.concatenate(ends, axis=0))

        kinds = [kind(k) for k in range(KINDS)]
        density, flow = kinds[10], kinds[11:14]
        beyond, beyond2, beyond3 = kinds[14:]
        own0, own1, own2, own3 = [field[:, 8 + at, :] for at in (x, second, third, fourth)]

        seen0 = keep * own0 + frac * turn(own0, 1)
        seen1 = keep * own1 + frac * turn(own1, 1)
        inner = potential_of(beyond2, beyond3, beyond)
        middle = potential_of(beyond, beyond2, seen0)
        outer = potential_of(seen0, beyond, seen1)
        low, high = ordered(inner, outer)
        layer = Layer(beyond, low, middle, high, density, flow)
        for k, i in enumerate(members):
            change = layer.change(i, jump)
            sent = (
                layer.fluid(i, kinds[k]) + density * change,
                layer.order(i, kinds[5 + k]) + beyond * change,
            )
            for lift, value in zip((0, 19), sent):
                ghost = keep * value + frac * turn(value, WIDE - 1)
                state[lift + i, :, x, :] = streamed(ghost, i)

        near = keep * beyond + frac * turn(beyond, WIDE - 1)
        far = keep * beyond2 + frac * turn(beyond2, WIDE - 1)
        pots = [
            potential_of(near, far, own0),
            potential_of(own0, near, own1),
            potential_of(own1, own0, own2),
            potential_of(own2, own1, own3),
        ]
        columns = [a_near[step, j, pl.ds(LX, NZ), :] for j in range(2)]
        for depth, (at, phi) in enumerate(((x, own0), (second, own1))):
            n = EDGES.index(at)

            def from_left(k):
                return turn(columns[0], LY - 1 - (32 * n + k))

            def from_right(k):
                return turn(columns[1], (LY - (32 * n + k)) % LY)

            def wide_moment(k):
                ends = jnp.where(rim == 0, from_right(10 + k), from_left(10 + k))
                return jnp.concatenate([mom[k, :, at, :], ends], axis=1)

            low, high = ordered(pots[depth], pots[depth + 2])
            layer = Layer(
                phi, low, pots[depth + 1], high, wide_moment(0), [wide_moment(k) for k in (1, 2, 3)]
            )
            for i in range(19):
                shift_x, shift_y, _ = VELOCITY[i]
                target = at + shift_x
                if target < 0 or target >= LX:
                    continue
                for lift, function, k in ((0, layer.fluid, 0), (19, layer.order, 5)):
                    tile = kept[lift + i, n]
                    if shift_y == 1:
                        ends = from_left(Y_PLUS.index(i) + k)
                    elif shift_y == -1:
                        ends = from_right(Y_MINUS.index(i) + k)
                    else:
                        ends = tile
                    value = function(i, jnp.concatenate([tile, ends], axis=1))
                    state[lift + i, :, target, :] = streamed(value, i)

    for step in range(STEPS):
        last = step == STEPS - 1
        send_faces(step)
        if step > 0:
            order_pass()
            moments()
            keep_edges()
            pack_columns()
        send_columns(step)
        put_columns(step)
        if step == 0:
            lax.fori_loop(0, NZ, potentials, 0)
            pass_faces(step)
        else:
            pass_faces(step)
            lax.fori_loop(0, NZ, potentials, 0)
        lax.fori_loop(0, NZ, collide, 0)
        lax.fori_loop(0, NZ, stream_level, 0)
        lax.fori_loop(0, NZ, stream_along_y, collide_beyond(step))

        wait_bytes(r_send, send_sem.at[0])
        wait_bytes(a_edge, send_sem.at[1])
        wait_bytes(r_ghost.at[step], recv_sem.at[2, step])
        for side in range(2):
            take_faces(step, side)
        if not last:
            prepare_faces()
            wait_bytes(r_slid.at[pl.ds(0, N_GY - 1)], send_sem.at[2])

    store_fluid = pltpu.make_async_copy(state.at[pl.ds(0, 19)], fluid_out, out_sem.at[0])
    store_order = pltpu.make_async_copy(state.at[pl.ds(19, 19)], order_out, out_sem.at[1])
    store_fluid.start()
    store_order.start()
    wait_bytes(r_slid.at[pl.ds(0, N_GY - 1)], send_sem.at[2])
    store_fluid.wait()
    store_order.wait()


def finish(fluid_in, order_in, fluid_out, order_out, held, in_sem, out_sem):
    loads, stores = [], []
    for start, size in ((0, 5), (5, 5), (10, 5), (15, 4)):
        for half, src, dst in ((0, fluid_in, fluid_out), (19, order_in, order_out)):
            k = len(loads)
            here = held.at[pl.ds(half + start, size)]
            cut = pl.ds(start, size)
            loads.append(pltpu.make_async_copy(src.at[cut], here, in_sem.at[k]))
            stores.append(pltpu.make_async_copy(here, dst.at[cut], out_sem.at[k]))
    for load in loads:
        load.start()
    for load, store in zip(loads, stores):
        load.wait()
        store.start()
    for store in stores:
        store.wait()


def per_device(fluid_dist, order_dist, plane_offset, plane_speed):
    shape = jax.ShapeDtypeStruct((19, NZ, LX, LY), jnp.float32)
    hbm = pl.BlockSpec(memory_space=pl.ANY)
    dma = pltpu.SemaphoreType.DMA

    def scratch(*dims):
        return pltpu.VMEM(dims, jnp.float32)

    results = pl.pallas_call(
        kernel,
        out_shape=(shape, shape),
        in_specs=[hbm] * 4,
        out_specs=(hbm, hbm),
        scratch_shapes=[
            pltpu.SMEM((STEPS, N_SEC), jnp.int32),
            pltpu.SMEM((N_SEC,), jnp.int32),
            scratch(38, NZ, LX, LY),
            scratch(38, NZ, LX, LY),
            scratch(NZ, 32, 2 * LY),
            scratch(NZ, 32, 2 * LY),
            scratch(4, NZ, LX, LY),
            scratch(38, 4, NZ, LY),
            scratch(2, 2 * LX + NZ, LY),
            scratch(STEPS, 2, 2 * LX + NZ, LY),
            scratch(2, ROLES, 5, LY),
            scratch(N_GY, 5, LY),
            scratch(N_GY, 5, LY),
            scratch(N_GY, 6, LY),
            scratch(STEPS, 2 * ROLES, 6, LY),
            dma((4,)),
            dma((2,)),
            dma((3,)),
            dma((3, STEPS)),
        ],
        compiler_params=pltpu.CompilerParams(
            collective_id=0, has_side_effects=True, vmem_limit_bytes=60 * 1024 * 1024
        ),
    )(fluid_dist, order_dist, plane_offset, plane_speed)
    return pl.pallas_call(
        finish,
        out_shape=(shape, shape),
        in_specs=[hbm] * 2,
        out_specs=(hbm, hbm),
        scratch_shapes=[scratch(38, NZ, LX, LY), dma((8,)), dma((8,))],
        compiler_params=pltpu.CompilerParams(vmem_limit_bytes=60 * 1024 * 1024),
    )(*results)


def solution(mesh):
    split = P(None, None, "sec", "gy")
    return jax.shard_map(
        per_device,
        mesh=mesh,
        in_specs=(split, split, P(), P()),
        out_specs=(split, split),
        check_vma=False,
    )
```

time: 60.1 us -> 56.9 us (0.947)
  Pallas kernels: 59.3 us -> 56.1 us
    pallas_call x2, Pallas kernels: 59.3 us -> 56.1 us  [the longest x1 53.6 us: per_device(): pl.pallas_call(kernel, out_shape=(shape, shape), in_specs=[hbm] * 4, out_...]
where the time goes in v5:
time: 56.9 us; the launch traced here: 56.8 us
  Pallas kernels  56.1 us (99%)
  between operations  0.64 us (1%)
    pallas_call x1, Pallas kernels, per_device(): pl.pallas_call(kernel, out_shape=(shape, shape), in_specs=[hbm] * 4, out_...  53.6 us
    pallas_call x1, Pallas kernels, per_device(): pl.pallas_call(finish, out_shape=(shape, shape), in_specs=[hbm] * 2, out_...  2.55 us

profile of v5, /device:TPU:1, one launch (start us, length us, event | category | flops | bytes accessed | tf_op | source)
XLA Modules:
  0.0 56.8 jit_solution(12260503414420505517)
XLA Ops:
  0.6 53.6 %shard_map.59 = (f32[19,8,16,128]{3,2,1,0:T(8,128)}, f32[19,8,16,128]{3,2,1,0:T(8,128)}) custom-call(f32[19,8,16,128]{3,2,1,0:T(8,128)} %fluid_in.1, f32[19,8,16,128]{3,2,1,0:T(8,128)} %order_in.1, s32[2,4]{1,0:T(2,128)} %offsets_in.1, s32[4]{0:T(128)} %speeds_in.1), custom_call_target="tpu_custom_call" | custom-call | tf_op jit(solution)/shard_map/pallas_call | solution.py:751
  54.2 2.5 %shard_map.60 = (f32[19,8,16,128]{3,2,1,0:T(8,128)}, f32[19,8,16,128]{3,2,1,0:T(8,128)}) custom-call(f32[19,8,16,128]{3,2,1,0:T(8,128)} %get-tuple-element.4.fluid_in, f32[19,8,16,128]{3,2,1,0:T(8,128)} %get-tuple-element.5.order_in), custom_call_target="tpu_custom_call" | custom-call | tf_op jit(solution)/shard_map/pallas_call | solution.py:781

commit v6 on v5

--- a/solution.py
+++ b/solution.py
@@ -147,28 +147,38 @@
             3.0 * MOBILITY / TAU_ORDER
         ) * middle - 1.5 * self.square_phi * self.square
 
-    def fluid(self, i, value):
-        kept = LEFT_F * value
-        if i == 0:
-            return kept + WEIGHTS[0] * self.base
+    def own(self):
+        part = object.__new__(Layer)
+        for name, value in vars(self).items():
+            if isinstance(value, tuple):
+                value = tuple(tile[:, :LY] for tile in value)
+            else:
+                value = value[:, :LY]
+            setattr(part, name, value)
+        return part
+
+    def rest(self, fluid, order):
+        return (
+            LEFT_F * fluid + WEIGHTS[0] * self.base,
+            LEFT_G * order
+            + (
+                self.square_phi * (1.0 - 0.5 * self.square)
+                - (2.0 * MOBILITY / TAU_ORDER) * self.middle
+            ),
+        )
+
+    def terms(self, i):
         along = signed_sum(self.vel, VELOCITY[i])
         pushed = signed_sum(self.force, VELOCITY[i])
-        return kept + WEIGHTS[i] * (
-            self.base
-            + along * (4.5 * self.scaled * along + (9.0 * KICK) * pushed)
-            + (3.0 * self.scaled * along + (3.0 * KICK) * pushed)
+        weight = WEIGHTS[i]
+        dense = self.scaled * along
+        carried = self.square_phi * along
+        return (
+            weight * (self.base + along * (4.5 * dense + (9.0 * KICK) * pushed)),
+            weight * (3.0 * dense + (3.0 * KICK) * pushed),
+            weight * (self.base_phi + 4.5 * carried * along),
+            (3.0 * weight) * carried,
         )
-
-    def order(self, i, value):
-        kept = LEFT_G * value
-        if i == 0:
-            return kept + (
-                self.square_phi * (1.0 - 0.5 * self.square)
-                - (2.0 * MOBILITY / TAU_ORDER) * self.middle
-            )
-        along = signed_sum(self.vel, VELOCITY[i])
-        carried = self.square_phi * along
-        return kept + WEIGHTS[i] * (self.base_phi + 4.5 * carried * along + 3.0 * carried)
 
     def change(self, i, jump):
         moved = self.vel[1] + jump
@@ -181,20 +191,25 @@
         )
 
 
-def streamed(value, i):
+def streamed(tile, ends, i):
     _, shift_y, shift_z = VELOCITY[i]
     if shift_y:
-        value = turn(value, shift_y % WIDE)
+        tile = next_to(tile, ends, -shift_y)
     if shift_z:
-        value = pltpu.roll(value, shift_z % NZ, 0)
-    return value[:, :LY]
+        tile = pltpu.roll(tile, shift_z % NZ, 0)
+    return tile
+
+
+def next_to(tile, ends, step):
+    lane, shift = (LY - 1, LY - 1) if step == 1 else (0, 1)
+    return jnp.where(lanes(tile.shape) == lane, turn(ends, shift), turn(tile, shift))
 
 
 def kernel(
     fluid_in, order_in, offsets_in, speeds_in, fluid_out, order_out,
     offsets, speeds, state, post, field, pot, mom, kept,
     a_edge, a_near,
-    r_send, r_land_0, r_land_1, r_slid, r_ghost,
+    r_send, r_land_0, r_land_1, r_slid, r_ghost, wide, pots,
     in_sem, out_sem, send_sem, recv_sem,
 ):
     lands = (r_land_0, r_land_1)
@@ -267,14 +282,17 @@
             for k in range(KINDS - 1):
                 r_send[side, 2 * k, pl.ds(0, 4), :] = tiles[k][:4]
                 r_send[side, 2 * k + 1, pl.ds(0, 4), :] = tiles[k][4:]
-            r_send[side, pl.ds(0, NZ), 4, :] = tiles[KINDS - 1]
+            for z in range(NZ):
+                r_send[side, 4 * z, pl.ds(4, 1), :] = tiles[KINDS - 1][z : z + 1]
 
     def send_faces(step):
         for change in FAR_GROUPS:
             for place in range(4):
                 role = 4 * ((gy >> 3) ^ change) + place
-                send(r_send.at[0, role], lands[step].at[gy], 0, step, above, 2 * role)
-                send(r_send.at[1, role], lands[step].at[gy], 0, step, below, 2 * role + 1)
+                rows = pl.ds(0, 5 if place == 0 else 4)
+                land = lands[step].at[gy, rows]
+                send(r_send.at[0, role, rows], land, 0, step, above, 2 * role)
+                send(r_send.at[1, role, rows], land, 0, step, below, 2 * role + 1)
 
     def pack_columns():
         to_left = jnp.zeros(plane, jnp.float32)
@@ -514,34 +532,52 @@
 
     def pass_faces(step):
         whole = units_of(step) >> 8
-        wait_bytes(lands[step], recv_sem.at[0, step])
+        has_extra = ((gy >> 1) & 3) == 0
+
+        @pl.when(has_extra)
+        def _():
+            wait_bytes(lands[step], recv_sem.at[0, step])
+
+        @pl.when(jnp.logical_not(has_extra))
+        def _():
+            wait_bytes(lands[step].at[:, pl.ds(0, 4)], recv_sem.at[0, step])
+
         tall = lanes((N_GY, LY))
         ends = jnp.zeros((N_GY, LY), jnp.float32)
         for j in range(5):
             line = shifted_line(lands[step][:, j, :], whole)
-            r_slid[:, j, :] = line
+            r_slid[:, j if j < 4 else 5, :] = line
             ends = jnp.where(
                 (tall >> 2) == 2 * j,
                 turn(rows_after(line), 8 * j) if j else rows_after(line),
                 jnp.where((tall >> 2) == 2 * j + 1, turn(rows_before(line), 8 * j + 8), ends),
             )
-        r_slid[:, 5, :] = ends
-
-        def one(k, m):
-            block = far_first(gy, k, m)
-            send(r_slid.at[block], r_ghost.at[step, slot], 2, step, sec, block)
-
-        def several(k, carry):
-            for m in range(8):
-                one(k, m)
-            return carry
-
-        lax.fori_loop(0, 7, several, 0)
-        for m in range(7):
-            one(7, m)
-        pltpu.make_async_copy(
-            r_slid.at[gy], r_ghost.at[step, slot], recv_sem.at[2, step]
-        ).start()
+        r_slid[:, 4, :] = ends
+
+        def pass_on(rows):
+            def one(k, m):
+                block = far_first(gy, k, m)
+                send(r_slid.at[block, rows], r_ghost.at[step, slot, rows], 2, step, sec, block)
+
+            def several(k, carry):
+                for m in range(8):
+                    one(k, m)
+                return carry
+
+            lax.fori_loop(0, 7, several, 0)
+            for m in range(7):
+                one(7, m)
+            pltpu.make_async_copy(
+                r_slid.at[gy, rows], r_ghost.at[step, slot, rows], recv_sem.at[2, step]
+            ).start()
+
+        @pl.when(has_extra)
+        def _():
+            pass_on(pl.ds(0, 6))
+
+        @pl.when(jnp.logical_not(has_extra))
+        def _():
+            pass_on(pl.ds(0, 5))
 
     def stream_level(z, carry):
         for which in range(38):
@@ -609,80 +645,131 @@
 
         def kind(k):
             if k == KINDS - 1:
-                roles = pl.ds(first, NZ)
-                return widened(
-                    r_ghost[step, roles, 4, :], turn(r_ghost[step, roles, 5, :], LY - 32)
-                )
+                rows = [
+                    jnp.concatenate(
+                        [r_ghost[step, first + 4 * z, pl.ds(j, 1), :] for z in range(NZ)], axis=0
+                    )
+                    for j in (5, 4)
+                ]
+                return widened(rows[0], turn(rows[1], LY - 32))
             pair = r_ghost[step, pl.ds(first + 2 * k, 2), pl.ds(0, 4), :].reshape(NZ, LY)
             ends = [
-                jnp.broadcast_to(r_ghost[step, first + 2 * k + j, pl.ds(5, 1), :], (4, LY))
+                jnp.broadcast_to(r_ghost[step, first + 2 * k + j, pl.ds(4, 1), :], (4, LY))
                 for j in range(2)
             ]
             return unpacked(pair, jnp.concatenate(ends, axis=0))
 
-        kinds = [kind(k) for k in range(KINDS)]
-        density, flow = kinds[10], kinds[11:14]
-        beyond, beyond2, beyond3 = kinds[14:]
-        own0, own1, own2, own3 = [field[:, 8 + at, :] for at in (x, second, third, fourth)]
-
-        seen0 = keep * own0 + frac * turn(own0, 1)
-        seen1 = keep * own1 + frac * turn(own1, 1)
-        inner = potential_of(beyond2, beyond3, beyond)
-        middle = potential_of(beyond, beyond2, seen0)
-        outer = potential_of(seen0, beyond, seen1)
-        low, high = ordered(inner, outer)
-        layer = Layer(beyond, low, middle, high, density, flow)
-        for k, i in enumerate(members):
-            change = layer.change(i, jump)
-            sent = (
-                layer.fluid(i, kinds[k]) + density * change,
-                layer.order(i, kinds[5 + k]) + beyond * change,
-            )
-            for lift, value in zip((0, 19), sent):
-                ghost = keep * value + frac * turn(value, WIDE - 1)
-                state[lift + i, :, x, :] = streamed(ghost, i)
-
-        near = keep * beyond + frac * turn(beyond, WIDE - 1)
-        far = keep * beyond2 + frac * turn(beyond2, WIDE - 1)
-        pots = [
-            potential_of(near, far, own0),
-            potential_of(own0, near, own1),
-            potential_of(own1, own0, own2),
-            potential_of(own2, own1, own3),
-        ]
-        columns = [a_near[step, j, pl.ds(LX, NZ), :] for j in range(2)]
-        for depth, (at, phi) in enumerate(((x, own0), (second, own1))):
-            n = EDGES.index(at)
-
-            def from_left(k):
-                return turn(columns[0], LY - 1 - (32 * n + k))
-
-            def from_right(k):
-                return turn(columns[1], (LY - (32 * n + k)) % LY)
-
-            def wide_moment(k):
-                ends = jnp.where(rim == 0, from_right(10 + k), from_left(10 + k))
-                return jnp.concatenate([mom[k, :, at, :], ends], axis=1)
-
-            low, high = ordered(pots[depth], pots[depth + 2])
-            layer = Layer(
-                phi, low, pots[depth + 1], high, wide_moment(0), [wide_moment(k) for k in (1, 2, 3)]
-            )
-            for i in range(19):
-                shift_x, shift_y, _ = VELOCITY[i]
-                target = at + shift_x
-                if target < 0 or target >= LX:
-                    continue
-                for lift, function, k in ((0, layer.fluid, 0), (19, layer.order, 5)):
-                    tile = kept[lift + i, n]
-                    if shift_y == 1:
-                        ends = from_left(Y_PLUS.index(i) + k)
-                    elif shift_y == -1:
-                        ends = from_right(Y_MINUS.index(i) + k)
+        @pl.when(gy >= 0)
+        def _():
+            for k in range(KINDS):
+                wide[k] = kind(k)
+
+        @pl.when(gy >= 0)
+        def _():
+            kinds = [wide[k] for k in range(KINDS)]
+            density, flow = kinds[10], kinds[11:14]
+            beyond, beyond2, beyond3 = kinds[14:]
+            own0, own1 = [field[:, 8 + at, :] for at in (x, second)]
+
+            seen0 = keep * own0 + frac * turn(own0, 1)
+            seen1 = keep * own1 + frac * turn(own1, 1)
+            inner = potential_of(beyond2, beyond3, beyond)
+            middle = potential_of(beyond, beyond2, seen0)
+            outer = potential_of(seen0, beyond, seen1)
+            low, high = ordered(inner, outer)
+            layer = Layer(beyond, low, middle, high, density, flow)
+            for k, i in enumerate(members):
+                change = layer.change(i, jump)
+                even_f, odd_f, even_g, odd_g = layer.terms(i)
+                sent = (
+                    LEFT_F * kinds[k] + (even_f + odd_f) + density * change,
+                    LEFT_G * kinds[5 + k] + (even_g + odd_g) + beyond * change,
+                )
+                for lift, value in zip((0, 19), sent):
+                    if VELOCITY[i][1]:
+                        ghost = keep * value + frac * turn(value, WIDE - 1)
+                        tile, ends = ghost[:, :LY], ghost[:, LY:]
                     else:
-                        ends = tile
-                    value = function(i, jnp.concatenate([tile, ends], axis=1))
-                    state[lift + i, :, target, :] = streamed(value, i)
+                        tile, ends = value[:, :LY], value[:, LY:]
+                        tile = keep * tile + frac * next_to(tile, ends, 1)
+                    state[lift + i, :, x, :] = streamed(tile, ends, i)
+
+        @pl.when(gy >= 0)
+        def _():
+            beyond, beyond2 = wide[14], wide[15]
+            own0, own1, own2, own3 = [field[:, 8 + at, :] for at in (x, second, third, fourth)]
+            near = keep * beyond + frac * turn(beyond, WIDE - 1)
+            far = keep * beyond2 + frac * turn(beyond2, WIDE - 1)
+            made = [
+                potential_of(near, far, own0),
+                potential_of(own0, near, own1),
+                potential_of(own1, own0, own2),
+                potential_of(own2, own1, own3),
+            ]
+            for k in range(4):
+                pots[k] = made[k]
+
+        for depth, at in enumerate((x, second)):
+
+            @pl.when(gy >= 0)
+            def _():
+                columns = [a_near[step, j, pl.ds(LX, NZ), :] for j in range(2)]
+                phi = field[:, 8 + at, :]
+                n = EDGES.index(at)
+
+                def from_left(k):
+                    return turn(columns[0], LY - 1 - (32 * n + k))
+
+                def from_right(k):
+                    return turn(columns[1], (LY - (32 * n + k)) % LY)
+
+                def wide_moment(k):
+                    ends = jnp.where(rim == 0, from_right(10 + k), from_left(10 + k))
+                    return jnp.concatenate([mom[k, :, at, :], ends], axis=1)
+
+                low, high = ordered(pots[depth], pots[depth + 2])
+                layer = Layer(
+                    phi, low, pots[depth + 1], high, wide_moment(0), [wide_moment(k) for k in (1, 2, 3)]
+                )
+                narrow = layer.own()
+
+                def put(which, target, tile, ends, i):
+                    if 0 <= target < LX:
+                        state[which, :, target, :] = streamed(tile, ends, i)
+
+                fluid, order = narrow.rest(kept[0, n], kept[19, n])
+                put(0, at, fluid, None, 0)
+                put(19, at, order, None, 0)
+                for i in range(1, 19, 2):
+                    shift_x, shift_y, _ = VELOCITY[i]
+                    even_f, odd_f, even_g, odd_g = (layer if shift_y else narrow).terms(i)
+                    for sign, member in ((1, i), (-1, i + 1)):
+                        target = at + sign * shift_x
+                        if target < 0 or target >= LX:
+                            continue
+                        for lift, left, even, odd, k in (
+                            (0, LEFT_F, even_f, odd_f, 0),
+                            (19, LEFT_G, even_g, odd_g, 5),
+                        ):
+                            gain = even + odd if sign == 1 else even - odd
+                            tile = left * kept[lift + member, n] + gain[:, :LY]
+                            ends = None
+                            if sign * shift_y == 1:
+                                ends = left * from_left(Y_PLUS.index(member) + k) + gain[:, LY:]
+                            elif sign * shift_y == -1:
+                                ends = left * from_right(Y_MINUS.index(member) + k) + gain[:, LY:]
+                            put(lift + member, target, tile, ends, member)
+
+    def wait_slid():
+        has_extra = ((gy >> 1) & 3) == 0
+
+        @pl.when(has_extra)
+        def _():
+            wait_bytes(r_slid.at[pl.ds(0, N_GY - 1)], send_sem.at[2])
+
+        @pl.when(jnp.logical_not(has_extra))
+        def _():
+            wait_bytes(r_slid.at[pl.ds(0, N_GY - 1), pl.ds(0, 5)], send_sem.at[2])
 
     for step in range(STEPS):
         last = step == STEPS - 1
@@ -704,20 +791,21 @@
         lax.fori_loop(0, NZ, stream_level, 0)
         lax.fori_loop(0, NZ, stream_along_y, collide_beyond(step))
 
-        wait_bytes(r_send, send_sem.at[0])
+        wait_bytes(r_send.at[:, :, pl.ds(0, 4)], send_sem.at[0])
+        wait_bytes(r_send.at[:, pl.ds(0, NZ), 4], send_sem.at[0])
         wait_bytes(a_edge, send_sem.at[1])
-        wait_bytes(r_ghost.at[step], recv_sem.at[2, step])
+        wait_bytes(r_ghost.at[step, pl.ds(0, 56)], recv_sem.at[2, step])
         for side in range(2):
             take_faces(step, side)
         if not last:
             prepare_faces()
-            wait_bytes(r_slid.at[pl.ds(0, N_GY - 1)], send_sem.at[2])
+            wait_slid()
 
     store_fluid = pltpu.make_async_copy(state.at[pl.ds(0, 19)], fluid_out, out_sem.at[0])
     store_order = pltpu.make_async_copy(state.at[pl.ds(19, 19)], order_out, out_sem.at[1])
     store_fluid.start()
     store_order.start()
-    wait_bytes(r_slid.at[pl.ds(0, N_GY - 1)], send_sem.at[2])
+    wait_slid()
     store_fluid.wait()
     store_order.wait()
 
@@ -769,6 +857,8 @@
             scratch(N_GY, 5, LY),
             scratch(N_GY, 6, LY),
             scratch(STEPS, 2 * ROLES, 6, LY),
+            scratch(KINDS, NZ, WIDE),
+            scratch(4, NZ, WIDE),
             dma((4,)),
             dma((2,)),
             dma((3,)),

time: 56.9 us -> 53.1 us (0.933)
  Pallas kernels: 56.1 us -> 52.4 us
    pallas_call x1, Pallas kernels: 53.6 us -> 49.8 us  [per_device(): pl.pallas_call(kernel, out_shape=(shape, shape), in_specs=[hbm] * 4, out_...]
where the time goes in v6:
time: 53.1 us; the launch traced here: 53 us
  Pallas kernels  52.4 us (99%)
  between operations  0.64 us (1%)
    pallas_call x1, Pallas kernels, per_device(): pl.pallas_call(kernel, out_shape=(shape, shape), in_specs=[hbm] * 4, out_...  49.8 us
    pallas_call x1, Pallas kernels, per_device(): pl.pallas_call(finish, out_shape=(shape, shape), in_specs=[hbm] * 2, out_...  2.55 us

profile of v6, /device:TPU:1, one launch (start us, length us, event | category | flops | bytes accessed | tf_op | source)
XLA Modules:
  0.0 53.0 jit_solution(2213886679856562602)
XLA Ops:
  0.6 49.8 %shard_map.59 = (f32[19,8,16,128]{3,2,1,0:T(8,128)}, f32[19,8,16,128]{3,2,1,0:T(8,128)}) custom-call(f32[19,8,16,128]{3,2,1,0:T(8,128)} %fluid_in.1, f32[19,8,16,128]{3,2,1,0:T(8,128)} %order_in.1, s32[2,4]{1,0:T(2,128)} %offsets_in.1, s32[4]{0:T(128)} %speeds_in.1), custom_call_target="tpu_custom_call" | custom-call | tf_op jit(solution)/shard_map/pallas_call | solution.py:839
  50.5 2.5 %shard_map.60 = (f32[19,8,16,128]{3,2,1,0:T(8,128)}, f32[19,8,16,128]{3,2,1,0:T(8,128)}) custom-call(f32[19,8,16,128]{3,2,1,0:T(8,128)} %get-tuple-element.4.fluid_in, f32[19,8,16,128]{3,2,1,0:T(8,128)} %get-tuple-element.5.order_in), custom_call_target="tpu_custom_call" | custom-call | tf_op jit(solution)/shard_map/pallas_call | solution.py:871

commit v7 on v6

--- a/solution.py
+++ b/solution.py
@@ -147,14 +147,19 @@
             3.0 * MOBILITY / TAU_ORDER
         ) * middle - 1.5 * self.square_phi * self.square
 
-    def own(self):
+    def save(self, ref):
+        tiles = (self.phi, self.middle, self.density, self.square, self.scaled, self.base)
+        tiles += (self.square_phi, self.base_phi) + self.force + self.vel
+        for k, tile in enumerate(tiles):
+            ref[k] = tile
+
+    @staticmethod
+    def saved(ref, columns):
         part = object.__new__(Layer)
-        for name, value in vars(self).items():
-            if isinstance(value, tuple):
-                value = tuple(tile[:, :LY] for tile in value)
-            else:
-                value = value[:, :LY]
-            setattr(part, name, value)
+        tiles = [ref[k, :, columns] for k in range(14)]
+        part.phi, part.middle, part.density, part.square, part.scaled, part.base = tiles[:6]
+        part.square_phi, part.base_phi = tiles[6:8]
+        part.force, part.vel = tuple(tiles[8:11]), tuple(tiles[11:])
         return part
 
     def rest(self, fluid, order):
@@ -209,7 +214,7 @@
     fluid_in, order_in, offsets_in, speeds_in, fluid_out, order_out,
     offsets, speeds, state, post, field, pot, mom, kept,
     a_edge, a_near,
-    r_send, r_land_0, r_land_1, r_slid, r_ghost, wide, pots,
+    r_send, r_land_0, r_land_1, r_slid, r_ghost, wide, pots, held,
     in_sem, out_sem, send_sem, recv_sem,
 ):
     lands = (r_land_0, r_land_1)
@@ -731,34 +736,52 @@
                 layer = Layer(
                     phi, low, pots[depth + 1], high, wide_moment(0), [wide_moment(k) for k in (1, 2, 3)]
                 )
-                narrow = layer.own()
-
-                def put(which, target, tile, ends, i):
-                    if 0 <= target < LX:
-                        state[which, :, target, :] = streamed(tile, ends, i)
-
-                fluid, order = narrow.rest(kept[0, n], kept[19, n])
-                put(0, at, fluid, None, 0)
-                put(19, at, order, None, 0)
-                for i in range(1, 19, 2):
-                    shift_x, shift_y, _ = VELOCITY[i]
-                    even_f, odd_f, even_g, odd_g = (layer if shift_y else narrow).terms(i)
-                    for sign, member in ((1, i), (-1, i + 1)):
-                        target = at + sign * shift_x
-                        if target < 0 or target >= LX:
-                            continue
-                        for lift, left, even, odd, k in (
-                            (0, LEFT_F, even_f, odd_f, 0),
-                            (19, LEFT_G, even_g, odd_g, 5),
-                        ):
-                            gain = even + odd if sign == 1 else even - odd
-                            tile = left * kept[lift + member, n] + gain[:, :LY]
-                            ends = None
-                            if sign * shift_y == 1:
-                                ends = left * from_left(Y_PLUS.index(member) + k) + gain[:, LY:]
-                            elif sign * shift_y == -1:
-                                ends = left * from_right(Y_MINUS.index(member) + k) + gain[:, LY:]
-                            put(lift + member, target, tile, ends, member)
+                layer.save(held)
+
+            both = pl.ds(0, WIDE)
+            for cut, pairs in (
+                (own, (1, 5)), (own, (11, 13)), (both, (3, 7, 9)), (both, (15, 17))
+            ):
+
+                @pl.when(gy >= 0)
+                def _():
+                    layer = Layer.saved(held, cut)
+                    columns = [a_near[step, j, pl.ds(LX, NZ), :] for j in range(2)]
+                    n = EDGES.index(at)
+
+                    def from_left(k):
+                        return turn(columns[0], LY - 1 - (32 * n + k))
+
+                    def from_right(k):
+                        return turn(columns[1], (LY - (32 * n + k)) % LY)
+
+                    def put(which, target, tile, ends, i):
+                        if 0 <= target < LX:
+                            state[which, :, target, :] = streamed(tile, ends, i)
+
+                    if pairs[0] == 1:
+                        fluid, order = layer.rest(kept[0, n], kept[19, n])
+                        put(0, at, fluid, None, 0)
+                        put(19, at, order, None, 0)
+                    for i in pairs:
+                        shift_x, shift_y, _ = VELOCITY[i]
+                        even_f, odd_f, even_g, odd_g = layer.terms(i)
+                        for sign, member in ((1, i), (-1, i + 1)):
+                            target = at + sign * shift_x
+                            if target < 0 or target >= LX:
+                                continue
+                            for lift, left, even, odd, k in (
+                                (0, LEFT_F, even_f, odd_f, 0),
+                                (19, LEFT_G, even_g, odd_g, 5),
+                            ):
+                                gain = even + odd if sign == 1 else even - odd
+                                tile = left * kept[lift + member, n] + gain[:, :LY]
+                                ends = None
+                                if sign * shift_y == 1:
+                                    ends = left * from_left(Y_PLUS.index(member) + k) + gain[:, LY:]
+                                elif sign * shift_y == -1:
+                                    ends = left * from_right(Y_MINUS.index(member) + k) + gain[:, LY:]
+                                put(lift + member, target, tile, ends, member)
 
     def wait_slid():
         has_extra = ((gy >> 1) & 3) == 0
@@ -771,6 +794,7 @@
         def _():
             wait_bytes(r_slid.at[pl.ds(0, N_GY - 1), pl.ds(0, 5)], send_sem.at[2])
 
+    stores = []
     for step in range(STEPS):
         last = step == STEPS - 1
         send_faces(step)
@@ -780,13 +804,9 @@
             keep_edges()
             pack_columns()
         send_columns(step)
+        pass_faces(step)
         put_columns(step)
-        if step == 0:
-            lax.fori_loop(0, NZ, potentials, 0)
-            pass_faces(step)
-        else:
-            pass_faces(step)
-            lax.fori_loop(0, NZ, potentials, 0)
+        lax.fori_loop(0, NZ, potentials, 0)
         lax.fori_loop(0, NZ, collide, 0)
         lax.fori_loop(0, NZ, stream_level, 0)
         lax.fori_loop(0, NZ, stream_along_y, collide_beyond(step))
@@ -797,17 +817,21 @@
         wait_bytes(r_ghost.at[step, pl.ds(0, 56)], recv_sem.at[2, step])
         for side in range(2):
             take_faces(step, side)
+            if last:
+                half = pl.ds(8 * side, 8)
+                for k, (first, out) in enumerate(((0, fluid_out), (19, order_out))):
+                    store = pltpu.make_async_copy(
+                        state.at[pl.ds(first, 19), :, half], out.at[:, :, half], out_sem.at[k, side]
+                    )
+                    store.start()
+                    stores.append(store)
         if not last:
             prepare_faces()
             wait_slid()
 
-    store_fluid = pltpu.make_async_copy(state.at[pl.ds(0, 19)], fluid_out, out_sem.at[0])
-    store_order = pltpu.make_async_copy(state.at[pl.ds(19, 19)], order_out, out_sem.at[1])
-    store_fluid.start()
-    store_order.start()
     wait_slid()
-    store_fluid.wait()
-    store_order.wait()
+    for store in stores:
+        store.wait()
 
 
 def finish(fluid_in, order_in, fluid_out, order_out, held, in_sem, out_sem):
@@ -859,8 +883,9 @@
             scratch(STEPS, 2 * ROLES, 6, LY),
             scratch(KINDS, NZ, WIDE),
             scratch(4, NZ, WIDE),
+            scratch(14, NZ, WIDE),
             dma((4,)),
-            dma((2,)),
+            dma((2, 2)),
             dma((3,)),
             dma((3, STEPS)),
         ],

time: 53.1 us -> 52.3 us (0.985)
  Pallas kernels: 52.4 us -> 51.5 us
    pallas_call x1, Pallas kernels: 49.8 us -> 48.9 us  [per_device(): pl.pallas_call(kernel, out_shape=(shape, shape), in_specs=[hbm] * 4, out_...]
where the time goes in v7:
time: 52.3 us; the launch traced here: 52.1 us
  Pallas kernels  51.5 us (98%)
  between operations  0.64 us (1%)
    pallas_call x1, Pallas kernels, per_device(): pl.pallas_call(kernel, out_shape=(shape, shape), in_specs=[hbm] * 4, out_...  48.9 us
    pallas_call x1, Pallas kernels, per_device(): pl.pallas_call(finish, out_shape=(shape, shape), in_specs=[hbm] * 2, out_...  2.55 us

profile of v7, /device:TPU:1, one launch (start us, length us, event | category | flops | bytes accessed | tf_op | source)
XLA Modules:
  0.0 52.1 jit_solution(11237571872862195637)
XLA Ops:
  0.6 48.9 %shard_map.59 = (f32[19,8,16,128]{3,2,1,0:T(8,128)}, f32[19,8,16,128]{3,2,1,0:T(8,128)}) custom-call(f32[19,8,16,128]{3,2,1,0:T(8,128)} %fluid_in.1, f32[19,8,16,128]{3,2,1,0:T(8,128)} %order_in.1, s32[2,4]{1,0:T(2,128)} %offsets_in.1, s32[4]{0:T(128)} %speeds_in.1), custom_call_target="tpu_custom_call" | custom-call | tf_op jit(solution)/shard_map/pallas_call | solution.py:863
  49.6 2.5 %shard_map.60 = (f32[19,8,16,128]{3,2,1,0:T(8,128)}, f32[19,8,16,128]{3,2,1,0:T(8,128)}) custom-call(f32[19,8,16,128]{3,2,1,0:T(8,128)} %get-tuple-element.4.fluid_in, f32[19,8,16,128]{3,2,1,0:T(8,128)} %get-tuple-element.5.order_in), custom_call_target="tpu_custom_call" | custom-call | tf_op jit(solution)/shard_map/pallas_call | solution.py:896

commit v8 on v7

--- a/solution.py
+++ b/solution.py
@@ -350,12 +350,12 @@
 
     left_f, left_g, kick = LEFT_F, LEFT_G, KICK
 
-    def send(src, dst, which, slot, to_sec, to_gy):
+    def send(src, dst, which, slot, to_sec, to_gy, arrival=None):
         pltpu.make_async_remote_copy(
             src_ref=src,
             dst_ref=dst,
             send_sem=send_sem.at[which],
-            recv_sem=recv_sem.at[which, slot],
+            recv_sem=recv_sem.at[which if arrival is None else arrival, slot],
             device_id=(to_sec, to_gy),
             device_id_type=MESH,
         ).start()
@@ -559,10 +559,14 @@
             )
         r_slid[:, 4, :] = ends
 
+        arrival = 2 + is_down
+
         def pass_on(rows):
             def one(k, m):
                 block = far_first(gy, k, m)
-                send(r_slid.at[block, rows], r_ghost.at[step, slot, rows], 2, step, sec, block)
+                send(
+                    r_slid.at[block, rows], r_ghost.at[step, slot, rows], 2, step, sec, block, arrival
+                )
 
             def several(k, carry):
                 for m in range(8):
@@ -573,7 +577,7 @@
             for m in range(7):
                 one(7, m)
             pltpu.make_async_copy(
-                r_slid.at[gy, rows], r_ghost.at[step, slot, rows], recv_sem.at[2, step]
+                r_slid.at[gy, rows], r_ghost.at[step, slot, rows], recv_sem.at[arrival, step]
             ).start()
 
         @pl.when(has_extra)
@@ -814,8 +818,8 @@
         wait_bytes(r_send.at[:, :, pl.ds(0, 4)], send_sem.at[0])
         wait_bytes(r_send.at[:, pl.ds(0, NZ), 4], send_sem.at[0])
         wait_bytes(a_edge, send_sem.at[1])
-        wait_bytes(r_ghost.at[step, pl.ds(0, 56)], recv_sem.at[2, step])
         for side in range(2):
+            wait_bytes(r_ghost.at[step, pl.ds(ROLES * side, 28)], recv_sem.at[2 + side, step])
             take_faces(step, side)
             if last:
                 half = pl.ds(8 * side, 8)
@@ -887,7 +891,7 @@
             dma((4,)),
             dma((2, 2)),
             dma((3,)),
-            dma((3, STEPS)),
+            dma((4, STEPS)),
         ],
         compiler_params=pltpu.CompilerParams(
             collective_id=0, has_side_effects=True, vmem_limit_bytes=60 * 1024 * 1024

time: 52.3 us -> 50.9 us (0.973)
  Pallas kernels: 51.5 us -> 50.2 us
    pallas_call x1, Pallas kernels: 48.9 us -> 47.6 us  [per_device(): pl.pallas_call(kernel, out_shape=(shape, shape), in_specs=[hbm] * 4, out_...]
where the time goes in v8:
time: 50.9 us; the launch traced here: 50.8 us
  Pallas kernels  50.2 us (99%)
  between operations  0.64 us (1%)
    pallas_call x1, Pallas kernels, per_device(): pl.pallas_call(kernel, out_shape=(shape, shape), in_specs=[hbm] * 4, out_...  47.6 us
    pallas_call x1, Pallas kernels, per_device(): pl.pallas_call(finish, out_shape=(shape, shape), in_specs=[hbm] * 2, out_...  2.55 us

profile of v8, /device:TPU:1, one launch (start us, length us, event | category | flops | bytes accessed | tf_op | source)
XLA Modules:
  0.0 50.8 jit_solution(9618113815018214091)
XLA Ops:
  0.6 47.6 %shard_map.59 = (f32[19,8,16,128]{3,2,1,0:T(8,128)}, f32[19,8,16,128]{3,2,1,0:T(8,128)}) custom-call(f32[19,8,16,128]{3,2,1,0:T(8,128)} %fluid_in.1, f32[19,8,16,128]{3,2,1,0:T(8,128)} %order_in.1, s32[2,4]{1,0:T(2,128)} %offsets_in.1, s32[4]{0:T(128)} %speeds_in.1), custom_call_target="tpu_custom_call" | custom-call | tf_op jit(solution)/shard_map/pallas_call | solution.py:867
  48.2 2.5 %shard_map.60 = (f32[19,8,16,128]{3,2,1,0:T(8,128)}, f32[19,8,16,128]{3,2,1,0:T(8,128)}) custom-call(f32[19,8,16,128]{3,2,1,0:T(8,128)} %get-tuple-element.4.fluid_in, f32[19,8,16,128]{3,2,1,0:T(8,128)} %get-tuple-element.5.order_in), custom_call_target="tpu_custom_call" | custom-call | tf_op jit(solution)/shard_map/pallas_call | solution.py:900
